TPU v7x, 32 devices: a whole 2x2x4 slice. The times are simulated.
32 devices in a mesh: dp: 8 (over y, x, core), tensor: 4 (over z).
Axes of the slice: x: 2, y: 2, z: 4, core: 2. Of those that a mesh axis runs over, the one named last changes fastest.
Arguments:
- char_ids: int32 [512, 8, 50], P(None, 'dp'), may hold values from 0 to 261, as said below
- seq_lengths: int32 [8], P('dp'), may hold values from 40 to 512, as said below
- char_table: bfloat16 [262, 16], replicated, may hold values from -6 to 6
- conv_weight: bfloat16 [112, 2048], P(None, 'tensor'), may hold values from -0.75 to 0.75
- conv_bias: bfloat16 [2048], P('tensor'), may hold values from -3 to 3
- highway_weight: bfloat16 [2, 2, 2048, 2048], P(None, None, None, 'tensor'), may hold values from -0.125 to 0.125
- highway_bias: bfloat16 [2, 2, 2048], P(None, None, 'tensor'), may hold values from -3 to 3
- proj_weight: bfloat16 [2048, 768], P('tensor'), may hold values from -0.125 to 0.125
- proj_bias: bfloat16 [768], replicated, may hold values from -2 to 2
- norm_gain: bfloat16 [3, 768], replicated, may hold values from 0.5 to 1.5
- norm_shift: bfloat16 [3, 768], replicated, may hold values from -2 to 2
- qkv_weight: bfloat16 [768, 3, 768], P(None, None, 'tensor'), may hold values from -0.21875 to 0.21875
- qv_bias: bfloat16 [2, 768], P(None, 'tensor'), may hold values from -2 to 2
- output_projection_weight: bfloat16 [768, 768], P('tensor'), may hold values from -2.5 to 2.5
- out_bias: bfloat16 [768], replicated, may hold values from -2 to 2
- up_weight: bfloat16 [768, 3072], P(None, 'tensor'), may hold values from -0.21875 to 0.21875
- up_bias: bfloat16 [3072], P('tensor'), may hold values from -2 to 2
- down_weight: bfloat16 [3072, 768], P('tensor'), may hold values from -0.109375 to 0.109375
- down_bias: bfloat16 [768], replicated, may hold values from -2 to 2
- out_grad: bfloat16 [512, 8, 768], P('tensor', 'dp'), may hold values from -6 to 6
Outputs:
- encoded: bfloat16 [512, 8, 768], P('tensor', 'dp')
- char_table_grad: float32 [262, 16], replicated
- conv_weight_grad: float32 [112, 2048], replicated
- conv_bias_grad: float32 [2048], replicated
- highway_weight_grad: float32 [2, 2, 2048, 2048], P(None, None, 'dp', 'tensor')
- highway_bias_grad: float32 [2, 2, 2048], replicated
- proj_weight_grad: float32 [2048, 768], P('tensor', 'dp')
- proj_bias_grad: float32 [768], replicated
- norm_gain_grad: float32 [3, 768], replicated
- norm_shift_grad: float32 [3, 768], replicated
- qkv_weight_grad: float32 [768, 3, 768], P('dp', None, 'tensor')
- qv_bias_grad: float32 [2, 768], replicated
- out_weight_grad: float32 [768, 768], P('tensor', 'dp')
- out_bias_grad: float32 [768], replicated
- up_weight_grad: float32 [768, 3072], P('dp', 'tensor')
- up_bias_grad: float32 [3072], replicated
- down_weight_grad: float32 [3072, 768], P('tensor', 'dp')
- down_bias_grad: float32 [768], replicated
Inputs may be any that keep to these rules, and one draw needn't show every extreme that they name: `char_ids`: each word has 1 to 50 characters with ids 1 to 261, followed by id 0 in its remaining places. Sequence n holds words in slots 0 to seq_lengths[n] - 1; the later slots are padding and are never attended to. In each aligned group of min(8, 8) consecutive sequences exactly one has 512 words.
All inputs are finite; a program needn't handle non-finite values.
Results may differ from a plain program's by a relative error of at most 0.013.
Values may be sent and summed in bfloat16 or wider, within the bound.
A program may use at most 192 MiB of HBM per device.

v0:
```python
import math

import jax
import jax.numpy as jnp
from jax import lax
from jax.sharding import PartitionSpec as P

HEAD_DIM = 64


norm_eps = 1e-06
big_neg = -1e30


def width_counts(block):
    unit = block // 64
    return [unit, unit, 2 * unit, 4 * unit, 8 * unit, 16 * unit, 32 * unit]


def layer_norm(values, gain, shift):
    centered = values - jnp.mean(values, axis=-1, keepdims=True)
    variance = jnp.mean(centered * centered, axis=-1, keepdims=True)
    return centered * lax.rsqrt(variance + norm_eps) * gain + shift


def norm_back(values, gain, shift, cotangent):
    unused, pull_back = jax.vjp(layer_norm, values, gain, shift)
    return pull_back(cotangent)


def gelu_exact(values):
    return jax.nn.gelu(values, approximate=False)


def highway_mix(pre_acts, previous):
    gate = jax.nn.sigmoid(pre_acts[:, 1])
    return gate * jax.nn.silu(pre_acts[:, 0]) + (1.0 - gate) * previous


def gather_rows(local_rows):
    return lax.all_gather(local_rows, "tensor", axis=0, tiled=True)


def gather_grads(local_rows):
    return lax.all_gather(local_rows, "tensor", axis=0, tiled=True)


def gather_features(local_cols):
    return lax.all_gather(local_cols, "tensor", axis=1, tiled=True)


def scatter_features(partial_cols):
    return lax.psum_scatter(
        partial_cols.astype(jnp.bfloat16), "tensor", scatter_dimension=1, tiled=True
    ).astype(jnp.float32)


def project_rows(hidden, weight):
    return lax.psum_scatter(
        jnp.einsum("snk,kd->snd", hidden, weight, preferred_element_type=jnp.float32),
        "tensor",
        scatter_dimension=0,
        tiled=True,
    )


def back_rows(grads, weight):
    return lax.psum_scatter(
        jnp.einsum("snf,df->snd", grads, weight, preferred_element_type=jnp.float32),
        "tensor",
        scatter_dimension=0,
        tiled=True,
    )


def lookup_chars(id_block, lookup_table):
    one_hot_matrix = (
        id_block[:, :, None] == lax.broadcasted_iota(jnp.int32, (1, 1, lookup_table.shape[0]), 2)
    ).astype(jnp.bfloat16)
    embedding_rows = jnp.einsum(
        "tmw,wq->tmq", one_hot_matrix, lookup_table, preferred_element_type=jnp.float32
    ).astype(jnp.bfloat16)
    return (one_hot_matrix, embedding_rows)


def char_windows(embedding_rows, span_len):
    positions = embedding_rows.shape[1] - span_len + 1
    return jnp.concatenate(
        [
            embedding_rows[:, start_offset : start_offset + positions, :]
            for start_offset in range(span_len)
        ],
        axis=2,
    )


def pool_block(id_block, lookup_table, conv_w, conv_b):
    one_hot_matrix, embedding_rows = lookup_chars(id_block, lookup_table)
    char_dim = lookup_table.shape[1]
    pieces = []
    start_offset = 0
    for index, item_count in enumerate(width_counts(conv_w.shape[1])):
        span_len = index + 1
        filter_window = char_windows(embedding_rows, span_len)
        convolved_rows = jnp.einsum(
            "npc,cf->npf",
            filter_window,
            conv_w[: char_dim * span_len, start_offset : start_offset + item_count],
            preferred_element_type=jnp.float32,
        ) + conv_b[start_offset : start_offset + item_count].astype(jnp.float32)
        pieces.append(jax.nn.logsumexp(convolved_rows, axis=1) - math.log(filter_window.shape[1]))
        start_offset += item_count
    return jnp.concatenate(pieces, axis=1)


def pool_block_back(id_block, d_pooled, lookup_table, conv_w, conv_b):
    one_hot_matrix, embedding_rows = lookup_chars(id_block, lookup_table)
    char_dim = lookup_table.shape[1]
    chars_word = embedding_rows.shape[1]
    embedding_gradient = jnp.zeros(embedding_rows.shape, jnp.float32)
    weight_parts = []
    bias_parts = []
    start_offset = 0
    for index, item_count in enumerate(width_counts(conv_w.shape[1])):
        span_len = index + 1
        filter_window = char_windows(embedding_rows, span_len)
        positions = filter_window.shape[1]
        weight = conv_w[: char_dim * span_len, start_offset : start_offset + item_count]
        convolved_rows = jnp.einsum(
            "npc,cf->npf", filter_window, weight, preferred_element_type=jnp.float32
        ) + conv_b[start_offset : start_offset + item_count].astype(jnp.float32)
        probs = jax.nn.softmax(convolved_rows, axis=1)
        conv_grad = (d_pooled[:, None, start_offset : start_offset + item_count] * probs).astype(
            jnp.bfloat16
        )
        part_grad = jnp.einsum(
            "npc,npf->cf", filter_window, conv_grad, preferred_element_type=jnp.float32
        )
        weight_parts.append(jnp.pad(part_grad, ((0, conv_w.shape[0] - part_grad.shape[0]), (0, 0))))
        bias_parts.append(jnp.sum(conv_grad.astype(jnp.float32), axis=(0, 1)))
        window_grad = jnp.einsum(
            "npf,cf->npc", conv_grad, weight, preferred_element_type=jnp.float32
        )
        for tap in range(span_len):
            embedding_gradient = embedding_gradient + jnp.pad(
                window_grad[:, :, tap * char_dim : (tap + 1) * char_dim],
                ((0, 0), (tap, chars_word - positions - tap), (0, 0)),
            )
        start_offset += item_count
    table_grad = jnp.einsum(
        "jsu,jsi->ui",
        one_hot_matrix.astype(jnp.float32),
        embedding_gradient,
        precision=lax.Precision.HIGHEST,
    )
    return (jnp.concatenate(weight_parts, axis=1), jnp.concatenate(bias_parts, axis=0), table_grad)


def head_scores(queries, key_rows, seq_lengths):
    raw = jnp.einsum(
        "qnhd,knhd->nhqk", queries, key_rows, preferred_element_type=jnp.float32
    ) * HEAD_DIM ** (-0.5)
    place = lax.broadcasted_iota(jnp.int32, raw.shape, 3)
    return jnp.where(place < seq_lengths[:, None, None, None], raw, big_neg)


def place_piece(piece, dim, tensor_rank, tensor_count):
    full_shape = list(piece.shape)
    full_shape[dim] = full_shape[dim] * tensor_count
    full_array = jnp.zeros(full_shape, jnp.float32)
    starts = [0] * len(full_shape)
    starts[dim] = tensor_rank * piece.shape[dim]
    return lax.dynamic_update_slice(full_array, piece, starts)


def body(
    char_ids,
    seq_lengths,
    char_table,
    conv_weight,
    conv_bias,
    highway_weight,
    highway_bias,
    proj_weight,
    proj_bias,
    norm_gain,
    norm_shift,
    qkv_weight,
    qv_bias,
    output_projection_weight,
    out_bias,
    up_weight,
    up_bias,
    down_weight,
    down_bias,
    out_grad,
):
    slots = char_ids.shape[0]
    nseq = char_ids.shape[1]
    chars_word = char_ids.shape[2]
    word_rows = slots * nseq
    block_rows = min(256, word_rows)
    id_blocks = char_ids.reshape(word_rows // block_rows, block_rows, chars_word)
    gains = norm_gain.astype(jnp.float32)
    shifts = norm_shift.astype(jnp.float32)
    heads_local = qkv_weight.shape[2] // HEAD_DIM
    pooled = lax.map(
        lambda id_block: pool_block(id_block, char_table, conv_weight, conv_bias), id_blocks
    )
    pooled = pooled.reshape(word_rows, -1)
    hidden = jax.nn.silu(pooled)
    kept_layers = []
    for layer in range(highway_weight.shape[0]):
        whole = gather_features(hidden.astype(jnp.bfloat16))
        pre_acts = jnp.einsum(
            "rk,jkf->rjf", whole, highway_weight[layer], preferred_element_type=jnp.float32
        ) + highway_bias[layer].astype(jnp.float32)
        kept_layers.append((hidden, whole, pre_acts))
        hidden = highway_mix(pre_acts, hidden)
    top_sent = hidden.astype(jnp.bfloat16).reshape(slots, nseq, -1)
    embedded = project_rows(top_sent, proj_weight) + proj_bias.astype(jnp.float32)
    inputs = layer_norm(embedded, gains[0], shifts[0])
    rows_first = gather_rows(inputs.astype(jnp.bfloat16))
    projected = jnp.einsum(
        "snd,dkh->snkh", rows_first, qkv_weight, preferred_element_type=jnp.float32
    )
    queries = (
        (projected[:, :, 0] + qv_bias[0].astype(jnp.float32))
        .astype(jnp.bfloat16)
        .reshape(slots, nseq, heads_local, HEAD_DIM)
    )
    key_rows = projected[:, :, 1].astype(jnp.bfloat16).reshape(slots, nseq, heads_local, HEAD_DIM)
    values = (
        (projected[:, :, 2] + qv_bias[1].astype(jnp.float32))
        .astype(jnp.bfloat16)
        .reshape(slots, nseq, heads_local, HEAD_DIM)
    )
    scores = head_scores(queries, key_rows, seq_lengths)
    log_total = jax.nn.logsumexp(scores, axis=3)
    probs = jnp.exp(scores - log_total[..., None])
    attention_result = jnp.einsum(
        "nhqk,knhd->qnhd", probs.astype(jnp.bfloat16), values, preferred_element_type=jnp.float32
    )
    attention_result = attention_result.astype(jnp.bfloat16).reshape(slots, nseq, -1)
    residual_branch = project_rows(attention_result, output_projection_weight) + out_bias.astype(
        jnp.float32
    )
    middle_pre = inputs + residual_branch
    middle = layer_norm(middle_pre, gains[1], shifts[1])
    rows_mid = gather_rows(middle.astype(jnp.bfloat16))
    upper = jnp.einsum(
        "snd,df->snf", rows_mid, up_weight, preferred_element_type=jnp.float32
    ) + up_bias.astype(jnp.float32)
    activated = gelu_exact(upper).astype(jnp.bfloat16)
    branch_two = project_rows(activated, down_weight) + down_bias.astype(jnp.float32)
    final_pre = middle + branch_two
    encoded = layer_norm(final_pre, gains[2], shifts[2]).astype(jnp.bfloat16)
    d_pre2, d_gain2, d_shift2 = norm_back(
        final_pre, gains[2], shifts[2], out_grad.astype(jnp.float32)
    )
    d_branch_two = d_pre2.astype(jnp.bfloat16)
    down_bias_grad = jnp.sum(d_branch_two.astype(jnp.float32), axis=(0, 1))
    grads_down = gather_grads(d_branch_two)
    d_down_w = jnp.einsum("snf,snd->fd", activated, grads_down, preferred_element_type=jnp.float32)
    d_activated = jnp.einsum(
        "snd,fd->snf", grads_down, down_weight, preferred_element_type=jnp.float32
    )
    unused, gelu_pull = jax.vjp(gelu_exact, upper)
    d_upper = gelu_pull(d_activated)[0].astype(jnp.bfloat16)
    up_bias_part = jnp.sum(d_upper.astype(jnp.float32), axis=(0, 1))
    d_up_w = jnp.einsum("snd,snf->df", rows_mid, d_upper, preferred_element_type=jnp.float32)
    d_middle = d_pre2 + back_rows(d_upper, up_weight)
    d_pre1, d_gain1, d_shift1 = norm_back(middle_pre, gains[1], shifts[1], d_middle)
    d_branch = d_pre1.astype(jnp.bfloat16)
    out_bias_grad = jnp.sum(d_branch.astype(jnp.float32), axis=(0, 1))
    attention_gradients = gather_grads(d_branch)
    output_weight_delta = jnp.einsum(
        "xlz,xlw->zw", attention_result, attention_gradients, preferred_element_type=jnp.float32
    )
    d_attended = jnp.einsum(
        "qfi,hi->qfh",
        attention_gradients,
        output_projection_weight,
        preferred_element_type=jnp.float32,
    ).astype(jnp.bfloat16)
    d_heads = d_attended.reshape(slots, nseq, heads_local, HEAD_DIM)
    scores = head_scores(queries, key_rows, seq_lengths)
    probs = jnp.exp(scores - log_total[..., None])
    d_values = jnp.einsum(
        "nhqk,qnhd->knhd", probs.astype(jnp.bfloat16), d_heads, preferred_element_type=jnp.float32
    ).astype(jnp.bfloat16)
    d_probs = jnp.einsum("qnhd,knhd->nhqk", d_heads, values, preferred_element_type=jnp.float32)
    d_scores = (probs * (d_probs - jnp.sum(d_probs * probs, axis=3, keepdims=True))).astype(
        jnp.bfloat16
    )
    d_queries = (
        jnp.einsum("nhqk,knhd->qnhd", d_scores, key_rows, preferred_element_type=jnp.float32)
        * HEAD_DIM ** (-0.5)
    ).astype(jnp.bfloat16)
    d_keys = (
        jnp.einsum("nhqk,qnhd->knhd", d_scores, queries, preferred_element_type=jnp.float32)
        * HEAD_DIM ** (-0.5)
    ).astype(jnp.bfloat16)
    d_proj = jnp.stack([d_queries, d_keys, d_values], axis=2).reshape(slots, nseq, 3, -1)
    qv_part = jnp.stack(
        [
            jnp.sum(d_proj[:, :, 0].astype(jnp.float32), axis=(0, 1)),
            jnp.sum(d_proj[:, :, 2].astype(jnp.float32), axis=(0, 1)),
        ],
        axis=0,
    )
    d_qkv_w = jnp.einsum("snd,snkh->dkh", rows_first, d_proj, preferred_element_type=jnp.float32)
    d_inputs = d_pre1 + back_rows(
        d_proj.reshape(slots, nseq, -1), qkv_weight.reshape(qkv_weight.shape[0], -1)
    )
    d_embedded, d_gain0, d_shift0 = norm_back(embedded, gains[0], shifts[0], d_inputs)
    d_emb_low = d_embedded.astype(jnp.bfloat16)
    proj_bias_grad = jnp.sum(d_emb_low.astype(jnp.float32), axis=(0, 1))
    grads_emb = gather_grads(d_emb_low)
    d_proj_w = jnp.einsum("snk,snd->kd", top_sent, grads_emb, preferred_element_type=jnp.float32)
    d_hidden = jnp.einsum(
        "snd,kd->snk", grads_emb, proj_weight, preferred_element_type=jnp.float32
    ).reshape(word_rows, -1)
    hw_weight_parts = []
    hw_bias_parts = []
    for layer in reversed(range(len(kept_layers))):
        previous, whole, pre_acts = kept_layers[layer]
        unused, mix_pull = jax.vjp(highway_mix, pre_acts, previous)
        d_pre, d_previous = mix_pull(d_hidden)
        d_pre = d_pre.astype(jnp.bfloat16)
        hw_weight_parts.insert(
            0, jnp.einsum("rk,rjf->jkf", whole, d_pre, preferred_element_type=jnp.float32)
        )
        hw_bias_parts.insert(0, jnp.sum(d_pre.astype(jnp.float32), axis=0))
        partial_sum = jnp.einsum(
            "rjf,jkf->rk", d_pre, highway_weight[layer], preferred_element_type=jnp.float32
        )
        d_hidden = d_previous + scatter_features(partial_sum)
    d_hw_w = jnp.stack(hw_weight_parts, axis=0)
    hw_bias_part = jnp.stack(hw_bias_parts, axis=0)
    unused, silu_pull = jax.vjp(jax.nn.silu, pooled)
    d_pooled = silu_pull(d_hidden)[0].reshape(word_rows // block_rows, block_rows, -1)

    def back_step(totals, block_pair):
        weight_grad, bias_grad, table_grad = pool_block_back(
            block_pair[0], block_pair[1], char_table, conv_weight, conv_bias
        )
        return ((totals[0] + weight_grad, totals[1] + bias_grad, totals[2] + table_grad), None)

    start_totals = (
        jnp.zeros(conv_weight.shape, jnp.float32),
        jnp.zeros(conv_bias.shape, jnp.float32),
        jnp.zeros(char_table.shape, jnp.float32),
    )
    totals, unused = lax.scan(back_step, start_totals, (id_blocks, d_pooled))
    conv_w_part, conv_b_part, table_part = totals
    hw_w_grad, proj_w_grad, qkv_w_grad, out_w_grad, up_w_grad, down_w_grad = (
        lax.psum_scatter(d_hw_w, "dp", scatter_dimension=2, tiled=True),
        lax.psum_scatter(d_proj_w, "dp", scatter_dimension=1, tiled=True),
        lax.psum_scatter(d_qkv_w, "dp", scatter_dimension=0, tiled=True),
        lax.psum_scatter(output_weight_delta, "dp", scatter_dimension=1, tiled=True),
        lax.psum_scatter(d_up_w, "dp", scatter_dimension=0, tiled=True),
        lax.psum_scatter(d_down_w, "dp", scatter_dimension=1, tiled=True),
    )
    tensor_rank = lax.axis_index("tensor")
    tensor_count = lax.axis_size("tensor")
    gain_part = jnp.stack([d_gain0, d_gain1, d_gain2], axis=0)
    shift_part = jnp.stack([d_shift0, d_shift1, d_shift2], axis=0)
    small_done = lax.psum(
        (
            table_part,
            place_piece(conv_w_part, 1, tensor_rank, tensor_count),
            place_piece(conv_b_part, 0, tensor_rank, tensor_count),
            place_piece(hw_bias_part, 2, tensor_rank, tensor_count),
            proj_bias_grad,
            gain_part,
            shift_part,
            place_piece(qv_part, 1, tensor_rank, tensor_count),
            out_bias_grad,
            place_piece(up_bias_part, 0, tensor_rank, tensor_count),
            down_bias_grad,
        ),
        ("dp", "tensor"),
    )
    (
        table_grad,
        conv_w_grad,
        conv_b_grad,
        hw_b_grad,
        proj_b_grad,
        gain_grad,
        shift_grad,
        qv_grad,
        out_b_grad,
        up_b_grad,
        down_b_grad,
    ) = small_done
    return (
        encoded,
        table_grad,
        conv_w_grad,
        conv_b_grad,
        hw_w_grad,
        hw_b_grad,
        proj_w_grad,
        proj_b_grad,
        gain_grad,
        shift_grad,
        qkv_w_grad,
        qv_grad,
        out_w_grad,
        out_b_grad,
        up_w_grad,
        up_b_grad,
        down_w_grad,
        down_b_grad,
    )


def solution(mesh):
    return jax.shard_map(
        body,
        mesh=mesh,
        in_specs=(
            P(None, "dp", None),
            P("dp"),
            P(),
            P(None, "tensor"),
            P("tensor"),
            P(None, None, None, "tensor"),
            P(None, None, "tensor"),
            P("tensor", None),
            P(),
            P(),
            P(),
            P(None, None, "tensor"),
            P(None, "tensor"),
            P("tensor", None),
            P(),
            P(None, "tensor"),
            P("tensor"),
            P("tensor", None),
            P(),
            P("tensor", "dp", None),
        ),
        out_specs=(
            P("tensor", "dp", None),
            P(),
            P(),
            P(),
            P(None, None, "dp", "tensor"),
            P(),
            P("tensor", "dp"),
            P(),
            P(),
            P(),
            P("dp", None, "tensor"),
            P(),
            P("tensor", "dp"),
            P(),
            P("dp", "tensor"),
            P(),
            P("tensor", "dp"),
            P(),
        ),
        check_vma=False,
    )
```

profile of v0, /device:TPU:1, one launch (start us, length us, event | category | flops | bytes accessed | tf_op | source)
XLA Modules:
  0.0 1218.2 jit_solution(11447035356953941860)
XLA Ops:
  10.2 51.2 %while.29 = (s32[]{:T(128)}, f32[2,256,512]{2,1,0:T(8,128)S(1)}, s32[2,256,50]{1,2,0:T(8,128)}, bf16[262,16]{0,1:T(8,128)(2,1)}, bf16[112,512]{0,1:T(8,128)(2,1)S(1)}, /*index=5*/bf16[512]{0:T(512)(128)(2,1)}, s32[]{:T(128)}) while((s32[]{:T(128)}, f32[2,256,512]{2,1,0:T(8,128)S(1)}, s32[2,256,50]{1,2,0:T(8,128)}, ...), condition=%wide.region_15.16_spmd, body=%wide.region_0.15_spmd.sunk | while | flops 1279012352 | bytes 85519440 | solution.py:207
  11.9 2.9 fusion.393
  37.4 2.9 fusion.393
  63.3 47.4 %all-gather.3.cloned.1.call-done = bf16[512,2048]{1,0:T(8,128)(2,1)} async-done(((bf16[512,512]{1,0:T(8,128)(2,1)}), bf16[512,2048]{1,0:T(8,128)(2,1)}) %all-gather.3.cloned.1.call-update) | async-done | bytes 2097168 | tf_op jit(solution)/shard_map/all_gather | solution.py:49
  110.7 5.2 fusion.142
  118.0 44.8 %all-gather.5.cloned.1.call-done = bf16[512,2048]{1,0:T(8,128)(2,1)} async-done(((bf16[512,512]{1,0:T(8,128)(2,1)}), bf16[512,2048]{1,0:T(8,128)(2,1)}) %all-gather.5.cloned.1.call-update) | async-done | bytes 2097168 | tf_op jit(solution)/shard_map/all_gather | solution.py:49
  162.8 5.2 fusion.147
  173.1 33.0 %reduce-scatter.16.cloned.1.call-done = f32[128,1,768]{2,0,1:T(8,128)} async-done(((f32[512,1,768]{2,0,1:T(8,128)}), f32[128,1,768]{2,0,1:T(8,128)}) %reduce-scatter.16.cloned.1.call-update) | async-done | bytes 393232 | tf_op jit(solution)/shard_map/reduce_scatter | solution.py:59
  209.7 15.6 %all_gather.23 = bf16[512,1,768]{2,0,1:T(8,128)(2,1)S(1)} all-gather(bf16[128,1,768]{2,0,1:T(8,128)(2,1)S(1)} %fusion.225), channel_id=1, replica_groups=mesh['dp'=8,'tensor'=4] {'tensor'}, dimensions={0}, use_global_device_ids=true | all-gather | bytes 983040 | tf_op jit(solution)/shard_map/all_gather | solution.py:41
  231.8 37.1 %reduce-scatter.18.cloned.1.call-done = f32[128,1,768]{2,0,1:T(8,128)} async-done(((f32[512,1,768]{2,0,1:T(8,128)}), f32[128,1,768]{2,0,1:T(8,128)}) %reduce-scatter.18.cloned.1.call-update) | async-done | bytes 393232 | tf_op jit(solution)/shard_map/reduce_scatter | solution.py:59
  271.1 15.5 %all_gather.24 = bf16[512,1,768]{2,0,1:T(8,128)(2,1)S(1)} all-gather(bf16[128,1,768]{2,0,1:T(8,128)(2,1)S(1)} %fusion.226), channel_id=1, replica_groups=mesh['dp'=8,'tensor'=4] {'tensor'}, dimensions={0}, use_global_device_ids=true | all-gather | bytes 983040 | tf_op jit(solution)/shard_map/all_gather | solution.py:41
  286.7 5.9 multiply_convert_fusion.8
  295.6 37.2 %reduce-scatter.20.cloned.1.call-done = f32[128,1,768]{2,0,1:T(8,128)} async-done(((f32[512,1,768]{2,0,1:T(8,128)}), f32[128,1,768]{2,0,1:T(8,128)}) %reduce-scatter.20.cloned.1.call-update) | async-done | bytes 393232 | tf_op jit(solution)/shard_map/reduce_scatter | solution.py:59
  338.1 15.5 %all_gather.25 = bf16[512,1,768]{2,0,1:T(8,128)(2,1)S(1)} all-gather(bf16[128,1,768]{2,0,1:T(8,128)(2,1)S(1)} %get-tuple-element.422), channel_id=1, replica_groups=mesh['dp'=8,'tensor'=4] {'tensor'}, dimensions={0}, use_global_device_ids=true | all-gather | bytes 983040 | tf_op jit(solution)/shard_map/all_gather | solution.py:45
  357.9 37.3 %reduce-scatter.22.cloned.1.call-done = f32[128,1,768]{2,0,1:T(8,128)} async-done(((f32[512,1,768]{2,0,1:T(8,128)}), f32[128,1,768]{2,0,1:T(8,128)}) %reduce-scatter.22.cloned.1.call-update) | async-done | bytes 393232 | tf_op jit(solution)/shard_map/reduce_scatter | solution.py:68
  397.7 15.7 %all_gather.26 = bf16[512,1,768]{2,0,1:T(8,128)(2,1)S(1)} all-gather(bf16[128,1,768]{2,0,1:T(8,128)(2,1)S(1)} %get-tuple-element.424), channel_id=1, replica_groups=mesh['dp'=8,'tensor'=4] {'tensor'}, dimensions={0}, use_global_device_ids=true | all-gather | bytes 983040 | tf_op jit(solution)/shard_map/all_gather | solution.py:45
  421.7 37.2 %reduce-scatter.24.cloned.1.call-done = f32[128,1,768]{2,0,1:T(8,128)} async-done(((f32[512,1,768]{2,0,1:T(8,128)}), f32[128,1,768]{2,0,1:T(8,128)}) %reduce-scatter.24.cloned.1.call-update) | async-done | bytes 393232 | tf_op jit(solution)/shard_map/reduce_scatter | solution.py:68
  461.4 15.8 %all_gather.27 = bf16[512,1,768]{2,0,1:T(8,128)(2,1)S(1)} all-gather(bf16[128,1,768]{2,0,1:T(8,128)(2,1)S(1)} %get-tuple-element.426), channel_id=1, replica_groups=mesh['dp'=8,'tensor'=4] {'tensor'}, dimensions={0}, use_global_device_ids=true | all-gather | bytes 983040 | tf_op jit(solution)/shard_map/all_gather | solution.py:45
  481.1 5.9 bitcast_convert_fusion.1
  487.1 45.9 %reduce-scatter.26.cloned.1.call-done = bf16[512,512]{1,0:T(8,128)(2,1)} async-done(((bf16[512,2048]{1,0:T(8,128)(2,1)}), bf16[512,512]{1,0:T(8,128)(2,1)}) %reduce-scatter.26.cloned.1.call-update) | async-done | bytes 524304 | tf_op jit(solution)/shard_map/reduce_scatter | solution.py:53
  537.5 5.9 bitcast_convert_fusion
  546.4 4.8 convolution_bitcast_fusion.7
  553.7 6.1 pad_maximum_fusion.9
  559.8 3.5 fusion.208
  563.4 3.7 fusion.202
  567.2 3.6 fusion.194
  578.4 8.4 reduce-scatter.28.cloned.1.call-done
  586.8 3.1 fusion.168
  589.9 184.8 %while.30 = (s32[]{:T(128)}, f32[112,512]{1,0:T(8,128)}, f32[512]{0:T(512)}, f32[262,16]{0,1:T(8,128)}, s32[2,256,50]{1,2,0:T(8,128)}, /*index=5*/bf16[262,16]{0...) while((s32[]{:T(128)}, f32[112,512]{1,0:T(8,128)}, ...), condition=%wide.region_60.61_spmd.clone, body=%wide.region_38.60_spmd.clone.sunk | while | flops 4237749504 | bytes 389838272 | solution.py:355
  641.9 5.2 convert_reduce_fusion.30
  647.1 3.9 convolution_bitcast_fusion.27
  654.5 3.2 fusion.445
  660.8 6.9 convert_reduce_fusion.31
  671.8 4.8 fusion.446
  687.1 6.3 fusion.459
  724.4 4.2 convert_reduce_fusion.30
  728.5 3.6 convolution_bitcast_fusion.27
  735.5 3.2 fusion.445
  741.8 6.5 convert_reduce_fusion.31
  752.3 4.8 fusion.446
  767.7 6.3 fusion.459
  780.0 2.9 copy.122
  782.8 7.4 reduce-scatter.36.cloned.1.call-done
  790.3 46.8 %reduce-scatter.38.cloned.1.call-done = f32[768,96]{0,1:T(8,128)} async-done(((f32[768,768]{0,1:T(8,128)}), f32[768,96]{0,1:T(8,128)}) %reduce-scatter.38.cloned.1.call-update) | async-done | bytes 294928 | tf_op jit(solution)/shard_map/reduce_scatter | solution.py:363
  837.1 46.3 %reduce-scatter.34.cloned.1.call-done = f32[96,3,192]{2,0,1:T(8,128)} async-done(((f32[768,3,192]{2,0,1:T(8,128)}), f32[96,3,192]{2,0,1:T(8,128)}) %reduce-scatter.34.cloned.1.call-update) | async-done | bytes 221200 | tf_op jit(solution)/shard_map/reduce_scatter | solution.py:360
  883.3 42.5 %reduce-scatter.32.cloned.1.call-done = f32[512,96]{0,1:T(8,128)} async-done(((f32[512,768]{0,1:T(8,128)}), f32[512,96]{0,1:T(8,128)}) %reduce-scatter.32.cloned.1.call-update) | async-done | bytes 196624 | tf_op jit(solution)/shard_map/reduce_scatter | solution.py:359
  925.9 136.4 %all-reduce.43.cloned.1.call-done = (f32[262,16]{0,1:T(8,128)}, f32[2048]{0:T(1024)}, f32[2,2,2048]{2,1,0:T(2,128)}, f32[768]{0:T(1024)}, f32[3,768]{1,0:T(4,128...) async-done(((f32[262,16]{0,1:T(8,128)}, f32[2048]{0:T(1024)}, f32[2,2,2048]{2,1,0:T(2,128)}, f32[768]{0:T(1024)}, ...) | async-done | bytes 103824 | tf_op jit(solution)/shard_map/psum | solution.py:369
  1062.3 133.8 %all-reduce.41.cloned.1.call-done = f32[112,2048]{1,0:T(8,128)} async-done(((f32[112,2048]{1,0:T(8,128)}), f32[112,2048]{1,0:T(8,128)}) %all-reduce.41.cloned.1.call-update) | async-done | bytes 917520 | tf_op jit(solution)/shard_map/psum | solution.py:369
  (742 shorter events, 238.8 us)
Async XLA Ops:
  7.2 279.5 %copy-start = (bf16[768,768]{1,0:T(8,128)(2,1)S(1)}, bf16[768,768]{1,0:T(8,128)(2,1)}, u32[]{:S(2)}) copy-start(bf16[768,768]{1,0:T(8,128)(2,1)} %param.39) | copy-start | bytes 3538948
  7.2 103.5 %all-gather.3.cloned.1.call-start = ((), (), s32[]{:S(2)}) async-start(), calls=%async_computation.13 | async-start | bytes 2621440 | tf_op jit(solution)/shard_map/all_gather | solution.py:49
  61.4 49.3 %copy-start.13 = (f32[2,256,512]{2,1,0:T(8,128)}, f32[2,256,512]{2,1,0:T(8,128)S(1)}, u32[]{:S(2)}) copy-start(f32[2,256,512]{2,1,0:T(8,128)S(1)} %get-tuple-element.216) | copy-start | bytes 3145732
  62.6 100.2 %all-gather.5.cloned.1.call-start = ((), (), s32[]{:S(2)}) async-start(), calls=%async_computation.14 | async-start | bytes 2621440 | tf_op jit(solution)/shard_map/all_gather | solution.py:49
  110.7 5.2 copy-start.14
  118.0 88.2 %reduce-scatter.16.cloned.1.call-start = ((), (), s32[]{:S(2)}) async-start(), calls=%async_computation.15 | async-start | bytes 1966080 | tf_op jit(solution)/shard_map/reduce_scatter | solution.py:59
  162.8 5.2 copy-start.15
  172.1 96.9 %reduce-scatter.18.cloned.1.call-start = ((), (), s32[]{:S(2)}) async-start(), calls=%async_computation.16 | async-start | bytes 1966080 | tf_op jit(solution)/shard_map/reduce_scatter | solution.py:59
  206.1 19.2 %copy-start.54 = (bf16[768,3,192]{0,2,1:T(8,128)(2,1)S(1)}, bf16[768,3,192]{0,2,1:T(8,128)(2,1)}, u32[]{:S(2)}) copy-start(bf16[768,3,192]{0,2,1:T(8,128)(2,1)} %param.35) | copy-start | bytes 2654212
  231.7 101.2 %reduce-scatter.20.cloned.1.call-start = ((), (), s32[]{:S(2)}) async-start(), calls=%async_computation.17 | async-start | bytes 1966080 | tf_op jit(solution)/shard_map/reduce_scatter | solution.py:59
  286.7 6.0 copy-start.43
  286.7 6.9 copy-start.102
  295.5 99.7 %reduce-scatter.22.cloned.1.call-start = ((), (), s32[]{:S(2)}) async-start(), calls=%async_computation.18 | async-start | bytes 1966080 | tf_op jit(solution)/shard_map/reduce_scatter | solution.py:68
  332.9 20.8 %copy-start.103 = (bf16[768,768]{1,0:T(8,128)(2,1)S(1)}, bf16[768,768]{1,0:T(8,128)(2,1)}, u32[]{:S(2)}) copy-start(bf16[768,768]{1,0:T(8,128)(2,1)} %param.41) | copy-start | bytes 3538948
  332.9 20.8 %copy-start.106 = (f32[512,768]{1,0:T(8,128)S(1)}, f32[512,768]{1,0:T(8,128)}, u32[]{:S(2)}) copy-start(f32[512,768]{1,0:T(8,128)} %get-tuple-element.438) | copy-start | bytes 4718596
  332.9 20.8 %copy-start.107 = (f32[512,768]{1,0:T(8,128)S(1)}, f32[512,768]{1,0:T(8,128)}, u32[]{:S(2)}) copy-start(f32[512,768]{1,0:T(8,128)} %get-tuple-element.531) | copy-start | bytes 4718596
  357.8 38.9 %copy-start.24 = (f32[128,1,768]{2,0,1:T(8,128)S(1)}, f32[128,1,768]{2,0,1:T(8,128)}, u32[]{:S(2)}) copy-start(f32[128,1,768]{2,0,1:T(8,128)} %copy-done.23) | copy-start | bytes 1179652
  357.9 101.0 %reduce-scatter.24.cloned.1.call-start = ((), (), s32[]{:S(2)}) async-start(), calls=%async_computation.19 | async-start | bytes 1966080 | tf_op jit(solution)/shard_map/reduce_scatter | solution.py:68
  396.7 18.4 %copy-start.10 = (f32[3,512,512]{1,2,0:T(8,128)S(1)}, f32[3,512,512]{1,2,0:T(8,128)}, u32[]{:S(2)}) copy-start(f32[3,512,512]{1,2,0:T(8,128)} %copy-done.9) | copy-start | bytes 9437188
  419.7 39.2 %copy-start.21 = (f32[128,1,768]{2,0,1:T(8,128)S(1)}, f32[128,1,768]{2,0,1:T(8,128)}, u32[]{:S(2)}) copy-start(f32[128,1,768]{2,0,1:T(8,128)} %reduce-scatter.16.cloned.1.call-done) | copy-start | bytes 1179652
  419.7 39.2 %copy-start.59 = (f32[128,1,768]{2,0,1:T(8,128)S(1)}, f32[128,1,768]{2,0,1:T(8,128)}, u32[]{:S(2)}) copy-start(f32[128,1,768]{2,0,1:T(8,128)} %copy-done.58) | copy-start | bytes 1179652
  421.7 111.2 %reduce-scatter.26.cloned.1.call-start = ((), (), s32[]{:S(2)}) async-start(), calls=%async_computation.20 | async-start | bytes 2621440 | tf_op jit(solution)/shard_map/reduce_scatter | solution.py:53
  458.9 19.1 %copy-start.62 = (bf16[512,768]{1,0:T(8,128)(2,1)S(1)}, bf16[512,768]{1,0:T(8,128)(2,1)}, u32[]{:S(2)}) copy-start(bf16[512,768]{1,0:T(8,128)(2,1)} %param.31) | copy-start | bytes 2359300
  460.6 18.1 %copy-start.27 = (f32[512,2,512]{2,0,1:T(8,128)S(1)}, f32[512,2,512]{2,0,1:T(8,128)}, u32[]{:S(2)}) copy-start(f32[512,2,512]{2,0,1:T(8,128)} %copy-done.26) | copy-start | bytes 6291460
  460.6 18.1 %copy-start.52 = (f32[512,512]{1,0:T(8,128)S(1)}, f32[512,512]{1,0:T(8,128)}, u32[]{:S(2)}) copy-start(f32[512,512]{1,0:T(8,128)} %get-tuple-element.442) | copy-start | bytes 3145732
  487.0 48.5 %copy-start.16 = (f32[2,256,512]{2,1,0:T(8,128)S(1)}, f32[2,256,512]{2,1,0:T(8,128)}, u32[]{:S(2)}) copy-start(f32[2,256,512]{2,1,0:T(8,128)} %copy-done.13) | copy-start | bytes 3145732
  487.0 99.7 %reduce-scatter.28.cloned.1.call-start = ((), (), s32[]{:S(2)}) async-start(), calls=%async_computation.21 | async-start | bytes 2621440 | tf_op jit(solution)/shard_map/reduce_scatter | solution.py:53
  543.4 234.8 %reduce-scatter.40.cloned.1.call-start = ((), (), s32[]{:S(2)}) async-start(), calls=%async_computation.28 | async-start | bytes 884736
  546.0 233.9 %reduce-scatter.30.cloned.1.call-start = ((), (), s32[]{:S(2)}) async-start(), calls=%async_computation.23 | async-start | bytes 18874368 | tf_op jit(solution)/shard_map/reduce_scatter | solution.py:358
  559.7 230.5 %reduce-scatter.36.cloned.1.call-start = ((), (), s32[]{:S(2)}) async-start(), calls=%async_computation.26 | async-start | bytes 2654208 | tf_op jit(solution)/shard_map/reduce_scatter | solution.py:362
  563.4 273.7 %reduce-scatter.38.cloned.1.call-start = ((), (), s32[]{:S(2)}) async-start(), calls=%async_computation.27 | async-start | bytes 2654208 | tf_op jit(solution)/shard_map/reduce_scatter | solution.py:363
  567.1 316.2 %reduce-scatter.34.cloned.1.call-start = ((), (), s32[]{:S(2)}) async-start(), calls=%async_computation.25 | async-start | bytes 2654208 | tf_op jit(solution)/shard_map/reduce_scatter | solution.py:360
  570.7 355.1 %reduce-scatter.32.cloned.1.call-start = ((), (), s32[]{:S(2)}) async-start(), calls=%async_computation.24 | async-start | bytes 1769472 | tf_op jit(solution)/shard_map/reduce_scatter | solution.py:359
  575.4 486.9 %all-reduce.43.cloned.1.call-start = ((), (), s32[]{:S(2)}) async-start(), calls=%async_computation.29 | async-start | bytes 241664 | tf_op jit(solution)/shard_map/psum | solution.py:369
  578.4 11.5 copy-start.78
  578.4 11.5 copy-start.80
  578.4 11.5 copy-start.104
  610.7 22.0 %copy-start.17 = (bf16[112,512]{0,1:T(8,128)(2,1)}, bf16[112,512]{0,1:T(8,128)(2,1)S(1)}, u32[]{:S(2)}) copy-start(bf16[112,512]{0,1:T(8,128)(2,1)S(1)} %get-tuple-element.873) | copy-start | bytes 344068 | tf_op jit(solution)/shard_map/while
  660.8 9.4 copy-start.8
  671.6 5.0 copy-start.32
  671.8 4.8 copy-start.82
  687.1 7.0 copy-start.105
  694.0 22.0 %copy-start.17 = (bf16[112,512]{0,1:T(8,128)(2,1)}, bf16[112,512]{0,1:T(8,128)(2,1)S(1)}, u32[]{:S(2)}) copy-start(bf16[112,512]{0,1:T(8,128)(2,1)S(1)} %get-tuple-element.873) | copy-start | bytes 344068 | tf_op jit(solution)/shard_map/while
  741.8 9.0 copy-start.8
  752.2 4.9 copy-start.32
  767.7 7.0 copy-start.105
  776.1 419.9 %all-reduce.41.cloned.1.call-start = ((), (), s32[]{:S(2)}) async-start(), calls=%async_computation.22 | async-start | bytes 1835008 | tf_op jit(solution)/shard_map/psum | solution.py:369
  778.2 433.1 %copy-start.1 = (bf16[768,768]{1,0:T(8,128)(2,1)S(1)}, bf16[768,768]{1,0:T(8,128)(2,1)}, u32[]{:S(2)}) copy-start(bf16[768,768]{1,0:T(8,128)(2,1)} %param.39) | copy-start | bytes 3538948
  (115 other events, 201.0 us)
Sparse Core Ops, SparseCore 0:
  62.7 47.9 all-gather.2
  118.1 44.6 all-gather.4
  172.2 33.9 reduce-scatter.15
  231.8 37.0 reduce-scatter.17
  295.7 37.1 reduce-scatter.19
  358.0 37.1 reduce-scatter.21
  421.8 37.0 reduce-scatter.23
  487.1 45.7 reduce-scatter.25
  543.5 43.1 reduce-scatter.27
  589.8 34.3 reduce-scatter.39
  627.7 116.2 reduce-scatter.29
  747.7 42.4 reduce-scatter.35
  794.6 42.4 reduce-scatter.37
  840.8 42.4 reduce-scatter.33
  887.4 38.4 reduce-scatter.31
  935.0 127.2 all-reduce.42
  1067.9 128.1 all-reduce.40
where the time goes:
time: 1230 us; the launch traced here: 1220 us
  waiting for transfers between devices  742 us (60%)
  matrix products  149 us (12%)
  local copies, waits for them, and re-layouts  112 us (9%)
  other arithmetic  97.5 us (8%)
  blocking collectives  78.2 us (6%)
  loops' own time  23.3 us (2%)
  between operations  16 us (1%)
    psum x2, waiting for transfers between devices, body(): lax.psum((table_part, place_piece(conv_w_part, 1, tensor_rank, tensor_cou...  270 us
    reduce_scatter x3, waiting for transfers between devices, project_rows(): lax.psum_scatter(jnp.einsum('snk,kd->snd', hidden, weight, preferred_elem...  107 us
    all_gather x2, waiting for transfers between devices, gather_features(): return lax.all_gather(local_cols, 'tensor', axis=1, tiled=True)  92.1 us
    reduce_scatter x2, waiting for transfers between devices, back_rows(): lax.psum_scatter(jnp.einsum('snf,df->snd', grads, weight, preferred_eleme...  74.5 us
    reduce_scatter x2, waiting for transfers between devices, scatter_features(): lax.psum_scatter(partial_cols.astype(jnp.bfloat16), 'tensor', scatter_dim...  54.2 us
    all_gather x3, blocking collectives, gather_grads(): return lax.all_gather(local_rows, 'tensor', axis=0, tiled=True)  47 us
    reduce_scatter x1, waiting for transfers between devices, body(): lax.psum_scatter(d_down_w, 'dp', scatter_dimension=1, tiled=True)  46.8 us
    reduce_scatter x1, waiting for transfers between devices, body(): lax.psum_scatter(d_qkv_w, 'dp', scatter_dimension=0, tiled=True)  46.3 us
  transfers between devices with their start and end apart: 17, of which 15 were waited for; matrix products, arithmetic and copies ran while one was open for 15% of the time, Pallas kernels for 0%

commit v1 on v0

v1 whole, which is shorter than its diff:
```python
import functools
import math

import jax
import jax.numpy as jnp
import numpy as np
from jax import lax
from jax.experimental import pallas as pl
from jax.experimental.pallas import tpu as pltpu
from jax.sharding import PartitionSpec as P

HEAD_DIM = 64
WORD_TILE = 16
LANES = 128

norm_eps = 1e-06
big_neg = -1e30
f32 = jnp.float32
bf16 = jnp.bfloat16
MESH = pl.DeviceIdType.MESH
VMEM = pl.BlockSpec(memory_space=pltpu.VMEM)
ANY = pl.BlockSpec(memory_space=pl.ANY)
DMA = pltpu.SemaphoreType.DMA
MIB = 1 << 20


def params(cid, vmem):
    return pltpu.CompilerParams(
        collective_id=cid, has_side_effects=True, vmem_limit_bytes=vmem * MIB
    )


def width_counts(block):
    unit = block // 64
    return [unit, unit, 2 * unit, 4 * unit, 8 * unit, 16 * unit, 32 * unit]


def filter_widths(block):
    return np.concatenate(
        [np.full((n,), i + 1, np.int32) for i, n in enumerate(width_counts(block))]
    )


def dot(a, b, ca, cb):
    return lax.dot_general(a, b, (((ca,), (cb,)), ((), ())), preferred_element_type=f32)


def line_barrier(me, count):
    barrier = pltpu.get_barrier_semaphore()
    for there, ok in ((me - 1, me > 0), (me + 1, me < count - 1)):

        @pl.when(ok)
        def greet():
            pl.semaphore_signal(barrier, inc=1, device_id={"tensor": there}, device_id_type=MESH)

    pl.semaphore_wait(barrier, jnp.minimum(me, 1) + jnp.minimum(count - 1 - me, 1))


def line_copy(view, me, count, right, block, chunk, sems):
    send, recv = sems[:2] if right else sems[2:]
    to = jnp.minimum(me + 1, count - 1) if right else jnp.maximum(me - 1, 0)
    ref = view(block, chunk)
    return pltpu.make_async_remote_copy(
        src_ref=ref,
        dst_ref=ref,
        send_sem=send.at[block, chunk],
        recv_sem=recv.at[block, chunk],
        device_id={"tensor": to},
        device_id_type=MESH,
    )


def gather_step(view, step, chunks, me, count, sems):
    for hop in range(count):
        chunk = step - hop
        here = (chunk >= 0) & (chunk < chunks)
        safe = jnp.clip(chunk, 0, chunks - 1)
        for right in (True, False):
            block = me - hop if right else me + hop
            there = (block >= 0) & (block < count)
            block = jnp.clip(block, 0, count - 1)
            more = me < count - 1 if right else me > 0
            copy = functools.partial(line_copy, view, me, count, right, block, safe, sems)

            @pl.when(here & there)
            def pass_on():
                if hop > 0:
                    copy().wait_recv()

                @pl.when(more)
                def send():
                    copy().start()


def gather_drain(view, chunks, me, count, sems):
    def one(chunk, carry):
        for hop in range(count):
            for right in (True, False):
                block = me - hop if right else me + hop
                there = (block >= 0) & (block < count)
                block = jnp.clip(block, 0, count - 1)
                more = me < count - 1 if right else me > 0
                copy = functools.partial(line_copy, view, me, count, right, block, chunk, sems)

                @pl.when(there & more)
                def sent():
                    copy().wait_send()

        return carry

    lax.fori_loop(0, chunks, one, 0)


def windows(y_ref, start, chars):
    group = lax.broadcasted_iota(jnp.int32, (1, WORD_TILE, LANES), 2) // 16
    tile = pl.ds(start, WORD_TILE)
    value = y_ref[0:chars, tile, :]
    for tap in range(1, 7):
        value = jnp.where(group == tap, y_ref[tap : chars + tap, tile, :], value)
    return value.reshape(chars * WORD_TILE, LANES)


def conv_forward_kernel(count, chars, chunks, y_ref, w_ref, off_ref, log_ref, whole_ref, *sems):
    me = lax.axis_index("tensor")
    words, filters = log_ref.shape
    rows = words // chunks
    line_barrier(me, count)

    def view(block, chunk):
        return whole_ref.at[
            pl.ds(pl.multiple_of(chunk * rows, rows), rows),
            pl.ds(pl.multiple_of(block * filters, filters), filters),
        ]

    def tile_step(index, carry):
        start = pl.multiple_of(index * WORD_TILE, WORD_TILE)
        conv = dot(windows(y_ref, start, chars), w_ref[...], 1, 0)
        conv = conv.reshape(chars, WORD_TILE, filters)
        top = jnp.max(conv, axis=0)
        total = top + jnp.log(jnp.sum(jnp.exp(conv - top[None]), axis=0))
        log_ref[pl.ds(start, WORD_TILE), :] = total
        pooled = total - off_ref[...]
        whole_ref[
            pl.ds(start, WORD_TILE), pl.ds(pl.multiple_of(me * filters, filters), filters)
        ] = (pooled * jax.nn.sigmoid(pooled)).astype(bf16)
        return carry

    per = rows // WORD_TILE

    def chunk_step(step, carry):
        @pl.when(step < chunks)
        def work():
            lax.fori_loop(step * per, step * per + per, tile_step, 0)

        gather_step(view, step, chunks, me, count, sems)
        return carry

    lax.fori_loop(0, chunks + count - 1, chunk_step, 0)
    gather_drain(view, chunks, me, count, sems)


def conv_forward(y, w, off, count, chars, cid):
    words, filters = y.shape[1], w.shape[1]
    chunks = 8
    return pl.pallas_call(
        functools.partial(conv_forward_kernel, count, chars, chunks),
        out_shape=(
            jax.ShapeDtypeStruct((words, filters), f32),
            jax.ShapeDtypeStruct((words, count * filters), bf16),
        ),
        in_specs=[VMEM] * 3,
        out_specs=(VMEM, VMEM),
        scratch_shapes=[DMA((count, chunks))] * 4,
        compiler_params=params(cid, 40),
        name="conv_forward",
    )(y, w, off)


def gather_kernel(count, chunks, x_ref, whole_ref, *sems):
    me = lax.axis_index("tensor")
    words, filters = x_ref.shape
    rows = words // chunks
    whole_ref[:, pl.ds(pl.multiple_of(me * filters, filters), filters)] = x_ref[...]
    line_barrier(me, count)

    def view(block, chunk):
        return whole_ref.at[
            pl.ds(pl.multiple_of(chunk * rows, rows), rows),
            pl.ds(pl.multiple_of(block * filters, filters), filters),
        ]

    def chunk_step(step, carry):
        gather_step(view, step, chunks, me, count, sems)
        return carry

    lax.fori_loop(0, chunks + count - 1, chunk_step, 0)
    gather_drain(view, chunks, me, count, sems)


def gather_features(x, count, cid):
    chunks = 4
    return pl.pallas_call(
        functools.partial(gather_kernel, count, chunks),
        out_shape=jax.ShapeDtypeStruct((x.shape[0], count * x.shape[1]), bf16),
        in_specs=[VMEM],
        out_specs=VMEM,
        scratch_shapes=[DMA((count, chunks))] * 4,
        compiler_params=params(cid, 16),
        name="gather_features",
    )(x)


def sum_kernel(count, chunks, p_ref, out_ref, from_left, from_right, s_right, r_right, s_left, r_left):
    me = lax.axis_index("tensor")
    rows = p_ref.shape[0] // chunks
    line_barrier(me, count)

    def tile(chunk):
        return pl.ds(pl.multiple_of(chunk * rows, rows), rows)

    def copies(right, chunk):
        buf = from_left if right else from_right
        send, recv = (s_right, r_right) if right else (s_left, r_left)
        to = jnp.minimum(me + 1, count - 1) if right else jnp.maximum(me - 1, 0)
        first, passed = [
            functools.partial(
                pltpu.make_async_remote_copy,
                src_ref=src.at[tile(chunk)],
                dst_ref=buf.at[tile(chunk)],
                send_sem=send.at[chunk],
                recv_sem=recv.at[chunk],
                device_id={"tensor": to},
                device_id_type=MESH,
            )
            for src in (p_ref, buf)
        ]
        return buf, first, passed

    def step_fn(step, carry):
        for right in (True, False):
            lag = me if right else count - 1 - me
            chunk = step - lag
            here = (chunk >= 0) & (chunk < chunks)
            chunk = jnp.clip(chunk, 0, chunks - 1)
            buf, first, passed = copies(right, chunk)

            @pl.when(here & (lag == 0))
            def start():
                first().start()

            @pl.when(here & (lag > 0))
            def middle():
                first().wait_recv()
                got = buf[tile(chunk), :].astype(f32)

                @pl.when(lag < count - 1)
                def forward():
                    buf[tile(chunk), :] = (got + p_ref[tile(chunk), :].astype(f32)).astype(bf16)
                    passed().start()

                out_ref[tile(chunk), :] += got

        return carry

    out_ref[...] = p_ref[...].astype(f32)
    lax.fori_loop(0, chunks + count - 1, step_fn, 0)

    def drain(chunk, carry):
        for right in (True, False):
            lag = me if right else count - 1 - me

            @pl.when(lag < count - 1)
            def sent():
                copies(right, chunk)[1]().wait_send()

        return carry

    lax.fori_loop(0, chunks, drain, 0)


def sum_rows(partial, count, cid):
    chunks = 8
    shape = partial.shape
    return pl.pallas_call(
        functools.partial(sum_kernel, count, chunks),
        out_shape=jax.ShapeDtypeStruct(shape, f32),
        in_specs=[VMEM],
        out_specs=VMEM,
        scratch_shapes=[pltpu.VMEM(shape, bf16)] * 2 + [DMA((chunks,))] * 4,
        compiler_params=params(cid, 16),
        name="sum_rows",
    )(partial)


def scatter_kernel(count, chunks, p_ref, out_ref, from_left, from_right, *sems):
    me = lax.axis_index("tensor")
    words, filters = out_ref.shape
    rows = words // chunks
    line_barrier(me, count)

    def copies(right, block, chunk):
        buf = from_left if right else from_right
        send, recv = sems[:2] if right else sems[2:]
        to = jnp.minimum(me + 1, count - 1) if right else jnp.maximum(me - 1, 0)
        tile = pl.ds(pl.multiple_of(chunk * rows, rows), rows)
        lanes = pl.ds(pl.multiple_of(block * filters, filters), filters)
        first, passed = [
            functools.partial(
                pltpu.make_async_remote_copy,
                src_ref=src.at[tile, lanes],
                dst_ref=buf.at[tile, lanes],
                send_sem=send.at[block, chunk],
                recv_sem=recv.at[block, chunk],
                device_id={"tensor": to},
                device_id_type=MESH,
            )
            for src in (p_ref, buf)
        ]
        return buf, tile, lanes, first, passed

    out_ref[...] = p_ref[:, pl.ds(pl.multiple_of(me * filters, filters), filters)].astype(f32)
    messages = chunks * (count - 1)

    def step_fn(step, carry):
        for right in (True, False):
            lag = me if right else count - 1 - me
            number = step - lag
            here = (number >= 0) & (number < messages)
            number = jnp.clip(number, 0, messages - 1)
            chunk = number // (count - 1)
            far = count - 1 - number % (count - 1)
            block = far if right else count - 1 - far
            buf, tile, lanes, first, passed = copies(right, block, chunk)

            @pl.when(here & (lag == 0))
            def start():
                first().start()

            @pl.when(here & (lag > 0) & (far > lag))
            def middle():
                first().wait_recv()
                buf[tile, lanes] = (
                    buf[tile, lanes].astype(f32) + p_ref[tile, lanes].astype(f32)
                ).astype(bf16)
                passed().start()

            @pl.when(here & (lag > 0) & (far == lag))
            def last():
                first().wait_recv()
                out_ref[tile, :] += buf[tile, lanes].astype(f32)

        return carry

    lax.fori_loop(0, messages + count - 1, step_fn, 0)

    def drain(number, carry):
        chunk = number // (count - 1)
        far = count - 1 - number % (count - 1)
        for right in (True, False):
            lag = me if right else count - 1 - me
            block = far if right else count - 1 - far

            @pl.when(far > lag)
            def sent():
                copies(right, block, chunk)[3]().wait_send()

        return carry

    lax.fori_loop(0, messages, drain, 0)


def scatter_features(partial, count, cid):
    chunks = 8
    words, whole = partial.shape
    return pl.pallas_call(
        functools.partial(scatter_kernel, count, chunks),
        out_shape=jax.ShapeDtypeStruct((words, whole // count), f32),
        in_specs=[VMEM],
        out_specs=VMEM,
        scratch_shapes=[pltpu.VMEM((words, whole), bf16)] * 2 + [DMA((count, chunks))] * 4,
        compiler_params=params(cid, 20),
        name="scatter_features",
    )(partial)


def conv_backward_kernel(count, chars, chunks, cuts, ids_ref, y_ref, w_ref, wb_ref, off_ref,
                         log_ref, prev_ref, part_ref, *rest):
    if cuts:
        (hw_ref, tr_ref, dw_ref, table_ref, hw_out, tr_out, pad_ref, got_ref, part_send, part_recv,
         hw0, hw0_in, tr0, tr0_in, hwa1, hwb1, tra1, trb1, hwa2, hwb2, tra2, trb2,
         local_sem, dp_send, dp_recv) = rest
    else:
        dw_ref, table_ref, pad_ref, got_ref, part_send, part_recv = rest
    me = lax.axis_index("tensor")
    place = lax.axis_index("dp")
    words, filters = log_ref.shape
    rows = words // chunks
    padded = y_ref.shape[0]
    cell = [place % 2, (place // 2) % 2, place // 4]
    peers = [{"dp": place + (1 - 2 * cell[bit]) * 2**bit} for bit in range(3)] if cuts else []
    peers += [{"tensor": lax.rem(me + k, count)} for k in range(1, count)]
    barrier = pltpu.get_barrier_semaphore()
    for peer in peers:
        pl.semaphore_signal(barrier, inc=1, device_id=peer, device_id_type=MESH)
    pl.semaphore_wait(barrier, len(peers))

    def part_copy(hop, chunk):
        to = lax.rem(me + hop, count)
        tile = pl.ds(pl.multiple_of(chunk * rows, rows), rows)
        return pltpu.make_async_remote_copy(
            src_ref=part_ref.at[tile, pl.ds(pl.multiple_of(to * filters, filters), filters)],
            dst_ref=got_ref.at[hop - 1, tile],
            send_sem=part_send.at[hop - 1, chunk],
            recv_sem=part_recv.at[hop - 1, chunk],
            device_id={"tensor": to},
            device_id_type=MESH,
        )

    def part_start(chunk, carry):
        for hop in range(1, count):
            part_copy(hop, chunk).start()
        return carry

    lax.fori_loop(0, chunks, part_start, 0)

    stages = []
    if cuts:
        c, x, y = cell
        half = hw_ref.shape[0] // 2
        lane_a, lane_b = tra1.shape[-1], trb1.shape[-1]
        part_a, part_b = pl.ds(0, lane_a), pl.ds(lane_a, lane_b)

        def remote(number, src, dst, bit):
            return pltpu.make_async_remote_copy(
                src_ref=src, dst_ref=dst, send_sem=dp_send.at[number], recv_sem=dp_recv.at[number],
                device_id=peers[bit], device_id_type=MESH,
            )

        keep = [
            pltpu.make_async_copy(hw_ref.at[:, :, :, c], hw0, local_sem.at[0]),
            pltpu.make_async_copy(tr_ref.at[:, :, c], tr0, local_sem.at[1]),
        ]
        stages = [
            [
                remote(0, hw_ref.at[:, :, :, 1 - c], hw0_in, 0),
                remote(1, tr_ref.at[:, :, 1 - c], tr0_in, 0),
            ],
            [
                remote(2, hw0.at[pl.ds(0, half), :, 1 - x], hwa1, 1),
                remote(3, hw0.at[pl.ds(half, half), 1 - y], hwb1, 2),
                remote(4, tr0.at[:, 1 - x, :, part_a], tra1, 1),
                remote(5, tr0.at[1 - y, :, :, part_b], trb1, 2),
            ],
            [
                remote(6, hw0.at[pl.ds(0, half), 1 - y, x], hwa2, 2),
                remote(7, hw0.at[pl.ds(half, half), y, 1 - x], hwb2, 1),
                remote(8, tr0.at[1 - y, x, :, part_a], tra2, 2),
                remote(9, tr0.at[y, 1 - x, :, part_b], trb2, 1),
            ],
        ]

        def add(ref, index, other):
            ref[index] = (ref[index].astype(f32) + other.astype(f32)).astype(bf16)

        def after0():
            for copy in keep:
                copy.wait()
            for copy in stages[0]:
                copy.wait()

            def one(k, carry):
                for i in range(2):
                    for j in range(2):
                        add(hw0, (k, i, j), hw0_in[k, i, j])
                return carry

            lax.fori_loop(0, 2 * half, one, 0)
            for i in range(2):
                for j in range(2):
                    add(tr0, (i, j), tr0_in[i, j])

        def after1():
            for copy in stages[1]:
                copy.wait()

            def one(k, carry):
                for i in range(2):
                    add(hw0, (k, i, x), hwa1[k, i])
                    add(hw0, (k + half, y, i), hwb1[k, i])
                return carry

            lax.fori_loop(0, half, one, 0)
            for i in range(2):
                add(tr0, (i, x, slice(None), part_a), tra1[i])
                add(tr0, (y, i, slice(None), part_b), trb1[i])

        def after2():
            for copy in stages[2]:
                copy.wait()

            def one(k, carry):
                hw_out[k] = hw0[k, y, x].astype(f32) + hwa2[k].astype(f32)
                hw_out[k + half] = hw0[k + half, y, x].astype(f32) + hwb2[k].astype(f32)
                return carry

            lax.fori_loop(0, half, one, 0)
            tr_out[:, part_a] = tr0[y, x, :, part_a].astype(f32) + tra2[...].astype(f32)
            tr_out[:, part_b] = tr0[y, x, :, part_b].astype(f32) + trb2[...].astype(f32)

        for copy in keep + stages[0]:
            copy.start()

    dw_ref[...] = jnp.zeros_like(dw_ref)
    table_ref[...] = jnp.zeros_like(table_ref)
    pad_ref[...] = jnp.zeros_like(pad_ref)
    per = rows // WORD_TILE
    group = lax.broadcasted_iota(jnp.int32, (1, WORD_TILE, LANES), 2) // 16
    vocab = lax.broadcasted_iota(jnp.int32, (table_ref.shape[0], padded * WORD_TILE), 0)

    def tile_step(index, carry):
        @pl.when(index % per == 0)
        def arrived():
            for hop in range(1, count):
                part_copy(hop, index // per).wait_recv()

        start = pl.multiple_of(index * WORD_TILE, WORD_TILE)
        tile = pl.ds(start, WORD_TILE)
        x2 = windows(y_ref, start, chars)
        conv = dot(x2, w_ref[...], 1, 0).reshape(chars, WORD_TILE, filters)
        total = log_ref[tile, :]
        pooled = total - off_ref[...]
        sig = jax.nn.sigmoid(pooled)
        grad = prev_ref[tile, :] + part_ref[
            tile, pl.ds(pl.multiple_of(me * filters, filters), filters)
        ].astype(f32)
        for hop in range(count - 1):
            grad = grad + got_ref[hop, tile, :].astype(f32)
        grad = grad * (sig * (1.0 + pooled * (1.0 - sig)))
        d_conv = (grad[None] * jnp.exp(conv - total[None])).astype(bf16)
        d_conv = d_conv.reshape(chars * WORD_TILE, filters)
        dw_ref[...] += dot(x2, d_conv, 0, 0)
        d_win = dot(d_conv, wb_ref[...], 1, 1).astype(bf16)
        pad_ref[6 : 6 + chars] = d_win.reshape(chars, WORD_TILE, LANES)
        d_emb = pad_ref[6 : 6 + padded]
        for tap in range(1, 7):
            d_emb = jnp.where(group == tap, pad_ref[6 - tap : 6 - tap + padded], d_emb)
        one_hot = jnp.where(vocab == ids_ref[pl.ds(index, 1), :], 1.0, 0.0).astype(bf16)
        table_ref[...] += dot(one_hot, d_emb.reshape(padded * WORD_TILE, LANES), 1, 0)
        return carry

    tiles = words // WORD_TILE
    if cuts:
        lax.fori_loop(0, cuts[0], tile_step, 0)
        after0()
        for copy in stages[1]:
            copy.start()
        lax.fori_loop(cuts[0], cuts[1], tile_step, 0)
        after1()
        for copy in stages[2]:
            copy.start()
        lax.fori_loop(cuts[1], tiles, tile_step, 0)
        after2()
    else:
        lax.fori_loop(0, tiles, tile_step, 0)

    def part_drain(chunk, carry):
        for hop in range(1, count):
            part_copy(hop, chunk).wait_send()
        return carry

    lax.fori_loop(0, chunks, part_drain, 0)


def conv_backward(ids, y, w, wb, off, logs, prev, part, hw, tr, count, chars, cid):
    words, filters = logs.shape
    chunks = 8
    out_shape = [
        jax.ShapeDtypeStruct((LANES, filters), f32),
        jax.ShapeDtypeStruct((264, LANES), f32),
    ]
    scratch = [
        pltpu.VMEM((68, WORD_TILE, LANES), bf16),
        pltpu.VMEM((count - 1, words, filters), bf16),
        DMA((count - 1, chunks)),
        DMA((count - 1, chunks)),
    ]
    operands = [ids, y, w, wb, off, logs, prev, part]
    in_specs = [VMEM] * 8
    cuts = None
    if hw is not None:
        cuts = (10, 24)
        mats, rows, cols = hw.shape[0], hw.shape[-2], hw.shape[-1]
        tr_rows, tr_cols = tr.shape[-2], tr.shape[-1]
        lane_a = 1536
        lane_b = tr_cols - lane_a
        out_shape += [
            jax.ShapeDtypeStruct((mats, rows, cols), f32),
            jax.ShapeDtypeStruct((tr_rows, tr_cols), f32),
        ]
        operands += [hw, tr]
        in_specs += [ANY, ANY]
        half = mats // 2
        scratch += [pltpu.VMEM((mats, 2, 2, rows, cols), bf16)] * 2
        scratch += [pltpu.VMEM((2, 2, tr_rows, tr_cols), bf16)] * 2
        scratch += [pltpu.VMEM((half, 2, rows, cols), bf16)] * 2
        scratch += [pltpu.VMEM((2, tr_rows, lane), bf16) for lane in (lane_a, lane_b)]
        scratch += [pltpu.VMEM((half, rows, cols), bf16)] * 2
        scratch += [pltpu.VMEM((tr_rows, lane), bf16) for lane in (lane_a, lane_b)]
        scratch += [DMA((2,)), DMA((10,)), DMA((10,))]
    return pl.pallas_call(
        functools.partial(conv_backward_kernel, count, chars, chunks, cuts),
        out_shape=tuple(out_shape),
        in_specs=in_specs,
        out_specs=tuple([VMEM] * len(out_shape)),
        scratch_shapes=scratch,
        compiler_params=params(cid, 56),
        name="conv_backward",
    )(*operands)


def small_kernel(dp_count, count, in_ref, out_ref, got, mid, *sems):
    s1, r1, s2, r2, s3, r3 = sems
    me = lax.axis_index("tensor")
    place = lax.axis_index("dp")
    barrier = pltpu.get_barrier_semaphore()

    def dp_peer(hop):
        return lax.rem(place + hop, dp_count)

    def greet(hop, carry):
        pl.semaphore_signal(barrier, inc=1, device_id={"dp": dp_peer(hop)}, device_id_type=MESH)
        return carry

    lax.fori_loop(1, dp_count, greet, 0)
    for hop in range(1, count):
        pl.semaphore_signal(
            barrier, inc=1, device_id={"tensor": lax.rem(me + hop, count)}, device_id_type=MESH
        )
    pl.semaphore_wait(barrier, dp_count + count - 2)

    def scatter(hop):
        return pltpu.make_async_remote_copy(
            src_ref=in_ref.at[dp_peer(hop)], dst_ref=got.at[hop - 1], send_sem=s1.at[hop - 1],
            recv_sem=r1.at[hop - 1], device_id={"dp": dp_peer(hop)}, device_id_type=MESH,
        )

    def across(hop):
        return pltpu.make_async_remote_copy(
            src_ref=mid.at[me], dst_ref=mid.at[me], send_sem=s2.at[hop - 1], recv_sem=r2.at[hop - 1],
            device_id={"tensor": lax.rem(me + hop, count)}, device_id_type=MESH,
        )

    def around(hop):
        return pltpu.make_async_remote_copy(
            src_ref=mid, dst_ref=out_ref.at[place], send_sem=s3.at[hop - 1], recv_sem=r3.at[hop - 1],
            device_id={"dp": dp_peer(hop)}, device_id_type=MESH,
        )

    def loop(fn, stop):
        def one(hop, carry):
            fn(hop)
            return carry

        lax.fori_loop(1, stop, one, 0)

    loop(lambda hop: scatter(hop).start(), dp_count)
    loop(lambda hop: scatter(hop).wait(), dp_count)
    total = lax.fori_loop(
        0, dp_count - 1, lambda k, acc: acc + got[k], in_ref[place]
    )
    mid[me] = total.astype(bf16)
    for hop in range(1, count):
        across(hop).start()
    for hop in range(1, count):
        across(hop).wait()
    loop(lambda hop: around(hop).start(), dp_count)
    out_ref[place] = mid[...]
    loop(lambda hop: around(hop).wait(), dp_count)


def sum_small(packed, dp_count, count, cid):
    shape = packed.shape[1:]
    return pl.pallas_call(
        functools.partial(small_kernel, dp_count, count),
        out_shape=jax.ShapeDtypeStruct((dp_count, count) + shape, bf16),
        in_specs=[VMEM],
        out_specs=VMEM,
        scratch_shapes=[
            pltpu.VMEM((dp_count - 1,) + shape, f32),
            pltpu.VMEM((count,) + shape, bf16),
            DMA((dp_count - 1,)),
            DMA((dp_count - 1,)),
            DMA((count - 1,)),
            DMA((count - 1,)),
            DMA((dp_count - 1,)),
            DMA((dp_count - 1,)),
        ],
        compiler_params=params(cid, 32),
        name="sum_small",
    )(packed)


def layer_norm(values, gain, shift):
    centered = values - jnp.mean(values, axis=-1, keepdims=True)
    variance = jnp.mean(centered * centered, axis=-1, keepdims=True)
    return centered * lax.rsqrt(variance + norm_eps) * gain + shift


def norm_back(values, gain, shift, cotangent):
    unused, pull_back = jax.vjp(layer_norm, values, gain, shift)
    return pull_back(cotangent)


def gelu_exact(values):
    return jax.nn.gelu(values, approximate=False)


def highway_mix(pre_acts, previous):
    gate = jax.nn.sigmoid(pre_acts[:, 1])
    return gate * jax.nn.silu(pre_acts[:, 0]) + (1.0 - gate) * previous


def mm(spec, *operands):
    return jnp.einsum(spec, *operands, preferred_element_type=f32)


def body(
    char_ids,
    seq_lengths,
    char_table,
    conv_weight,
    conv_bias,
    highway_weight,
    highway_bias,
    proj_weight,
    proj_bias,
    norm_gain,
    norm_shift,
    qkv_weight,
    qv_bias,
    output_projection_weight,
    out_bias,
    up_weight,
    up_bias,
    down_weight,
    down_bias,
    out_grad,
):
    words, nseq, chars = char_ids.shape
    assert nseq == 1
    count = lax.axis_size("tensor")
    dp_count = lax.axis_size("dp")
    rank = lax.axis_index("tensor")
    vocab, char_dim = char_table.shape
    taps_dim, filters = conv_weight.shape
    features = proj_weight.shape[1]
    heads = qkv_weight.shape[2] // HEAD_DIM
    gains = norm_gain.astype(f32)
    shifts = norm_shift.astype(f32)

    d_out = lax.all_gather(out_grad[:, 0], "tensor", axis=0, tiled=True).astype(f32)

    padded = chars + 6
    ids = jnp.pad(char_ids[:, 0], ((0, 0), (0, 6)), constant_values=-1)
    ids_tiles = jnp.swapaxes(ids.reshape(words // WORD_TILE, WORD_TILE, padded), 1, 2)
    ids_tiles = ids_tiles.reshape(words // WORD_TILE, padded * WORD_TILE)
    table_wide = jnp.pad(jnp.tile(char_table, (1, 7)), ((0, 0), (0, LANES - taps_dim)))
    one_hot = (ids.T[:, :, None] == lax.broadcasted_iota(jnp.int32, (1, 1, vocab), 2)).astype(bf16)
    pattern = np.zeros((padded, LANES), np.float32)
    pattern[:, taps_dim] = 1.0
    for k in range(1, 7):
        pattern[chars - k, taps_dim + k] = 1.0
    y = (mm("qwv,vl->qwl", one_hot, table_wide) + pattern[:, None, :]).astype(bf16)

    widths = filter_widths(filters)
    off = jnp.asarray(np.log((chars - widths + 1).astype(np.float64)).astype(np.float32))[None]
    tap_of = np.arange(taps_dim)[:, None] // char_dim
    w_taps = jnp.where(tap_of < widths[None], conv_weight, 0).astype(bf16)
    ends = np.where(widths[None] > np.arange(1, 7)[:, None], big_neg, 0.0).astype(np.float32)
    tail = LANES - taps_dim - 7
    w_all = jnp.concatenate(
        [w_taps, conv_bias[None], jnp.asarray(ends, bf16), jnp.zeros((tail, filters), bf16)], axis=0
    )
    w_back = jnp.concatenate([w_taps, jnp.zeros((LANES - taps_dim, filters), bf16)], axis=0)

    logs, whole = conv_forward(y, w_all, off, count, chars, 1)
    hidden = jax.nn.silu(logs - off)
    kept_layers = []
    for layer in range(highway_weight.shape[0]):
        if layer > 0:
            whole = gather_features(hidden.astype(bf16), count, 1 + layer)
        pre_acts = mm("rk,jkf->rjf", whole, highway_weight[layer]) + highway_bias[layer].astype(f32)
        kept_layers.append((hidden, whole, pre_acts))
        hidden = highway_mix(pre_acts, hidden)
    top_sent = hidden.astype(bf16)
    embedded = sum_rows(mm("sk,kd->sd", top_sent, proj_weight).astype(bf16), count, 4)
    embedded = embedded + proj_bias.astype(f32)
    inputs = layer_norm(embedded, gains[0], shifts[0])
    sent = inputs.astype(bf16)
    projected = mm("sd,dkh->skh", sent, qkv_weight)
    queries = (projected[:, 0] + qv_bias[0].astype(f32)).astype(bf16).reshape(words, heads, HEAD_DIM)
    key_rows = projected[:, 1].astype(bf16).reshape(words, heads, HEAD_DIM)
    values = (projected[:, 2] + qv_bias[1].astype(f32)).astype(bf16).reshape(words, heads, HEAD_DIM)
    scale = HEAD_DIM ** (-0.5)
    scores = mm("qhd,khd->hqk", queries, key_rows) * scale
    live = lax.broadcasted_iota(jnp.int32, scores.shape, 2) < seq_lengths[0]
    scores = jnp.where(live, scores, big_neg)
    probs = jax.nn.softmax(scores, axis=2)
    attended = mm("hqk,khd->qhd", probs.astype(bf16), values).astype(bf16).reshape(words, -1)
    branch = sum_rows(mm("sh,hd->sd", attended, output_projection_weight).astype(bf16), count, 5)
    middle_pre = inputs + branch + out_bias.astype(f32)
    middle = layer_norm(middle_pre, gains[1], shifts[1])
    sent_mid = middle.astype(bf16)
    upper = mm("sd,df->sf", sent_mid, up_weight) + up_bias.astype(f32)
    activated = gelu_exact(upper).astype(bf16)
    branch_two = sum_rows(mm("sf,fd->sd", activated, down_weight).astype(bf16), count, 6)
    final_pre = middle + branch_two + down_bias.astype(f32)
    own_rows = words // count
    final_own = lax.dynamic_slice_in_dim(final_pre, rank * own_rows, own_rows, 0)
    encoded = layer_norm(final_own, gains[2], shifts[2]).astype(bf16)[:, None]

    d_pre2, d_gain2, d_shift2 = norm_back(final_pre, gains[2], shifts[2], d_out)
    d_branch_two = d_pre2.astype(bf16)
    down_bias_grad = jnp.sum(d_branch_two.astype(f32), axis=0)
    d_down_t = mm("sd,sf->df", d_branch_two, activated)
    d_activated = mm("sd,fd->sf", d_branch_two, down_weight)
    unused, gelu_pull = jax.vjp(gelu_exact, upper)
    d_upper = gelu_pull(d_activated)[0].astype(bf16)
    up_bias_part = jnp.sum(d_upper.astype(f32), axis=0)
    d_up = mm("sd,sf->df", sent_mid, d_upper)
    d_middle = d_pre2 + sum_rows(mm("sf,df->sd", d_upper, up_weight).astype(bf16), count, 7)
    d_pre1, d_gain1, d_shift1 = norm_back(middle_pre, gains[1], shifts[1], d_middle)
    d_branch = d_pre1.astype(bf16)
    out_bias_grad = jnp.sum(d_branch.astype(f32), axis=0)
    d_out_t = mm("sd,sh->dh", d_branch, attended)
    d_heads = mm("sd,hd->sh", d_branch, output_projection_weight).astype(bf16)
    d_heads = d_heads.reshape(words, heads, HEAD_DIM)
    d_values = mm("hqk,qhd->khd", probs.astype(bf16), d_heads).astype(bf16)
    d_probs = mm("qhd,khd->hqk", d_heads, values)
    d_scores = (probs * (d_probs - jnp.sum(d_probs * probs, axis=2, keepdims=True))).astype(bf16)
    d_queries = (mm("hqk,khd->qhd", d_scores, key_rows) * scale).astype(bf16)
    d_keys = (mm("hqk,qhd->khd", d_scores, queries) * scale).astype(bf16)
    d_proj = jnp.concatenate(
        [part.reshape(words, -1) for part in (d_queries, d_keys, d_values)], axis=1
    )
    proj_sums = jnp.sum(d_proj.astype(f32), axis=0).reshape(3, -1)
    qv_part = jnp.stack([proj_sums[0], proj_sums[2]], axis=0)
    d_qkv = mm("sd,sh->dh", sent, d_proj)
    d_inputs = d_pre1 + sum_rows(
        mm("sh,dh->sd", d_proj, qkv_weight.reshape(features, -1)).astype(bf16), count, 8
    )
    d_embedded, d_gain0, d_shift0 = norm_back(embedded, gains[0], shifts[0], d_inputs)
    grads_emb = d_embedded.astype(bf16)
    proj_bias_grad = jnp.sum(grads_emb.astype(f32), axis=0)
    d_proj_t = mm("sd,sk->dk", grads_emb, top_sent)
    d_hidden = mm("sd,kd->sk", grads_emb, proj_weight)

    hw_parts = []
    hw_bias_parts = []
    for layer in reversed(range(len(kept_layers))):
        previous, whole, pre_acts = kept_layers[layer]
        unused, mix_pull = jax.vjp(highway_mix, pre_acts, previous)
        d_pre, d_previous = mix_pull(d_hidden)
        d_pre = d_pre.astype(bf16)
        hw_parts.insert(0, mm("rk,rjf->jkf", whole, d_pre).astype(bf16))
        hw_bias_parts.insert(0, jnp.sum(d_pre.astype(f32), axis=0))
        partial_sum = mm("rjf,jkf->rk", d_pre, highway_weight[layer]).astype(bf16)
        if layer > 0:
            d_hidden = d_previous + scatter_features(partial_sum, count, 8 + layer)
    hw_bias_part = jnp.concatenate(hw_bias_parts, axis=0)

    mats = 2 * len(kept_layers)
    hw_all = jnp.concatenate(hw_parts, axis=0)
    tr_all = jnp.concatenate(
        [
            d_up.astype(bf16),
            d_down_t.astype(bf16),
            d_proj_t.astype(bf16),
            d_qkv.astype(bf16),
            jnp.zeros((features, 64), bf16),
            d_out_t.astype(bf16),
            jnp.zeros((features, 64), bf16),
        ],
        axis=1,
    )
    small = (ids_tiles, y, w_all, w_back, off, logs, d_previous, partial_sum)
    if dp_count == 8 and (features // dp_count) % 16 == 0:
        d_w_all, table_all, hw_sum, tr_sum = conv_backward(
            *small,
            hw_all.reshape(mats, 2, 2, 2, -1, filters),
            tr_all.reshape(2, 2, 2, features // dp_count, -1),
            count,
            chars,
            10,
        )
    else:
        d_w_all, table_all = conv_backward(*small, None, None, count, chars, 10)
        hw_sum = lax.psum_scatter(hw_all, "dp", scatter_dimension=1, tiled=True).astype(f32)
        tr_sum = lax.psum_scatter(tr_all, "dp", scatter_dimension=0, tiled=True).astype(f32)
    hw_w_grad = hw_sum.reshape(len(kept_layers), 2, -1, filters)
    up_w_grad = tr_sum[:, :768]
    down_w_grad = tr_sum[:, 768:1536].T
    proj_w_grad = tr_sum[:, 1536:2048].T
    qkv_w_grad = tr_sum[:, 2048:2624].reshape(-1, 3, heads * HEAD_DIM)
    out_w_grad = tr_sum[:, 2688:2880].T

    table_part = jnp.sum(
        table_all[:vocab, :taps_dim].reshape(vocab, taps_dim // char_dim, char_dim), axis=1
    )
    pieces = [
        d_w_all[: taps_dim + 1],
        hw_bias_part,
        qv_part,
        up_bias_part,
        table_part,
        proj_bias_grad,
        jnp.stack([d_gain0, d_gain1, d_gain2]),
        jnp.stack([d_shift0, d_shift1, d_shift2]),
        out_bias_grad,
        down_bias_grad,
    ]
    sizes = [piece.size for piece in pieces]
    flat = jnp.concatenate([piece.reshape(-1) for piece in pieces])
    width = -(-flat.size // (dp_count * 16 * LANES)) * LANES
    flat = jnp.pad(flat, (0, dp_count * 16 * width - flat.size))
    summed = sum_small(flat.reshape(dp_count, 16, width), dp_count, count, 11)
    summed = jnp.swapaxes(summed, 0, 1).reshape(count, -1).astype(f32)
    ends_at = np.cumsum(sizes)

    def piece(index):
        return summed[:, ends_at[index] - sizes[index] : ends_at[index]]

    conv_all = jnp.swapaxes(piece(0).reshape(count, taps_dim + 1, filters), 0, 1).reshape(
        taps_dim + 1, -1
    )
    conv_w_grad = jnp.where(
        tap_of < np.tile(widths, count)[None], conv_all[:taps_dim], 0.0
    )
    conv_b_grad = conv_all[taps_dim]
    hw_b_grad = jnp.swapaxes(piece(1).reshape(count, mats, filters), 0, 1).reshape(
        len(kept_layers), 2, -1
    )
    qv_grad = jnp.swapaxes(piece(2).reshape(count, 2, -1), 0, 1).reshape(2, -1)
    up_b_grad = piece(3).reshape(-1)
    table_grad = jnp.sum(piece(4), axis=0).reshape(vocab, char_dim)
    proj_b_grad = piece(5)[0]
    gain_grad = piece(6)[0].reshape(3, features)
    shift_grad = piece(7)[0].reshape(3, features)
    out_b_grad = piece(8)[0]
    down_b_grad = piece(9)[0]
    return (
        encoded,
        table_grad,
        conv_w_grad,
        conv_b_grad,
        hw_w_grad,
        hw_b_grad,
        proj_w_grad,
        proj_b_grad,
        gain_grad,
        shift_grad,
        qkv_w_grad,
        qv_grad,
        out_w_grad,
        out_b_grad,
        up_w_grad,
        up_b_grad,
        down_w_grad,
        down_b_grad,
    )


def solution(mesh):
    return jax.shard_map(
        body,
        mesh=mesh,
        in_specs=(
            P(None, "dp", None),
            P("dp"),
            P(),
            P(None, "tensor"),
            P("tensor"),
            P(None, None, None, "tensor"),
            P(None, None, "tensor"),
            P("tensor", None),
            P(),
            P(),
            P(),
            P(None, None, "tensor"),
            P(None, "tensor"),
            P("tensor", None),
            P(),
            P(None, "tensor"),
            P("tensor"),
            P("tensor", None),
            P(),
            P("tensor", "dp", None),
        ),
        out_specs=(
            P("tensor", "dp", None),
            P(),
            P(),
            P(),
            P(None, None, "dp", "tensor"),
            P(),
            P("tensor", "dp"),
            P(),
            P(),
            P(),
            P("dp", None, "tensor"),
            P(),
            P("tensor", "dp"),
            P(),
            P("dp", "tensor"),
            P(),
            P("tensor", "dp"),
            P(),
        ),
        check_vma=False,
    )
```

time: 1230 us -> 616 us (0.50)
  waiting for transfers between devices: 742 us -> 0 us
  Pallas kernels: 0 us -> 435 us
  matrix products: 149 us -> 69.2 us
  other arithmetic: 97.5 us -> 29.7 us
  blocking collectives: 78.2 us -> 14.1 us
  local copies, waits for them, and re-layouts: 112 us -> 57.5 us
  loops' own time: 23.3 us -> 0 us
  between operations: 16 us -> 3.21 us
    pallas_call x0 -> x10, Pallas kernels: none -> 435 us  [the longest x5 143 us: sum_rows(): pl.pallas_call(functools.partial(sum_kernel, count, chunks), out_shape=ja...]
    reduce_scatter x12 -> x0, waiting for transfers between devices: 379 us -> none  [the longest x3 107 us: project_rows(): lax.psum_scatter(jnp.einsum('snk,kd->snd', hidden, weight, preferred_elem...]
    psum x2 -> x0, waiting for transfers between devices: 270 us -> none  [body(): lax.psum((table_part, place_piece(conv_w_part, 1, tensor_rank, tensor_cou...]
    all_gather x2 -> x0, waiting for transfers between devices: 92.1 us -> none  [gather_features(): return lax.all_gather(local_cols, 'tensor', axis=1, tiled=True)]
    dot_general x87 -> x26, matrix products: 145 us -> 64.4 us  [mm(): return jnp.einsum(spec, *operands, preferred_element_type=f32)]
    all_gather x5 -> x1, blocking collectives: 78.2 us -> 14.1 us  [body(): lax.all_gather(out_grad[:, 0], 'tensor', axis=0, tiled=True).astype(f32)]
    reduce_sum x48 -> x7, other arithmetic: 59.5 us -> 4.9 us  [the longest x1 2.69 us: body(): proj_bias_grad = jnp.sum(grads_emb.astype(f32), axis=0)]
    while x216 -> x0, local copies, waits for them, and re-layouts: 38.5 us -> none
  transfers between devices with their start and end apart: 17 -> 0, of which waited for: 15 -> 0; matrix products, arithmetic and copies ran while one was open for 15% -> 0% of each run, Pallas kernels for 0% -> 0%
where the time goes in v1:
time: 616 us; the launch traced here: 608 us
  Pallas kernels  435 us (71%)
  matrix products  69.2 us (11%)
  local copies, waits for them, and re-layouts  57.5 us (9%)
  other arithmetic  29.7 us (5%)
  blocking collectives  14.1 us (2%)
    pallas_call x5, Pallas kernels, sum_rows(): pl.pallas_call(functools.partial(sum_kernel, count, chunks), out_shape=ja...  143 us
    pallas_call x1, Pallas kernels, conv_backward(): pl.pallas_call(functools.partial(conv_backward_kernel, count, chars, chun...  132 us
    dot_general x26, matrix products, mm(): return jnp.einsum(spec, *operands, preferred_element_type=f32)  64.4 us
    pallas_call x1, Pallas kernels, scatter_features(): pl.pallas_call(functools.partial(scatter_kernel, count, chunks), out_shap...  53.5 us
    pallas_call x1, Pallas kernels, conv_forward(): pl.pallas_call(functools.partial(conv_forward_kernel, count, chars, chunk...  42.4 us
    pallas_call x1, Pallas kernels, gather_features(): pl.pallas_call(functools.partial(gather_kernel, count, chunks), out_shape...  34.4 us
    pallas_call x1, Pallas kernels, sum_small(): pl.pallas_call(functools.partial(small_kernel, dp_count, count), out_shap...  29.2 us
    unnamed x166, local copies, waits for them, and re-layouts  16.8 us

profile of v1, /device:TPU:1, one launch (start us, length us, event | category | flops | bytes accessed | tf_op | source)
XLA Modules:
  0.0 608.2 jit_solution(5478825350605972231)
XLA Ops:
  0.7 1.1 copy.99
  2.9 11.9 %add_convert_fusion.y_ref = bf16[56,512,128]{2,1,0:T(8,128)(2,1)S(1)} fusion(s32[56,512]{1,0:T(8,128)S(1)} %copy.100, f32[56,128]{1,0:T(8,128)S(1)} %copy-done.72, bf16[262,112]{1,0:T(8,128)(2,1)S(1)} %copy.101), kind=kOutput, calls=%fused_computation.4 | convolution fusion | flops 1937940480 | bytes 7542080 | tf_op jit(solution)/shard_map/qwv,vl->qwl/dot_general | solution.py:724
  15.8 42.4 %conv_forward.1 = (f32[512,512]{1,0:T(8,128)S(1)}, bf16[512,2048]{1,0:T(8,128)(2,1)S(1)}) custom-call(bf16[56,512,128]{2,1,0:T(8,128)(2,1)S(1)} %add_convert_fusion.y_ref, bf16[128,512]{1,0:T(8,128)(2,1)S(1)} %get-tuple-element.159.w_ref, f32[1,512]{1,0:T(1,128)S(1)} %copy-done.8), custom_call_target="tpu_custom_call" | custom-call | tf_op jit(solution)/shard_map/conv_forward/pallas_call | solution.py:165
  58.3 5.7 fusion.41
  65.3 34.4 %gather_features.1 = bf16[512,2048]{1,0:T(8,128)(2,1)S(1)} custom-call(bf16[512,512]{1,0:T(8,128)(2,1)S(1)} %get-tuple-element.146.x_ref), custom_call_target="tpu_custom_call" | custom-call | tf_op jit(solution)/shard_map/gather_features/pallas_call | solution.py:202
  99.7 2.3 fusion.46
  104.4 29.6 %sum_rows.5 = f32[512,768]{1,0:T(8,128)S(1)} custom-call(bf16[512,768]{1,0:T(8,128)(2,1)S(1)} %convolution_convert_fusion.8.p_ref), custom_call_target="tpu_custom_call" | custom-call | tf_op jit(solution)/shard_map/sum_rows/pallas_call | solution.py:284
  138.6 3.9 fusion.116
  142.6 2.5 convolution_convert_fusion.11
  145.6 27.9 %sum_rows.6 = f32[512,768]{1,0:T(8,128)S(1)} custom-call(bf16[512,768]{1,0:T(8,128)(2,1)S(1)} %convolution_convert_fusion.7.p_ref), custom_call_target="tpu_custom_call" | custom-call | tf_op jit(solution)/shard_map/sum_rows/pallas_call | solution.py:284
  174.9 4.1 multiply_convert_fusion.1
  179.9 27.9 %sum_rows.7 = f32[512,768]{1,0:T(8,128)S(1)} custom-call(bf16[512,768]{1,0:T(8,128)(2,1)S(1)} %convolution_convert_fusion.4.p_ref), custom_call_target="tpu_custom_call" | custom-call | tf_op jit(solution)/shard_map/sum_rows/pallas_call | solution.py:284
  209.6 14.1 %all-gather = bf16[512,1,768]{2,0,1:T(8,128)(2,1)S(1)} all-gather(bf16[128,1,768]{2,0,1:T(8,128)(2,1)S(1)} %copy-done.46), channel_id=2, replica_groups=mesh['dp'=8,'tensor'=4] {'tensor'}, dimensions={0}, use_global_device_ids=true | all-gather | bytes 983040 | tf_op jit(solution)/shard_map/all_gather | solution.py:761
  226.0 1.8 convert_reduce_fusion.6
  229.5 30.1 %sum_rows.8 = f32[512,768]{1,0:T(8,128)S(1)} custom-call(bf16[512,768]{1,0:T(8,128)(2,1)S(1)} %convolution_convert_fusion.3.p_ref), custom_call_target="tpu_custom_call" | custom-call | tf_op jit(solution)/shard_map/sum_rows/pallas_call | solution.py:284
  259.6 1.4 multiply_reduce_fusion.1
  268.3 27.4 %sum_rows.9 = f32[512,768]{1,0:T(8,128)S(1)} custom-call(bf16[512,768]{1,0:T(8,128)(2,1)S(1)} %convolution_convert_fusion.6.p_ref), custom_call_target="tpu_custom_call" | custom-call | tf_op jit(solution)/shard_map/sum_rows/pallas_call | solution.py:284
  295.7 1.3 fusion.103
  299.1 2.7 convert_reduce_fusion.5
  302.4 1.0 copy-done.19
  303.4 1.0 fusion.68
  304.4 5.3 bitcast_convert_fusion.1.p_ref
  309.7 53.5 %scatter_features.1 = f32[512,512]{1,0:T(8,128)S(1)} custom-call(bf16[512,2048]{1,0:T(8,128)(2,1)S(1)} %bitcast_convert_fusion.1.p_ref), custom_call_target="tpu_custom_call" | custom-call | tf_op jit(solution)/shard_map/scatter_features/pallas_call | solution.py:375
  363.3 0.9 fusion.71
  364.5 1.8 fusion.60
  368.3 2.0 fusion.40
  370.3 1.9 fusion.39
  372.2 1.5 fusion.52
  373.7 1.7 fusion.51
  376.1 1.0 fusion.55
  377.8 6.8 %copy.110 = bf16[768,2944]{1,0:T(8,128)(2,1)} copy(bf16[768,2944]{0,1:T(8,128)(2,1)} %broadcast_dynamic-update-slice_fusion.1) | data formatting | bytes 9043968 | tf_op jit(solution)/shard_map/concatenate | solution.py:874
  384.6 5.7 convert_bitcast_fusion.1
  390.3 4.4 convert_bitcast_fusion
  394.6 7.4 %pad_maximum_fusion = bf16[4,2048,512]{1,2,0:T(8,128)(2,1)} fusion(bf16[2,2048,512]{1,2,0:T(8,128)(2,1)} %convert_bitcast_fusion, bf16[2,2048,512]{1,2,0:T(8,128)(2,1)} %convert_bitcast_fusion.1), kind=kLoop, calls=%fused_computation.5 | loop fusion | flops 4194304 | bytes 16777216 | tf_op jit(solution)/shard_map/concatenate | solution.py:873
  402.0 11.7 %copy.109 = bf16[4,2048,512]{2,1,0:T(8,128)(2,1)} copy(bf16[4,2048,512]{1,2,0:T(8,128)(2,1)} %pad_maximum_fusion) | data formatting | bytes 16777216 | tf_op jit(solution)/shard_map/concatenate | solution.py:873
  413.8 5.9 bitcast_convert_fusion.part_ref
  420.7 132.1 %conv_backward.1 = (f32[128,512]{1,0:T(8,128)}, f32[264,128]{1,0:T(8,128)}, f32[4,256,512]{2,1,0:T(8,128)}, f32[96,2944]{1,0:T(8,128)}) custom-call(s32[32,896]{1,0:T(8,128)} %copy.111.ids_ref, bf16[56,512,128]{2,1,0:T(8,128)(2,1)} %copy-done.2, bf16[128,512]{1,0:T(8,128)(2,1)} %copy-done.7, bf16[128,512]{1,0:T(8,128)(2,1)} %get-tuple-element.158.wb_ref, ...), custom_call_target="tpu_custom_call" | custom-call | tf_op jit(solution)/shard_map/conv_backward/pallas_call | solution.py:610
  552.9 1.0 slice.169
  554.0 1.0 copy.112
  555.6 1.9 concatenate.27
  557.6 29.2 %sum_small.1 = bf16[8,4,16,640]{3,2,1,0:T(8,128)(2,1)S(1)} custom-call(f32[8,16,640]{2,1,0:T(8,128)S(1)} %reshape.308.in_ref), custom_call_target="tpu_custom_call" | custom-call | tf_op jit(solution)/shard_map/sum_small/pallas_call | solution.py:683
  588.6 1.1 fusion.82
  589.7 1.0 copy.128
  596.3 1.0 slice.185
  598.3 1.9 slice_bitcast_fusion.2
  600.2 0.9 slice_bitcast_fusion.4
  601.8 1.6 slice_bitcast_fusion.3
  604.6 3.1 copy.139
  (280 shorter events, 43.2 us)
Async XLA Ops:
  0.7 174.3 %copy-start = (bf16[768,768]{1,0:T(8,128)(2,1)S(1)}, bf16[768,768]{1,0:T(8,128)(2,1)}, u32[]{:S(2)}) copy-start(bf16[768,768]{1,0:T(8,128)(2,1)} %param.40) | copy-start | bytes 3538948
  2.8 12.0 %copy-start.47 = (bf16[112,512]{1,0:T(8,128)(2,1)S(1)}, bf16[112,512]{1,0:T(8,128)(2,1)}, u32[]{:S(2)}) copy-start(bf16[112,512]{1,0:T(8,128)(2,1)} %param.28) | copy-start | bytes 344068
  2.8 12.0 %copy-start.48 = (pred[112,512]{1,0:T(8,128)(4,1)S(1)}, pred[112,512]{1,0:T(8,128)(4,1)}, u32[]{:S(2)}) copy-start(pred[112,512]{1,0:T(8,128)(4,1)} %constant.131.clone) | copy-start | bytes 172036
  2.9 12.0 %copy-start.68 = (bf16[512]{0:T(512)(128)(2,1)S(1)}, bf16[512]{0:T(512)(128)(2,1)}, u32[]{:S(2)}) copy-start(bf16[512]{0:T(512)(128)(2,1)} %param.29) | copy-start | bytes 3076
  2.9 12.1 %copy-start.58 = (bf16[6,512]{1,0:T(8,128)(2,1)S(1)}, bf16[6,512]{1,0:T(8,128)(2,1)}, u32[]{:S(2)}) copy-start(bf16[6,512]{1,0:T(8,128)(2,1)} %constant.132.clone) | copy-start | bytes 18436
  2.9 12.9 %copy-start.8 = (f32[1,512]{1,0:T(1,128)S(1)}, f32[1,512]{1,0:T(1,128)}, u32[]{:S(2)}) copy-start(f32[1,512]{1,0:T(1,128)} %constant.154.off_ref) | copy-start | bytes 6148
  14.8 43.4 %copy-start.2 = (bf16[56,512,128]{2,1,0:T(8,128)(2,1)}, bf16[56,512,128]{2,1,0:T(8,128)(2,1)S(1)}, u32[]{:S(2)}) copy-start(bf16[56,512,128]{2,1,0:T(8,128)(2,1)S(1)} %add_convert_fusion.y_ref) | copy-start | bytes 22020100
  15.8 42.4 %copy-start.7 = (bf16[128,512]{1,0:T(8,128)(2,1)}, bf16[128,512]{1,0:T(8,128)(2,1)S(1)}, u32[]{:S(2)}) copy-start(bf16[128,512]{1,0:T(8,128)(2,1)S(1)} %get-tuple-element.159.w_ref) | copy-start | bytes 393220
  15.8 42.4 %copy-start.62 = (bf16[2,2,512]{2,1,0:T(2,128)(2,1)S(1)}, bf16[2,2,512]{2,1,0:T(2,128)(2,1)}, u32[]{:S(2)}) copy-start(bf16[2,2,512]{2,1,0:T(2,128)(2,1)} %param.31) | copy-start | bytes 12292
  15.8 83.9 %slice-start = ((s8[8388608]{0:T(1024)(128)(4,1)}), s8[4194304]{0:T(1024)(128)(4,1)S(1)}, s32[]{:S(2)}) async-start(s8[8388608]{0:T(1024)(128)(4,1)} %bitcast.256), calls=%async_computation | async-start | bytes 8388608
  58.2 5.7 copy-start.9
  58.2 5.8 copy-start.3
  58.3 5.7 copy-start.56
  58.3 41.4 %slice-start.1 = ((s8[8388608]{0:T(1024)(128)(4,1)}), s8[4194304]{0:T(1024)(128)(4,1)S(1)}, s32[]{:S(2)}) async-start(s8[8388608]{0:T(1024)(128)(4,1)} %bitcast.256), calls=%async_computation.1 | async-start | bytes 8388608
  65.3 36.8 %copy-start.22 = (f32[512,512]{1,0:T(8,128)}, f32[512,512]{1,0:T(8,128)S(1)}, u32[]{:S(2)}) copy-start(f32[512,512]{1,0:T(8,128)S(1)} %get-tuple-element.147) | copy-start | bytes 3145732
  103.8 30.2 %copy-start.43 = (bf16[512,512]{1,0:T(8,128)(2,1)}, bf16[512,512]{1,0:T(8,128)(2,1)S(1)}, u32[]{:S(2)}) copy-start(bf16[512,512]{1,0:T(8,128)(2,1)S(1)} %fusion.62) | copy-start | bytes 1572868
  104.4 29.7 %copy-start.64 = (bf16[768]{0:T(1024)(128)(2,1)S(1)}, bf16[768]{0:T(1024)(128)(2,1)}, u32[]{:S(2)}) copy-start(bf16[768]{0:T(1024)(128)(2,1)} %param.33) | copy-start | bytes 4612
  142.6 2.5 copy-start.33
  145.1 28.4 %copy-start.34 = (bf16[3,64,512]{2,1,0:T(8,128)(2,1)}, bf16[3,64,512]{2,1,0:T(8,128)(2,1)S(1)}, u32[]{:S(2)}) copy-start(bf16[3,64,512]{2,1,0:T(8,128)(2,1)S(1)} %convolution_convert_fusion.11) | copy-start | bytes 589828
  145.1 28.4 %copy-start.65 = (bf16[768]{0:T(1024)(128)(2,1)S(1)}, bf16[768]{0:T(1024)(128)(2,1)}, u32[]{:S(2)}) copy-start(bf16[768]{0:T(1024)(128)(2,1)} %param.39) | copy-start | bytes 4612
  174.2 86.7 %copy-start.11 = (f32[512,768]{1,0:T(8,128)}, f32[512,768]{1,0:T(8,128)S(1)}, u32[]{:S(2)}) copy-start(f32[512,768]{1,0:T(8,128)S(1)} %get-tuple-element.145) | copy-start | bytes 4718596
  174.9 4.1 copy-start.69
  179.9 27.9 %copy-start.67 = (bf16[768]{0:T(1024)(128)(2,1)S(1)}, bf16[768]{0:T(1024)(128)(2,1)}, u32[]{:S(2)}) copy-start(bf16[768]{0:T(1024)(128)(2,1)} %param.43) | copy-start | bytes 4612
  208.4 16.1 %copy-start.13 = (f32[512,768]{1,0:T(8,128)}, f32[512,768]{1,0:T(8,128)S(1)}, u32[]{:S(2)}) copy-start(f32[512,768]{1,0:T(8,128)S(1)} %get-tuple-element.141) | copy-start | bytes 4718596
  299.1 2.7 copy-start.37
  299.1 3.3 copy-start.23
  304.3 62.0 %copy-start.26 = (f32[512,1,512]{2,0,1:T(8,128)}, f32[512,1,512]{2,0,1:T(8,128)S(1)}, u32[]{:S(2)}) copy-start(f32[512,1,512]{2,0,1:T(8,128)S(1)} %get-tuple-element.150) | copy-start | bytes 3145732
  304.3 62.0 %copy-start.28 = (f32[512,1,512]{2,0,1:T(8,128)}, f32[512,1,512]{2,0,1:T(8,128)S(1)}, u32[]{:S(2)}) copy-start(f32[512,1,512]{2,0,1:T(8,128)S(1)} %get-tuple-element.151) | copy-start | bytes 3145732
  309.7 53.5 %copy-start.16 = (f32[512,2,512]{2,0,1:T(8,128)S(1)}, f32[512,2,512]{2,0,1:T(8,128)}, u32[]{:S(2)}) copy-start(f32[512,2,512]{2,0,1:T(8,128)} %copy-done.15) | copy-start | bytes 6291460
  373.7 2.4 copy-start.35
  377.8 6.8 %copy-start.10 = (bf16[512,2048]{1,0:T(8,128)(2,1)S(1)}, bf16[512,2048]{1,0:T(8,128)(2,1)}, u32[]{:S(2)}) copy-start(bf16[512,2048]{1,0:T(8,128)(2,1)} %copy-done.9) | copy-start | bytes 6291460
  377.8 6.8 %copy-start.25 = (f32[512,1,512]{2,0,1:T(8,128)S(1)}, f32[512,1,512]{2,0,1:T(8,128)}, u32[]{:S(2)}) copy-start(f32[512,1,512]{2,0,1:T(8,128)} %copy-done.24) | copy-start | bytes 3145732
  384.6 5.7 copy-start.6
  384.6 5.7 copy-start.27
  384.6 5.7 copy-start.29
  402.0 11.7 %copy-start.31 = (f32[512,1,512]{2,0,1:T(8,128)S(1)}, f32[512,1,512]{2,0,1:T(8,128)}, u32[]{:S(2)}) copy-start(f32[512,1,512]{2,0,1:T(8,128)} %copy-done.30) | copy-start | bytes 3145732
  552.8 2.4 copy-start.55
  552.8 2.4 copy-start.54
  552.9 2.4 copy-start.21
  552.9 2.6 copy-start.49
  552.9 2.6 copy-start.50
  552.9 2.6 copy-start.51
  552.9 2.6 copy-start.52
  552.9 2.6 copy-start.57
  552.9 2.6 copy-start.61
  597.3 6.2 %copy-start.14 = (f32[512,768]{1,0:T(8,128)S(1)}, f32[512,768]{1,0:T(8,128)}, u32[]{:S(2)}) copy-start(f32[512,768]{1,0:T(8,128)} %copy-done.13) | copy-start | bytes 4718596
  597.4 6.4 %copy-start.53 = (f32[768]{0:T(1024)S(1)}, f32[768]{0:T(1024)}, u32[]{:S(2)}) copy-start(f32[768]{0:T(1024)} %get-tuple-element.119) | copy-start | bytes 9220
  603.8 3.9 copy-start.1
  (31 other events, 45.3 us)

commit v2 on v1

--- a/solution.py
+++ b/solution.py
@@ -10,7 +10,7 @@
 from jax.sharding import PartitionSpec as P
 
 HEAD_DIM = 64
-WORD_TILE = 16
+WORD_TILE = 32
 LANES = 128
 
 norm_eps = 1e-06
@@ -210,7 +210,7 @@
     )(x)
 
 
-def sum_kernel(count, chunks, p_ref, out_ref, from_left, from_right, s_right, r_right, s_left, r_left):
+def sum_kernel(count, chunks, spacing, p_ref, out_ref, from_left, from_right, s_right, r_right, s_left, r_left):
     me = lax.axis_index("tensor")
     rows = p_ref.shape[0] // chunks
     line_barrier(me, count)
@@ -239,7 +239,7 @@
     def step_fn(step, carry):
         for right in (True, False):
             lag = me if right else count - 1 - me
-            chunk = step - lag
+            chunk = step - spacing * lag
             here = (chunk >= 0) & (chunk < chunks)
             chunk = jnp.clip(chunk, 0, chunks - 1)
             buf, first, passed = copies(right, chunk)
@@ -263,7 +263,7 @@
         return carry
 
     out_ref[...] = p_ref[...].astype(f32)
-    lax.fori_loop(0, chunks + count - 1, step_fn, 0)
+    lax.fori_loop(0, chunks + spacing * (count - 1), step_fn, 0)
 
     def drain(chunk, carry):
         for right in (True, False):
@@ -279,10 +279,10 @@
 
 
 def sum_rows(partial, count, cid):
-    chunks = 8
+    chunks = 16
     shape = partial.shape
     return pl.pallas_call(
-        functools.partial(sum_kernel, count, chunks),
+        functools.partial(sum_kernel, count, chunks, 3),
         out_shape=jax.ShapeDtypeStruct(shape, f32),
         in_specs=[VMEM],
         out_specs=VMEM,
@@ -292,18 +292,27 @@
     )(partial)
 
 
-def scatter_kernel(count, chunks, p_ref, out_ref, from_left, from_right, *sems):
-    me = lax.axis_index("tensor")
-    words, filters = out_ref.shape
-    rows = words // chunks
-    line_barrier(me, count)
-
-    def copies(right, block, chunk):
-        buf = from_left if right else from_right
-        send, recv = sems[:2] if right else sems[2:]
-        to = jnp.minimum(me + 1, count - 1) if right else jnp.maximum(me - 1, 0)
+class LineScatter:
+    def __init__(self, count, me, chunks, spacing, p_ref, out_ref, from_left, from_right, sems):
+        self.count, self.me, self.chunks, self.spacing = count, me, chunks, spacing
+        self.p_ref, self.out_ref = p_ref, out_ref
+        self.from_left, self.from_right, self.sems = from_left, from_right, sems
+        self.messages = chunks * (count - 1)
+        self.steps = self.messages + spacing * (count - 1)
+
+    def place(self, right, number):
+        count, me = self.count, self.me
+        lag = me if right else count - 1 - me
+        chunk = number // (count - 1)
+        far = count - 1 - number % (count - 1)
+        block = far if right else count - 1 - far
+        words, filters = self.out_ref.shape
+        rows = words // self.chunks
         tile = pl.ds(pl.multiple_of(chunk * rows, rows), rows)
         lanes = pl.ds(pl.multiple_of(block * filters, filters), filters)
+        buf = self.from_left if right else self.from_right
+        send, recv = self.sems[:2] if right else self.sems[2:]
+        to = jnp.minimum(me + 1, count - 1) if right else jnp.maximum(me - 1, 0)
         first, passed = [
             functools.partial(
                 pltpu.make_async_remote_copy,
@@ -314,23 +323,17 @@
                 device_id={"tensor": to},
                 device_id_type=MESH,
             )
-            for src in (p_ref, buf)
+            for src in (self.p_ref, buf)
         ]
-        return buf, tile, lanes, first, passed
-
-    out_ref[...] = p_ref[:, pl.ds(pl.multiple_of(me * filters, filters), filters)].astype(f32)
-    messages = chunks * (count - 1)
-
-    def step_fn(step, carry):
+        return lag, far, tile, lanes, buf, first, passed
+
+    def step(self, step):
         for right in (True, False):
-            lag = me if right else count - 1 - me
-            number = step - lag
-            here = (number >= 0) & (number < messages)
-            number = jnp.clip(number, 0, messages - 1)
-            chunk = number // (count - 1)
-            far = count - 1 - number % (count - 1)
-            block = far if right else count - 1 - far
-            buf, tile, lanes, first, passed = copies(right, block, chunk)
+            lag = self.me if right else self.count - 1 - self.me
+            number = step - self.spacing * lag
+            here = (number >= 0) & (number < self.messages)
+            number = jnp.clip(number, 0, self.messages - 1)
+            lag, far, tile, lanes, buf, first, passed = self.place(right, number)
 
             @pl.when(here & (lag == 0))
             def start():
@@ -340,69 +343,286 @@
             def middle():
                 first().wait_recv()
                 buf[tile, lanes] = (
-                    buf[tile, lanes].astype(f32) + p_ref[tile, lanes].astype(f32)
+                    buf[tile, lanes].astype(f32) + self.p_ref[tile, lanes].astype(f32)
                 ).astype(bf16)
                 passed().start()
 
             @pl.when(here & (lag > 0) & (far == lag))
             def last():
                 first().wait_recv()
-                out_ref[tile, :] += buf[tile, lanes].astype(f32)
-
-        return carry
-
-    lax.fori_loop(0, messages + count - 1, step_fn, 0)
-
-    def drain(number, carry):
-        chunk = number // (count - 1)
-        far = count - 1 - number % (count - 1)
-        for right in (True, False):
-            lag = me if right else count - 1 - me
-            block = far if right else count - 1 - far
-
-            @pl.when(far > lag)
-            def sent():
-                copies(right, block, chunk)[3]().wait_send()
-
-        return carry
-
-    lax.fori_loop(0, messages, drain, 0)
-
-
-def scatter_features(partial, count, cid):
-    chunks = 8
-    words, whole = partial.shape
-    return pl.pallas_call(
-        functools.partial(scatter_kernel, count, chunks),
-        out_shape=jax.ShapeDtypeStruct((words, whole // count), f32),
-        in_specs=[VMEM],
-        out_specs=VMEM,
-        scratch_shapes=[pltpu.VMEM((words, whole), bf16)] * 2 + [DMA((count, chunks))] * 4,
-        compiler_params=params(cid, 20),
-        name="scatter_features",
-    )(partial)
-
-
-def conv_backward_kernel(count, chars, chunks, cuts, ids_ref, y_ref, w_ref, wb_ref, off_ref,
-                         log_ref, prev_ref, part_ref, *rest):
-    if cuts:
-        (hw_ref, tr_ref, dw_ref, table_ref, hw_out, tr_out, pad_ref, got_ref, part_send, part_recv,
-         hw0, hw0_in, tr0, tr0_in, hwa1, hwb1, tra1, trb1, hwa2, hwb2, tra2, trb2,
-         local_sem, dp_send, dp_recv) = rest
-    else:
-        dw_ref, table_ref, pad_ref, got_ref, part_send, part_recv = rest
-    me = lax.axis_index("tensor")
-    place = lax.axis_index("dp")
-    words, filters = log_ref.shape
-    rows = words // chunks
-    padded = y_ref.shape[0]
+                self.out_ref[tile, :] += buf[tile, lanes].astype(f32)
+
+    def drain(self):
+        def one(number, carry):
+            for right in (True, False):
+                lag, far, tile, lanes, buf, first, passed = self.place(right, number)
+
+                @pl.when(far > lag)
+                def sent():
+                    first().wait_send()
+
+            return carry
+
+        lax.fori_loop(0, self.messages, one, 0)
+
+
+class DpSum:
+    def __init__(self, cell, peers, x_first, sems, base):
+        self.c, self.x, self.y = cell
+        self.peers, self.x_first, self.base = peers, x_first, base
+        self.send, self.recv = sems
+        self.src = self.in0 = self.in1 = self.mid = self.in2 = self.out = None
+
+    def remote(self, number, src, dst, bit):
+        return pltpu.make_async_remote_copy(
+            src_ref=src,
+            dst_ref=dst,
+            send_sem=self.send.at[self.base + number],
+            recv_sem=self.recv.at[self.base + number],
+            device_id=self.peers[bit],
+            device_id_type=MESH,
+        )
+
+    def copy0(self):
+        return self.remote(0, self.src.at[:, :, 1 - self.c], self.in0, 0)
+
+    def copy1(self):
+        if self.x_first:
+            return self.remote(1, self.src.at[:, 1 - self.x, self.c], self.in1, 1)
+        return self.remote(1, self.src.at[1 - self.y, :, self.c], self.in1, 2)
+
+    def copy2(self):
+        own = self.y if self.x_first else self.x
+        return self.remote(2, self.mid.at[1 - own], self.in2, 2 if self.x_first else 1)
+
+    def finish0(self):
+        self.copy0().wait()
+
+        def one(k, carry):
+            i, j = k // 2, k % 2
+            self.src[i, j, self.c] = (
+                self.src[i, j, self.c].astype(f32) + self.in0[i, j].astype(f32)
+            ).astype(bf16)
+            return carry
+
+        lax.fori_loop(0, 4, one, 0)
+
+    def finish1(self):
+        self.copy1().wait()
+
+        def one(k, carry):
+            kept = self.src[k, self.x, self.c] if self.x_first else self.src[self.y, k, self.c]
+            self.mid[k] = (kept.astype(f32) + self.in1[k].astype(f32)).astype(bf16)
+            return carry
+
+        lax.fori_loop(0, 2, one, 0)
+
+    def finish2(self):
+        self.copy2().wait()
+        own = self.y if self.x_first else self.x
+        self.out[...] = self.mid[own].astype(f32) + self.in2[...].astype(f32)
+
+
+def dp_cell(place):
     cell = [place % 2, (place // 2) % 2, place // 4]
-    peers = [{"dp": place + (1 - 2 * cell[bit]) * 2**bit} for bit in range(3)] if cuts else []
-    peers += [{"tensor": lax.rem(me + k, count)} for k in range(1, count)]
+    return cell, [{"dp": place + (1 - 2 * cell[bit]) * 2**bit} for bit in range(3)]
+
+
+def greet_all(peers):
     barrier = pltpu.get_barrier_semaphore()
     for peer in peers:
         pl.semaphore_signal(barrier, inc=1, device_id=peer, device_id_type=MESH)
     pl.semaphore_wait(barrier, len(peers))
+
+
+def mix_back(d_hidden, trans, gate_pre, previous):
+    gate = jax.nn.sigmoid(gate_pre)
+    sig = jax.nn.sigmoid(trans)
+    act = trans * sig
+    d_trans = (d_hidden * gate * (sig * (1.0 + trans * (1.0 - sig)))).astype(bf16)
+    d_gate = (d_hidden * (act - previous) * gate * (1.0 - gate)).astype(bf16)
+    return d_trans, d_gate, (1.0 - gate) * d_hidden
+
+
+def weight_grad_piece(piece, whole_ref, d_refs, outs):
+    rows = outs[0].shape[-2]
+    lanes = pl.ds(pl.multiple_of(piece * rows, rows), rows)
+    index = (piece // 4, (piece // 2) % 2, piece % 2)
+    for d_ref, out in zip(d_refs, outs):
+        out[index] = dot(whole_ref[:, lanes], d_ref[...], 0, 0).astype(bf16)
+
+
+def highway_back_kernel(count, chunks, reduce, *refs):
+    (d_h2_ref, t1_ref, g1_ref, h1_ref, t0_ref, g0_ref, h0_ref, whole1_ref, w_ref) = refs[:9]
+    refs = refs[9:]
+    if reduce:
+        tra_ref, trb_ref = refs[:2]
+        refs = refs[2:]
+    part0_ref, prev0_ref, dt0_ref, dg0_ref, sums_ref = refs[:5]
+    refs = refs[5:]
+    if reduce:
+        mids = refs[:4]
+        hw_a, hw_b = refs[4:6]
+        in0s, in1s = refs[6:10], refs[10:14]
+        dp_sems = refs[14:16]
+        refs = refs[16:]
+    else:
+        hw_a, hw_b = refs[:2]
+        refs = refs[2:]
+    part1_ref, from_left, from_right, d_h1_ref, dt1_ref, dg1_ref = refs[:6]
+    sems = refs[6:]
+    me = lax.axis_index("tensor")
+    words, filters = d_h2_ref.shape
+    ring = [{"tensor": lax.rem(me + k, count)} for k in range(1, count)]
+    items = []
+    if reduce:
+        cell, peers = dp_cell(lax.axis_index("dp"))
+        greet_all(peers + ring)
+        for k, src in enumerate((hw_a, hw_b, tra_ref, trb_ref)):
+            item = DpSum(cell, peers, k % 2 == 0, dp_sems, 3 * k)
+            item.src, item.in0, item.in1, item.mid = src, in0s[k], in1s[k], mids[k]
+            items.append(item)
+        for item in items[2:]:
+            item.copy0().start()
+    else:
+        greet_all(ring)
+
+    def back(layer, d_h_ref, t_ref, g_ref, h_ref, dt_ref, dg_ref, prev_ref, p_ref):
+        dt, dg, prev = mix_back(d_h_ref[...], t_ref[...], g_ref[...], h_ref[...])
+        dt_ref[...] = dt
+        dg_ref[...] = dg
+        prev_ref[...] = prev
+        for j, d in enumerate((dt, dg)):
+            sums_ref[2 * layer + j : 2 * layer + j + 1, :] = jnp.sum(
+                d.astype(f32), axis=0, keepdims=True
+            )
+
+        def one(block, carry):
+            lanes = pl.ds(pl.multiple_of(block * filters, filters), filters)
+            p_ref[:, lanes] = (
+                dot(dt_ref[...], w_ref[layer, 0, lanes, :], 1, 1)
+                + dot(dg_ref[...], w_ref[layer, 1, lanes, :], 1, 1)
+            ).astype(bf16)
+            return carry
+
+        lax.fori_loop(0, count, one, 0)
+
+    back(1, d_h2_ref, t1_ref, g1_ref, h1_ref, dt1_ref, dg1_ref, d_h1_ref, part1_ref)
+    d_h1_ref[...] += part1_ref[
+        :, pl.ds(pl.multiple_of(me * filters, filters), filters)
+    ].astype(f32)
+    scatter = LineScatter(
+        count, me, chunks, 3, part1_ref, d_h1_ref, from_left, from_right, sems
+    )
+
+    def step_fn(step, carry):
+        scatter.step(step)
+
+        @pl.when(step < 8)
+        def grads():
+            weight_grad_piece(step, whole1_ref, (dt1_ref, dg1_ref), (hw_a, hw_b))
+
+        if reduce:
+
+            @pl.when(step == 8)
+            def start0():
+                for item in items[:2]:
+                    item.copy0().start()
+                for item in items[2:]:
+                    item.finish0()
+                    item.copy1().start()
+
+            @pl.when(step == 16)
+            def start1():
+                for item in items[:2]:
+                    item.finish0()
+                    item.copy1().start()
+
+        return carry
+
+    lax.fori_loop(0, scatter.steps, step_fn, 0)
+    back(0, d_h1_ref, t0_ref, g0_ref, h0_ref, dt0_ref, dg0_ref, prev0_ref, part0_ref)
+    for item in items:
+        item.finish1()
+    scatter.drain()
+
+
+def highway_back(d_h2, t1, g1, h1, t0, g0, h0, whole1, weight, tra, trb, count, cid):
+    words, filters = d_h2.shape
+    chunks = 8
+    reduce = tra is not None
+    rows = whole1.shape[1] // 8
+    shape = jax.ShapeDtypeStruct
+    out_shape = [
+        shape(whole1.shape, bf16),
+        shape((words, filters), f32),
+        shape((words, filters), bf16),
+        shape((words, filters), bf16),
+        shape((4, filters), f32),
+    ]
+    operands = [d_h2, t1, g1, h1, t0, g0, h0, whole1, weight]
+    hw_shape = (2, 2, 2, rows, filters)
+    scratch = []
+    if reduce:
+        operands += [tra, trb]
+        tails = [hw_shape[-2:], hw_shape[-2:], tra.shape[-2:], trb.shape[-2:]]
+        out_shape += [shape((2,) + tail, bf16) for tail in tails]
+        scratch += [pltpu.VMEM(hw_shape, bf16)] * 2
+        scratch += [pltpu.VMEM((2, 2) + tail, bf16) for tail in tails]
+        scratch += [pltpu.VMEM((2,) + tail, bf16) for tail in tails]
+        scratch += [DMA((12,))] * 2
+    else:
+        out_shape += [shape(hw_shape, bf16)] * 2
+    scratch += [pltpu.VMEM(whole1.shape, bf16)] * 3
+    scratch += [pltpu.VMEM((words, filters), f32)] + [pltpu.VMEM((words, filters), bf16)] * 2
+    scratch += [DMA((count, chunks))] * 4
+    return pl.pallas_call(
+        functools.partial(highway_back_kernel, count, chunks, reduce),
+        out_shape=tuple(out_shape),
+        in_specs=[VMEM] * len(operands),
+        out_specs=tuple([VMEM] * len(out_shape)),
+        scratch_shapes=scratch,
+        compiler_params=params(cid, 58),
+        name="highway_back",
+    )(*operands)
+
+
+def conv_backward_kernel(count, chars, chunks, cuts, *refs):
+    (ids_ref, y_ref, w_ref, wb_ref, off_ref, log_ref, prev_ref, part_ref, whole_ref, dt_ref,
+     dg_ref) = refs[:11]
+    refs = refs[11:]
+    if cuts:
+        mids_in = refs[:4]
+        dw_ref, table_ref = refs[4:6]
+        outs = refs[6:12]
+        hw_a, hw_b = refs[12:14]
+        in0s, in1s, mids, in2s = refs[14:16], refs[16:18], refs[18:20], refs[20:26]
+        dp_sems = refs[26:28]
+        refs = refs[28:]
+    else:
+        dw_ref, table_ref, hw_a, hw_b = refs[:4]
+        refs = refs[4:]
+    pad_ref, got_ref, part_send, part_recv = refs
+    me = lax.axis_index("tensor")
+    words, filters = log_ref.shape
+    rows = words // chunks
+    padded = y_ref.shape[0]
+    peers = [{"tensor": lax.rem(me + k, count)} for k in range(1, count)]
+    items = []
+    if cuts:
+        cell, dp_peers = dp_cell(lax.axis_index("dp"))
+        greet_all(dp_peers + peers)
+        for k in range(6):
+            item = DpSum(cell, dp_peers, k % 2 == 0, dp_sems, 3 * k)
+            item.in2, item.out = in2s[k], outs[k]
+            if k < 2:
+                item.src, item.in0, item.in1 = (hw_a, hw_b)[k], in0s[k], in1s[k]
+                item.mid = mids[k]
+            else:
+                item.mid = mids_in[k - 2]
+            items.append(item)
+    else:
+        greet_all(peers)
 
     def part_copy(hop, chunk):
         to = lax.rem(me + hop, count)
@@ -422,93 +642,16 @@
         return carry
 
     lax.fori_loop(0, chunks, part_start, 0)
-
-    stages = []
-    if cuts:
-        c, x, y = cell
-        half = hw_ref.shape[0] // 2
-        lane_a, lane_b = tra1.shape[-1], trb1.shape[-1]
-        part_a, part_b = pl.ds(0, lane_a), pl.ds(lane_a, lane_b)
-
-        def remote(number, src, dst, bit):
-            return pltpu.make_async_remote_copy(
-                src_ref=src, dst_ref=dst, send_sem=dp_send.at[number], recv_sem=dp_recv.at[number],
-                device_id=peers[bit], device_id_type=MESH,
-            )
-
-        keep = [
-            pltpu.make_async_copy(hw_ref.at[:, :, :, c], hw0, local_sem.at[0]),
-            pltpu.make_async_copy(tr_ref.at[:, :, c], tr0, local_sem.at[1]),
-        ]
-        stages = [
-            [
-                remote(0, hw_ref.at[:, :, :, 1 - c], hw0_in, 0),
-                remote(1, tr_ref.at[:, :, 1 - c], tr0_in, 0),
-            ],
-            [
-                remote(2, hw0.at[pl.ds(0, half), :, 1 - x], hwa1, 1),
-                remote(3, hw0.at[pl.ds(half, half), 1 - y], hwb1, 2),
-                remote(4, tr0.at[:, 1 - x, :, part_a], tra1, 1),
-                remote(5, tr0.at[1 - y, :, :, part_b], trb1, 2),
-            ],
-            [
-                remote(6, hw0.at[pl.ds(0, half), 1 - y, x], hwa2, 2),
-                remote(7, hw0.at[pl.ds(half, half), y, 1 - x], hwb2, 1),
-                remote(8, tr0.at[1 - y, x, :, part_a], tra2, 2),
-                remote(9, tr0.at[y, 1 - x, :, part_b], trb2, 1),
-            ],
-        ]
-
-        def add(ref, index, other):
-            ref[index] = (ref[index].astype(f32) + other.astype(f32)).astype(bf16)
-
-        def after0():
-            for copy in keep:
-                copy.wait()
-            for copy in stages[0]:
-                copy.wait()
-
-            def one(k, carry):
-                for i in range(2):
-                    for j in range(2):
-                        add(hw0, (k, i, j), hw0_in[k, i, j])
-                return carry
-
-            lax.fori_loop(0, 2 * half, one, 0)
-            for i in range(2):
-                for j in range(2):
-                    add(tr0, (i, j), tr0_in[i, j])
-
-        def after1():
-            for copy in stages[1]:
-                copy.wait()
-
-            def one(k, carry):
-                for i in range(2):
-                    add(hw0, (k, i, x), hwa1[k, i])
-                    add(hw0, (k + half, y, i), hwb1[k, i])
-                return carry
-
-            lax.fori_loop(0, half, one, 0)
-            for i in range(2):
-                add(tr0, (i, x, slice(None), part_a), tra1[i])
-                add(tr0, (y, i, slice(None), part_b), trb1[i])
-
-        def after2():
-            for copy in stages[2]:
-                copy.wait()
-
-            def one(k, carry):
-                hw_out[k] = hw0[k, y, x].astype(f32) + hwa2[k].astype(f32)
-                hw_out[k + half] = hw0[k + half, y, x].astype(f32) + hwb2[k].astype(f32)
-                return carry
-
-            lax.fori_loop(0, half, one, 0)
-            tr_out[:, part_a] = tr0[y, x, :, part_a].astype(f32) + tra2[...].astype(f32)
-            tr_out[:, part_b] = tr0[y, x, :, part_b].astype(f32) + trb2[...].astype(f32)
-
-        for copy in keep + stages[0]:
-            copy.start()
+    for item in items[2:]:
+        item.copy2().start()
+
+    def grads(piece, carry):
+        weight_grad_piece(piece, whole_ref, (dt_ref, dg_ref), (hw_a, hw_b))
+        return carry
+
+    lax.fori_loop(0, 8, grads, 0)
+    for item in items[:2]:
+        item.copy0().start()
 
     dw_ref[...] = jnp.zeros_like(dw_ref)
     table_ref[...] = jnp.zeros_like(table_ref)
@@ -551,15 +694,16 @@
     tiles = words // WORD_TILE
     if cuts:
         lax.fori_loop(0, cuts[0], tile_step, 0)
-        after0()
-        for copy in stages[1]:
-            copy.start()
+        for item in items[:2]:
+            item.finish0()
+            item.copy1().start()
         lax.fori_loop(cuts[0], cuts[1], tile_step, 0)
-        after1()
-        for copy in stages[2]:
-            copy.start()
+        for item in items[:2]:
+            item.finish1()
+            item.copy2().start()
         lax.fori_loop(cuts[1], tiles, tile_step, 0)
-        after2()
+        for item in items:
+            item.finish2()
     else:
         lax.fori_loop(0, tiles, tile_step, 0)
 
@@ -571,49 +715,40 @@
     lax.fori_loop(0, chunks, part_drain, 0)
 
 
-def conv_backward(ids, y, w, wb, off, logs, prev, part, hw, tr, count, chars, cid):
+def conv_backward(ids, y, w, wb, off, logs, prev, part, whole, dt, dg, mids, count, chars, cid):
     words, filters = logs.shape
     chunks = 8
-    out_shape = [
-        jax.ShapeDtypeStruct((LANES, filters), f32),
-        jax.ShapeDtypeStruct((264, LANES), f32),
-    ]
-    scratch = [
+    shape = jax.ShapeDtypeStruct
+    hw_shape = (2, 2, 2, whole.shape[1] // 8, filters)
+    out_shape = [shape((LANES, filters), f32), shape((264, LANES), f32)]
+    scratch = []
+    operands = [ids, y, w, wb, off, logs, prev, part, whole, dt, dg] + list(mids)
+    cuts = None
+    if mids:
+        cuts = (6, 12)
+        own = [hw_shape[-2:]] * 2
+        tails = own + [mid.shape[-2:] for mid in mids]
+        out_shape += [shape(tail, f32) for tail in tails]
+        scratch += [pltpu.VMEM(hw_shape, bf16)] * 2
+        scratch += [pltpu.VMEM((2, 2) + tail, bf16) for tail in own]
+        scratch += [pltpu.VMEM((2,) + tail, bf16) for tail in own + own]
+        scratch += [pltpu.VMEM(tail, bf16) for tail in tails]
+        scratch += [DMA((18,))] * 2
+    else:
+        out_shape += [shape(hw_shape, bf16)] * 2
+    scratch += [
         pltpu.VMEM((68, WORD_TILE, LANES), bf16),
         pltpu.VMEM((count - 1, words, filters), bf16),
         DMA((count - 1, chunks)),
         DMA((count - 1, chunks)),
     ]
-    operands = [ids, y, w, wb, off, logs, prev, part]
-    in_specs = [VMEM] * 8
-    cuts = None
-    if hw is not None:
-        cuts = (10, 24)
-        mats, rows, cols = hw.shape[0], hw.shape[-2], hw.shape[-1]
-        tr_rows, tr_cols = tr.shape[-2], tr.shape[-1]
-        lane_a = 1536
-        lane_b = tr_cols - lane_a
-        out_shape += [
-            jax.ShapeDtypeStruct((mats, rows, cols), f32),
-            jax.ShapeDtypeStruct((tr_rows, tr_cols), f32),
-        ]
-        operands += [hw, tr]
-        in_specs += [ANY, ANY]
-        half = mats // 2
-        scratch += [pltpu.VMEM((mats, 2, 2, rows, cols), bf16)] * 2
-        scratch += [pltpu.VMEM((2, 2, tr_rows, tr_cols), bf16)] * 2
-        scratch += [pltpu.VMEM((half, 2, rows, cols), bf16)] * 2
-        scratch += [pltpu.VMEM((2, tr_rows, lane), bf16) for lane in (lane_a, lane_b)]
-        scratch += [pltpu.VMEM((half, rows, cols), bf16)] * 2
-        scratch += [pltpu.VMEM((tr_rows, lane), bf16) for lane in (lane_a, lane_b)]
-        scratch += [DMA((2,)), DMA((10,)), DMA((10,))]
     return pl.pallas_call(
         functools.partial(conv_backward_kernel, count, chars, chunks, cuts),
         out_shape=tuple(out_shape),
-        in_specs=in_specs,
+        in_specs=[VMEM] * len(operands),
         out_specs=tuple([VMEM] * len(out_shape)),
         scratch_shapes=scratch,
-        compiler_params=params(cid, 56),
+        compiler_params=params(cid, 58),
         name="conv_backward",
     )(*operands)
 
@@ -713,11 +848,6 @@
 
 def gelu_exact(values):
     return jax.nn.gelu(values, approximate=False)
-
-
-def highway_mix(pre_acts, previous):
-    gate = jax.nn.sigmoid(pre_acts[:, 1])
-    return gate * jax.nn.silu(pre_acts[:, 0]) + (1.0 - gate) * previous
 
 
 def mm(spec, *operands):
@@ -789,9 +919,13 @@
     for layer in range(highway_weight.shape[0]):
         if layer > 0:
             whole = gather_features(hidden.astype(bf16), count, 1 + layer)
-        pre_acts = mm("rk,jkf->rjf", whole, highway_weight[layer]) + highway_bias[layer].astype(f32)
-        kept_layers.append((hidden, whole, pre_acts))
-        hidden = highway_mix(pre_acts, hidden)
+        trans, gate_pre = [
+            mm("rk,kf->rf", whole, highway_weight[layer, j]) + highway_bias[layer, j].astype(f32)
+            for j in range(2)
+        ]
+        kept_layers.append((hidden, whole, trans, gate_pre))
+        gate = jax.nn.sigmoid(gate_pre)
+        hidden = gate * jax.nn.silu(trans) + (1.0 - gate) * hidden
     top_sent = hidden.astype(bf16)
     embedded = sum_rows(mm("sk,kd->sd", top_sent, proj_weight).astype(bf16), count, 4)
     embedded = embedded + proj_bias.astype(f32)
@@ -855,26 +989,9 @@
     d_proj_t = mm("sd,sk->dk", grads_emb, top_sent)
     d_hidden = mm("sd,kd->sk", grads_emb, proj_weight)
 
-    hw_parts = []
-    hw_bias_parts = []
-    for layer in reversed(range(len(kept_layers))):
-        previous, whole, pre_acts = kept_layers[layer]
-        unused, mix_pull = jax.vjp(highway_mix, pre_acts, previous)
-        d_pre, d_previous = mix_pull(d_hidden)
-        d_pre = d_pre.astype(bf16)
-        hw_parts.insert(0, mm("rk,rjf->jkf", whole, d_pre).astype(bf16))
-        hw_bias_parts.insert(0, jnp.sum(d_pre.astype(f32), axis=0))
-        partial_sum = mm("rjf,jkf->rk", d_pre, highway_weight[layer]).astype(bf16)
-        if layer > 0:
-            d_hidden = d_previous + scatter_features(partial_sum, count, 8 + layer)
-    hw_bias_part = jnp.concatenate(hw_bias_parts, axis=0)
-
-    mats = 2 * len(kept_layers)
-    hw_all = jnp.concatenate(hw_parts, axis=0)
-    tr_all = jnp.concatenate(
+    tr_a = jnp.concatenate([d_up.astype(bf16), d_down_t.astype(bf16)], axis=1)
+    tr_b = jnp.concatenate(
         [
-            d_up.astype(bf16),
-            d_down_t.astype(bf16),
             d_proj_t.astype(bf16),
             d_qkv.astype(bf16),
             jnp.zeros((features, 64), bf16),
@@ -883,26 +1000,37 @@
         ],
         axis=1,
     )
-    small = (ids_tiles, y, w_all, w_back, off, logs, d_previous, partial_sum)
+    (h0, whole0, t0, g0), (h1, whole1, t1, g1) = kept_layers
+    mats = 4
+    back_args = (d_hidden, t1, g1, h1, t0, g0, h0, whole1, highway_weight)
+    conv_args = (ids_tiles, y, w_all, w_back, off, logs)
     if dp_count == 8 and (features // dp_count) % 16 == 0:
-        d_w_all, table_all, hw_sum, tr_sum = conv_backward(
-            *small,
-            hw_all.reshape(mats, 2, 2, 2, -1, filters),
-            tr_all.reshape(2, 2, 2, features // dp_count, -1),
-            count,
-            chars,
-            10,
+        blocks = (2, 2, 2, features // dp_count, -1)
+        part0, prev0, dt0, dg0, hw_bias_part, *mids = highway_back(
+            *back_args, tr_a.reshape(blocks), tr_b.reshape(blocks), count, 9
         )
+        d_w_all, table_all, *sums = conv_backward(
+            *conv_args, prev0, part0, whole0, dt0, dg0, mids, count, chars, 10
+        )
+        hw_sum = jnp.stack(sums[:4])
+        tr_a, tr_b = sums[4:]
     else:
-        d_w_all, table_all = conv_backward(*small, None, None, count, chars, 10)
-        hw_sum = lax.psum_scatter(hw_all, "dp", scatter_dimension=1, tiled=True).astype(f32)
-        tr_sum = lax.psum_scatter(tr_all, "dp", scatter_dimension=0, tiled=True).astype(f32)
-    hw_w_grad = hw_sum.reshape(len(kept_layers), 2, -1, filters)
-    up_w_grad = tr_sum[:, :768]
-    down_w_grad = tr_sum[:, 768:1536].T
-    proj_w_grad = tr_sum[:, 1536:2048].T
-    qkv_w_grad = tr_sum[:, 2048:2624].reshape(-1, 3, heads * HEAD_DIM)
-    out_w_grad = tr_sum[:, 2688:2880].T
+        part0, prev0, dt0, dg0, hw_bias_part, *hw1 = highway_back(*back_args, None, None, count, 9)
+        d_w_all, table_all, *hw0 = conv_backward(
+            *conv_args, prev0, part0, whole0, dt0, dg0, (), count, chars, 10
+        )
+        hw_sum = jnp.stack([part.reshape(-1, filters) for part in hw0 + hw1])
+        hw_sum = lax.psum_scatter(hw_sum, "dp", scatter_dimension=1, tiled=True).astype(f32)
+        tr_a, tr_b = [
+            lax.psum_scatter(part, "dp", scatter_dimension=0, tiled=True).astype(f32)
+            for part in (tr_a, tr_b)
+        ]
+    hw_w_grad = hw_sum.reshape(2, 2, -1, filters)
+    up_w_grad = tr_a[:, :768]
+    down_w_grad = tr_a[:, 768:].T
+    proj_w_grad = tr_b[:, :512].T
+    qkv_w_grad = tr_b[:, 512:1088].reshape(-1, 3, heads * HEAD_DIM)
+    out_w_grad = tr_b[:, 1152:1344].T
 
     table_part = jnp.sum(
         table_all[:vocab, :taps_dim].reshape(vocab, taps_dim // char_dim, char_dim), axis=1
@@ -937,9 +1065,7 @@
         tap_of < np.tile(widths, count)[None], conv_all[:taps_dim], 0.0
     )
     conv_b_grad = conv_all[taps_dim]
-    hw_b_grad = jnp.swapaxes(piece(1).reshape(count, mats, filters), 0, 1).reshape(
-        len(kept_layers), 2, -1
-    )
+    hw_b_grad = jnp.swapaxes(piece(1).reshape(count, mats, filters), 0, 1).reshape(2, 2, -1)
     qv_grad = jnp.swapaxes(piece(2).reshape(count, 2, -1), 0, 1).reshape(2, -1)
     up_b_grad = piece(3).reshape(-1)
     table_grad = jnp.sum(piece(4), axis=0).reshape(vocab, char_dim)

time: 616 us -> 506 us (0.82)
  Pallas kernels: 435 us -> 354 us
  matrix products: 69.2 us -> 50.2 us
  local copies, waits for them, and re-layouts: 57.5 us -> 42.6 us
    pallas_call x1, Pallas kernels: 132 us -> 60.2 us  [conv_backward(): pl.pallas_call(functools.partial(conv_backward_kernel, count, chars, chun...]
    dot_general x26 -> x24, matrix products: 64.4 us -> 44.7 us  [mm(): return jnp.einsum(spec, *operands, preferred_element_type=f32)]
    concatenate x3, local copies, waits for them, and re-layouts: 19.1 us -> 9.08 us  [the longest x2 4.8 us: body(): jnp.concatenate([d_proj_t.astype(bf16), d_qkv.astype(bf16), jnp.zeros((fe...]
    pallas_call x6, Pallas kernels: 197 us -> 188 us  [the longest x5 101 us: sum_rows(): pl.pallas_call(functools.partial(sum_kernel, count, chunks, 3), out_shape...]
    unnamed x166 -> x173, local copies, waits for them, and re-layouts: 16.8 us -> 10.3 us
where the time goes in v2:
time: 506 us; the launch traced here: 498 us
  Pallas kernels  354 us (70%)
  matrix products  50.2 us (10%)
  local copies, waits for them, and re-layouts  42.6 us (8%)
  other arithmetic  29.7 us (6%)
  blocking collectives  18 us (4%)
    pallas_call x5, Pallas kernels, sum_rows(): pl.pallas_call(functools.partial(sum_kernel, count, chunks, 3), out_shape...  101 us
    pallas_call x1, Pallas kernels, highway_back(): pl.pallas_call(functools.partial(highway_back_kernel, count, chunks, redu...  87.3 us
    pallas_call x1, Pallas kernels, conv_backward(): pl.pallas_call(functools.partial(conv_backward_kernel, count, chars, chun...  60.2 us
    dot_general x24, matrix products, mm(): return jnp.einsum(spec, *operands, preferred_element_type=f32)  44.7 us
    pallas_call x1, Pallas kernels, conv_forward(): pl.pallas_call(functools.partial(conv_forward_kernel, count, chars, chunk...  40.8 us
    pallas_call x1, Pallas kernels, gather_features(): pl.pallas_call(functools.partial(gather_kernel, count, chunks), out_shape...  32.7 us
    pallas_call x1, Pallas kernels, sum_small(): pl.pallas_call(functools.partial(small_kernel, dp_count, count), out_shap...  32.3 us
    all_gather x1, blocking collectives, body(): lax.all_gather(out_grad[:, 0], 'tensor', axis=0, tiled=True).astype(f32)  18 us

profile of v2, /device:TPU:1, one launch (start us, length us, event | category | flops | bytes accessed | tf_op | source)
XLA Modules:
  0.0 497.5 jit_solution(15168951908472413880)
XLA Ops:
  5.5 1.3 convert_element_type.229
  6.7 1.3 convert_element_type.231
  8.0 1.3 convert_element_type.234
  13.5 1.0 broadcast_select_fusion
  14.5 1.4 fusion.80
  15.9 1.1 copy.91
  18.2 18.0 %all-gather = bf16[512,1,768]{2,0,1:T(8,128)(2,1)S(1)} all-gather(bf16[128,1,768]{2,0,1:T(8,128)(2,1)S(1)} %copy-done.39), channel_id=2, replica_groups=mesh['dp'=8,'tensor'=4] {'tensor'}, dimensions={0}, use_global_device_ids=true | all-gather | bytes 983040 | tf_op jit(solution)/shard_map/all_gather | solution.py:891
  36.9 11.9 %add_convert_fusion.y_ref.refs_1_ = bf16[56,512,128]{2,1,0:T(8,128)(2,1)S(1)} fusion(s32[56,512]{1,0:T(8,128)S(1)} %copy.92, f32[56,128]{1,0:T(8,128)S(1)} %copy-done.77, bf16[262,112]{1,0:T(8,128)(2,1)S(1)} %copy.93), kind=kOutput, calls=%fused_computation.4 | convolution fusion | flops 1937940480 | bytes 7542080 | tf_op jit(solution)/shard_map/qwv,vl->qwl/dot_general | solution.py:854
  48.9 40.8 %conv_forward.1 = (f32[512,512]{1,0:T(8,128)S(1)}, bf16[512,2048]{1,0:T(8,128)(2,1)S(1)}) custom-call(bf16[56,512,128]{2,1,0:T(8,128)(2,1)S(1)} %add_convert_fusion.y_ref.refs_1_, bf16[128,512]{1,0:T(8,128)(2,1)S(1)} %get-tuple-element.180.w_ref.refs_2_, f32[1,512]{1,0:T(1,128)S(1)} %copy-done.7), custom_call_target="tpu_custom_call" | custom-call | tf_op jit(solution)/shard_map/conv_forward/pallas_call | solution.py:165
  89.7 1.2 fusion.33.refs_5_
  91.4 3.1 fusion.77
  94.5 32.7 %gather_features.1.refs_7_ = bf16[512,2048]{1,0:T(8,128)(2,1)S(1)} custom-call(bf16[512,512]{1,0:T(8,128)(2,1)S(1)} %get-tuple-element.170.x_ref), custom_call_target="tpu_custom_call" | custom-call | tf_op jit(solution)/shard_map/gather_features/pallas_call | solution.py:202
  127.2 1.2 fusion.39.refs_2_
  128.5 2.6 add_convert_fusion.5
  131.7 22.8 %sum_rows.5 = f32[512,768]{1,0:T(8,128)S(1)} custom-call(bf16[512,768]{1,0:T(8,128)(2,1)S(1)} %convolution_convert_fusion.8.p_ref), custom_call_target="tpu_custom_call" | custom-call | tf_op jit(solution)/shard_map/sum_rows/pallas_call | solution.py:284
  157.3 1.0 fusion.78
  158.2 4.7 fusion.82
  162.9 2.5 convolution_convert_fusion.11
  166.1 21.2 %sum_rows.6 = f32[512,768]{1,0:T(8,128)S(1)} custom-call(bf16[512,768]{1,0:T(8,128)(2,1)S(1)} %convolution_convert_fusion.7.p_ref), custom_call_target="tpu_custom_call" | custom-call | tf_op jit(solution)/shard_map/sum_rows/pallas_call | solution.py:284
  188.8 4.0 multiply_convert_fusion.1
  193.6 17.6 %sum_rows.7 = f32[512,768]{1,0:T(8,128)S(1)} custom-call(bf16[512,768]{1,0:T(8,128)(2,1)S(1)} %convolution_convert_fusion.4.p_ref), custom_call_target="tpu_custom_call" | custom-call | tf_op jit(solution)/shard_map/sum_rows/pallas_call | solution.py:284
  215.4 1.2 copy-done.11
  217.4 1.8 convert_reduce_fusion.4
  220.9 1.0 convolution_convert_fusion.1
  221.9 1.6 pad_maximum_fusion
  223.4 4.3 copy.99
  227.7 18.2 %sum_rows.8 = f32[512,768]{1,0:T(8,128)S(1)} custom-call(bf16[512,768]{1,0:T(8,128)(2,1)S(1)} %convolution_convert_fusion.3.p_ref), custom_call_target="tpu_custom_call" | custom-call | tf_op jit(solution)/shard_map/sum_rows/pallas_call | solution.py:284
  245.9 2.3 multiply_reduce_fusion.1
  251.1 1.0 copy-done.14
  257.0 2.0 convolution_convert_fusion.6.p_ref
  259.0 21.0 %sum_rows.9 = f32[512,768]{1,0:T(8,128)S(1)} custom-call(bf16[512,768]{1,0:T(8,128)(2,1)S(1)} %convolution_convert_fusion.6.p_ref), custom_call_target="tpu_custom_call" | custom-call | tf_op jit(solution)/shard_map/sum_rows/pallas_call | solution.py:284
  280.1 1.8 fusion.71
  282.5 2.3 multiply_reduce_fusion.2
  284.9 1.2 convert_reduce_fusion.3
  286.7 2.8 fusion.83.refs_0_
  289.5 1.5 fusion.32
  291.0 1.8 fusion.31
  293.5 1.1 fusion.47
  295.2 4.2 copy.100
  299.3 87.3 %highway_back.1 = (bf16[512,2048]{1,0:T(8,128)(2,1)}, f32[512,512]{1,0:T(8,128)}, bf16[512,512]{1,0:T(8,128)(2,1)}, bf16[512,512]{1,0:T(8,128)(2,1)}, f32[4,512]...) custom-call(f32[512,512]{1,0:T(8,128)} %fusion.83.refs_0_, ...), custom_call_target="tpu_custom_call" | custom-call | tf_op jit(solution)/shard_map/highway_back/pallas_call | solution.py:579
  386.7 60.2 %conv_backward.1 = (f32[128,512]{1,0:T(8,128)}, f32[264,128]{1,0:T(8,128)}, f32[256,512]{1,0:T(8,128)}, f32[256,512]{1,0:T(8,128)}, f32[256,512]{1,0:T(8,128)}, ...) custom-call(s32[16,1792]{1,0:T(8,128)} %reshape.303.refs_0_, bf16[56,512,128]{2,1,0:T(8,128)(2,1)} %copy-done.2, ...), custom_call_target="tpu_custom_call" | custom-call | tf_op jit(solution)/shard_map/conv_backward/pallas_call | solution.py:745
  447.0 1.0 slice.163
  448.1 1.0 copy.101
  450.2 1.9 concatenate.23
  453.1 0.9 copy.109
  454.0 32.3 %sum_small.1 = bf16[8,4,16,640]{3,2,1,0:T(8,128)(2,1)S(1)} custom-call(f32[8,16,640]{2,1,0:T(8,128)S(1)} %reshape.324.in_ref), custom_call_target="tpu_custom_call" | custom-call | tf_op jit(solution)/shard_map/sum_small/pallas_call | solution.py:818
  493.9 1.0 copy.115
  495.7 1.5 pad_maximum_fusion.1
  (279 shorter events, 44.0 us)
Async XLA Ops:
  0.7 187.7 %copy-start = (bf16[768,768]{1,0:T(8,128)(2,1)S(1)}, bf16[768,768]{1,0:T(8,128)(2,1)}, u32[]{:S(2)}) copy-start(bf16[768,768]{1,0:T(8,128)(2,1)} %param.40) | copy-start | bytes 3538948
  14.5 3.7 copy-start.39
  15.9 32.9 %copy-start.5 = (bf16[128,512]{1,0:T(8,128)(2,1)}, bf16[128,512]{1,0:T(8,128)(2,1)S(1)}, u32[]{:S(2)}) copy-start(bf16[128,512]{1,0:T(8,128)(2,1)S(1)} %get-tuple-element.180.w_ref.refs_2_) | copy-start | bytes 393220
  17.1 19.8 %copy-start.77 = (f32[56,128]{1,0:T(8,128)S(1)}, f32[56,128]{1,0:T(8,128)}, u32[]{:S(2)}) copy-start(f32[56,128]{1,0:T(8,128)} %constant.142) | copy-start | bytes 86020
  36.2 53.5 %slice-start = ((s8[8388608]{0:T(1024)(128)(4,1)}), s8[4194304]{0:T(1024)(128)(4,1)S(1)}, s32[]{:S(2)}) async-start(s8[8388608]{0:T(1024)(128)(4,1)} %bitcast.147), calls=%async_computation | async-start | bytes 8388608
  36.9 11.9 %copy-start.7 = (f32[1,512]{1,0:T(1,128)S(1)}, f32[1,512]{1,0:T(1,128)}, u32[]{:S(2)}) copy-start(f32[1,512]{1,0:T(1,128)} %constant.143.off_ref.refs_4_) | copy-start | bytes 6148
  36.9 52.8 %slice-start.1 = ((s8[8388608]{0:T(1024)(128)(4,1)}), s8[4194304]{0:T(1024)(128)(4,1)S(1)}, s32[]{:S(2)}) async-start(s8[8388608]{0:T(1024)(128)(4,1)} %bitcast.147), calls=%async_computation.1 | async-start | bytes 8388608
  48.9 40.8 %copy-start.2 = (bf16[56,512,128]{2,1,0:T(8,128)(2,1)}, bf16[56,512,128]{2,1,0:T(8,128)(2,1)S(1)}, u32[]{:S(2)}) copy-start(bf16[56,512,128]{2,1,0:T(8,128)(2,1)S(1)} %add_convert_fusion.y_ref.refs_1_) | copy-start | bytes 22020100
  91.4 3.1 copy-start.18
  94.5 33.9 %copy-start.19 = (f32[512,512]{1,0:T(8,128)}, f32[512,512]{1,0:T(8,128)S(1)}, u32[]{:S(2)}) copy-start(f32[512,512]{1,0:T(8,128)S(1)} %get-tuple-element.171.refs_3_) | copy-start | bytes 3145732
  128.5 2.6 copy-start.20
  128.5 2.6 copy-start.25
  131.1 23.4 %copy-start.79 = (bf16[512,512]{1,0:T(8,128)(2,1)}, bf16[512,512]{1,0:T(8,128)(2,1)S(1)}, u32[]{:S(2)}) copy-start(bf16[512,512]{1,0:T(8,128)(2,1)S(1)} %get-tuple-element.188) | copy-start | bytes 1572868
  162.9 2.5 copy-start.16
  165.4 21.9 %copy-start.47 = (f32[512]{0:T(512)S(1)}, f32[512]{0:T(512)}, u32[]{:S(2)}) copy-start(f32[512]{0:T(512)} %copy-done.46) | copy-start | bytes 6148
  165.4 21.9 %copy-start.58 = (f32[768]{0:T(1024)S(1)}, f32[768]{0:T(1024)}, u32[]{:S(2)}) copy-start(f32[768]{0:T(1024)} %convert_element_type.229) | copy-start | bytes 9220
  165.4 21.9 %copy-start.60 = (f32[768]{0:T(1024)S(1)}, f32[768]{0:T(1024)}, u32[]{:S(2)}) copy-start(f32[768]{0:T(1024)} %get-tuple-element.147) | copy-start | bytes 9220
  187.9 32.9 %copy-start.8 = (f32[512,768]{1,0:T(8,128)}, f32[512,768]{1,0:T(8,128)S(1)}, u32[]{:S(2)}) copy-start(f32[512,768]{1,0:T(8,128)S(1)} %get-tuple-element.169) | copy-start | bytes 4718596
  188.0 32.9 %copy-start.42 = (f32[512]{0:T(512)}, f32[512]{0:T(512)S(1)}, u32[]{:S(2)}) copy-start(f32[512]{0:T(512)S(1)} %broadcast_multiply_fusion.1) | copy-start | bytes 6148
  188.3 4.5 copy-start.53
  188.8 32.1 %copy-start.49 = (f32[512]{0:T(512)}, f32[512]{0:T(512)S(1)}, u32[]{:S(2)}) copy-start(f32[512]{0:T(512)S(1)} %fusion.60) | copy-start | bytes 6148
  188.8 4.1 copy-start.75
  193.6 17.6 %copy-start.63 = (f32[768]{0:T(1024)S(1)}, f32[768]{0:T(1024)}, u32[]{:S(2)}) copy-start(f32[768]{0:T(1024)} %convert_element_type.234) | copy-start | bytes 9220
  227.7 18.2 %copy-start.9 = (f32[512,768]{1,0:T(8,128)S(1)}, f32[512,768]{1,0:T(8,128)}, u32[]{:S(2)}) copy-start(f32[512,768]{1,0:T(8,128)} %copy-done.8) | copy-start | bytes 4718596
  227.7 18.2 %copy-start.41 = (f32[768]{0:T(1024)S(1)}, f32[768]{0:T(1024)}, u32[]{:S(2)}) copy-start(f32[768]{0:T(1024)} %get-tuple-element.143) | copy-start | bytes 9220
  227.7 18.2 %copy-start.43 = (f32[512]{0:T(512)S(1)}, f32[512]{0:T(512)}, u32[]{:S(2)}) copy-start(f32[512]{0:T(512)} %copy-done.42) | copy-start | bytes 6148
  227.7 18.2 %copy-start.50 = (f32[512]{0:T(512)S(1)}, f32[512]{0:T(512)}, u32[]{:S(2)}) copy-start(f32[512]{0:T(512)} %copy-done.49) | copy-start | bytes 6148
  245.9 2.9 copy-start.54
  249.5 2.5 copy-start.14
  249.5 2.5 copy-start.71
  252.6 4.4 copy-start.37
  255.7 3.3 copy-start.23
  256.1 2.9 copy-start.27
  259.0 21.1 %copy-start.13 = (f32[512,768]{1,0:T(8,128)S(1)}, f32[512,768]{1,0:T(8,128)}, u32[]{:S(2)}) copy-start(f32[512,768]{1,0:T(8,128)} %copy-done.12) | copy-start | bytes 4718596
  280.1 2.4 copy-start.48
  282.5 2.3 copy-start.10
  286.7 2.8 copy-start.80
  291.0 2.5 copy-start.22
  386.7 61.4 %copy-start.70 = (f32[4,512]{1,0:T(4,128)S(1)}, f32[4,512]{1,0:T(4,128)}, u32[]{:S(2)}) copy-start(f32[4,512]{1,0:T(4,128)} %get-tuple-element.48) | copy-start | bytes 24580
  446.9 3.2 copy-start.44
  446.9 3.2 copy-start.45
  446.9 3.2 copy-start.55
  446.9 3.2 copy-start.56
  447.0 3.2 copy-start.57
  447.0 3.2 copy-start.69
  447.0 3.2 copy-start.72
  452.2 34.1 %copy-start.29 = (f32[96,1536]{1,0:T(8,128)S(1)}, f32[96,1536]{1,0:T(8,128)}, u32[]{:S(2)}) copy-start(f32[96,1536]{1,0:T(8,128)} %get-tuple-element.55) | copy-start | bytes 1769476
  495.0 2.3 copy-start.1
  (35 other events, 46.9 us)

commit v3 on v2

v3 whole, which is shorter than its diff:
```python
import functools
import math

import jax
import jax.numpy as jnp
import numpy as np
from jax import lax
from jax.experimental import pallas as pl
from jax.experimental.pallas import tpu as pltpu
from jax.sharding import PartitionSpec as P

HEAD_DIM = 64
WORD_TILE = 32
LANES = 128

norm_eps = 1e-06
big_neg = -1e30
f32 = jnp.float32
bf16 = jnp.bfloat16
MESH = pl.DeviceIdType.MESH
VMEM = pl.BlockSpec(memory_space=pltpu.VMEM)
ANY = pl.BlockSpec(memory_space=pl.ANY)
DMA = pltpu.SemaphoreType.DMA
MIB = 1 << 20


def params(cid, vmem):
    return pltpu.CompilerParams(
        collective_id=cid, has_side_effects=True, vmem_limit_bytes=vmem * MIB
    )


def width_counts(block):
    unit = block // 64
    return [unit, unit, 2 * unit, 4 * unit, 8 * unit, 16 * unit, 32 * unit]


def filter_widths(block):
    return np.concatenate(
        [np.full((n,), i + 1, np.int32) for i, n in enumerate(width_counts(block))]
    )


def dot(a, b, ca, cb):
    return lax.dot_general(a, b, (((ca,), (cb,)), ((), ())), preferred_element_type=f32)


def line_barrier(me, count):
    barrier = pltpu.get_barrier_semaphore()
    for there, ok in ((me - 1, me > 0), (me + 1, me < count - 1)):

        @pl.when(ok)
        def greet():
            pl.semaphore_signal(barrier, inc=1, device_id={"tensor": there}, device_id_type=MESH)

    pl.semaphore_wait(barrier, jnp.minimum(me, 1) + jnp.minimum(count - 1 - me, 1))


def line_copy(view, me, count, right, block, chunk, sems):
    send, recv = sems[:2] if right else sems[2:]
    to = jnp.minimum(me + 1, count - 1) if right else jnp.maximum(me - 1, 0)
    ref = view(block, chunk)
    return pltpu.make_async_remote_copy(
        src_ref=ref,
        dst_ref=ref,
        send_sem=send.at[block, chunk],
        recv_sem=recv.at[block, chunk],
        device_id={"tensor": to},
        device_id_type=MESH,
    )


def gather_step(view, step, chunks, me, count, sems):
    for hop in range(count):
        chunk = step - hop
        here = (chunk >= 0) & (chunk < chunks)
        safe = jnp.clip(chunk, 0, chunks - 1)
        for right in (True, False):
            block = me - hop if right else me + hop
            there = (block >= 0) & (block < count)
            block = jnp.clip(block, 0, count - 1)
            more = me < count - 1 if right else me > 0
            copy = functools.partial(line_copy, view, me, count, right, block, safe, sems)

            @pl.when(here & there)
            def pass_on():
                if hop > 0:
                    copy().wait_recv()

                @pl.when(more)
                def send():
                    copy().start()


def gather_drain(view, chunks, me, count, sems):
    def one(chunk, carry):
        for hop in range(count):
            for right in (True, False):
                block = me - hop if right else me + hop
                there = (block >= 0) & (block < count)
                block = jnp.clip(block, 0, count - 1)
                more = me < count - 1 if right else me > 0
                copy = functools.partial(line_copy, view, me, count, right, block, chunk, sems)

                @pl.when(there & more)
                def sent():
                    copy().wait_send()

        return carry

    lax.fori_loop(0, chunks, one, 0)


def windows(y_ref, start, chars):
    group = lax.broadcasted_iota(jnp.int32, (1, WORD_TILE, LANES), 2) // 16
    tile = pl.ds(start, WORD_TILE)
    value = y_ref[0:chars, tile, :]
    for tap in range(1, 7):
        value = jnp.where(group == tap, y_ref[tap : chars + tap, tile, :], value)
    return value.reshape(chars * WORD_TILE, LANES)


def conv_forward_kernel(count, chars, chunks, y_ref, w_ref, off_ref, log_ref, whole_ref, x_hbm,
                        p_hbm, x_buf, p_buf, keep_sem, *sems):
    me = lax.axis_index("tensor")
    words, filters = log_ref.shape
    rows = words // chunks
    tiles = words // WORD_TILE
    line_barrier(me, count)

    def view(block, chunk):
        return whole_ref.at[
            pl.ds(pl.multiple_of(chunk * rows, rows), rows),
            pl.ds(pl.multiple_of(block * filters, filters), filters),
        ]

    def keep(index):
        slot = index % 2
        return [
            pltpu.make_async_copy(buf.at[slot], hbm.at[index], keep_sem.at[k, slot])
            for k, (buf, hbm) in enumerate(((x_buf, x_hbm), (p_buf, p_hbm)))
        ]

    def tile_step(index, carry):
        slot = index % 2

        @pl.when(index >= 2)
        def free():
            for copy in keep(index - 2):
                copy.wait()

        start = pl.multiple_of(index * WORD_TILE, WORD_TILE)
        x2 = windows(y_ref, start, chars)
        x_buf[slot] = x2
        conv = dot(x2, w_ref[...], 1, 0).reshape(chars, WORD_TILE, filters)
        top = jnp.max(conv, axis=0)
        exps = jnp.exp(conv - top[None])
        sums = jnp.sum(exps, axis=0)
        p_buf[slot] = (exps * (1.0 / sums)[None]).astype(bf16)
        for copy in keep(index):
            copy.start()
        total = top + jnp.log(sums)
        log_ref[pl.ds(start, WORD_TILE), :] = total
        pooled = total - off_ref[...]
        whole_ref[
            pl.ds(start, WORD_TILE), pl.ds(pl.multiple_of(me * filters, filters), filters)
        ] = (pooled * jax.nn.sigmoid(pooled)).astype(bf16)
        return carry

    per = rows // WORD_TILE

    def chunk_step(step, carry):
        @pl.when(step < chunks)
        def work():
            lax.fori_loop(step * per, step * per + per, tile_step, 0)

        gather_step(view, step, chunks, me, count, sems)
        return carry

    lax.fori_loop(0, chunks + count - 1, chunk_step, 0)
    for index in (tiles - 2, tiles - 1):
        for copy in keep(index):
            copy.wait()
    gather_drain(view, chunks, me, count, sems)


def conv_forward(y, w, off, count, chars, cid):
    words, filters = y.shape[1], w.shape[1]
    chunks = 8
    tiles = words // WORD_TILE
    shape = jax.ShapeDtypeStruct
    return pl.pallas_call(
        functools.partial(conv_forward_kernel, count, chars, chunks),
        out_shape=(
            shape((words, filters), f32),
            shape((words, count * filters), bf16),
            shape((tiles, chars * WORD_TILE, LANES), bf16),
            shape((tiles, chars, WORD_TILE, filters), bf16),
        ),
        in_specs=[VMEM] * 3,
        out_specs=(VMEM, VMEM, ANY, ANY),
        scratch_shapes=[
            pltpu.VMEM((2, chars * WORD_TILE, LANES), bf16),
            pltpu.VMEM((2, chars, WORD_TILE, filters), bf16),
            DMA((2, 2)),
        ]
        + [DMA((count, chunks))] * 4,
        compiler_params=params(cid, 50),
        name="conv_forward",
    )(y, w, off)


def gather_kernel(count, chunks, x_ref, whole_ref, *sems):
    me = lax.axis_index("tensor")
    words, filters = x_ref.shape
    rows = words // chunks
    whole_ref[:, pl.ds(pl.multiple_of(me * filters, filters), filters)] = x_ref[...]
    line_barrier(me, count)

    def view(block, chunk):
        return whole_ref.at[
            pl.ds(pl.multiple_of(chunk * rows, rows), rows),
            pl.ds(pl.multiple_of(block * filters, filters), filters),
        ]

    def chunk_step(step, carry):
        gather_step(view, step, chunks, me, count, sems)
        return carry

    lax.fori_loop(0, chunks + count - 1, chunk_step, 0)
    gather_drain(view, chunks, me, count, sems)


def gather_features(x, count, cid):
    chunks = 4
    return pl.pallas_call(
        functools.partial(gather_kernel, count, chunks),
        out_shape=jax.ShapeDtypeStruct((x.shape[0], count * x.shape[1]), bf16),
        in_specs=[VMEM],
        out_specs=VMEM,
        scratch_shapes=[DMA((count, chunks))] * 4,
        compiler_params=params(cid, 16),
        name="gather_features",
    )(x)


class LineSum:
    def __init__(self, count, me, chunks, spacing, number, p_ref, out_ref, buffers, sems):
        self.count, self.me, self.chunks, self.spacing = count, me, chunks, spacing
        self.number, self.p_ref, self.out_ref = number, p_ref, out_ref
        self.buffers, self.sems = buffers, sems
        self.steps = chunks + spacing * (count - 1)

    def place(self, right, chunk):
        count, me, number = self.count, self.me, self.number
        lag = me if right else count - 1 - me
        rows = self.p_ref.shape[0] // self.chunks
        tile = pl.ds(pl.multiple_of(chunk * rows, rows), rows)
        buf = self.buffers[0 if right else 1]
        send, recv = self.sems[:2] if right else self.sems[2:]
        to = jnp.minimum(me + 1, count - 1) if right else jnp.maximum(me - 1, 0)
        first, passed = [
            functools.partial(
                pltpu.make_async_remote_copy,
                src_ref=src,
                dst_ref=buf.at[number, tile],
                send_sem=send.at[number, chunk],
                recv_sem=recv.at[number, chunk],
                device_id={"tensor": to},
                device_id_type=MESH,
            )
            for src in (self.p_ref.at[tile], buf.at[number, tile])
        ]
        return lag, tile, buf, first, passed

    def step(self, step):
        for right in (True, False):
            lag = self.me if right else self.count - 1 - self.me
            chunk = step - self.spacing * lag
            here = (chunk >= 0) & (chunk < self.chunks)
            chunk = jnp.clip(chunk, 0, self.chunks - 1)
            lag, tile, buf, first, passed = self.place(right, chunk)

            @pl.when(here & (lag == 0))
            def start():
                first().start()

            @pl.when(here & (lag > 0))
            def middle():
                first().wait_recv()
                got = buf[self.number, tile, :].astype(f32)

                @pl.when(lag < self.count - 1)
                def forward():
                    buf[self.number, tile, :] = (got + self.p_ref[tile, :].astype(f32)).astype(bf16)
                    passed().start()

                self.out_ref[tile, :] += got

    def drain(self):
        def one(chunk, carry):
            for right in (True, False):
                lag, tile, buf, first, passed = self.place(right, chunk)

                @pl.when(lag < self.count - 1)
                def sent():
                    first().wait_send()

            return carry

        lax.fori_loop(0, self.chunks, one, 0)

    def run(self, done, extra=()):
        rows = self.p_ref.shape[0] // self.chunks
        fill = self.spacing * (self.count - 1)

        def one(step, carry):
            self.step(step)
            for k, work in enumerate(extra):
                pl.when(step == k)(work)

            @pl.when(step >= fill)
            def finish():
                chunk = jnp.maximum(step - fill, 0)
                done(pl.ds(pl.multiple_of(chunk * rows, rows), rows))

            return carry

        lax.fori_loop(0, self.steps, one, 0)
        self.drain()


def norm_parts(values):
    centered = values - jnp.mean(values, axis=-1, keepdims=True)
    root = lax.rsqrt(jnp.mean(centered * centered, axis=-1, keepdims=True) + norm_eps)
    return centered * root, root


def norm_back(values, gain, cotangent):
    nv, root = norm_parts(values)
    scaled = cotangent * gain
    inner = jnp.mean(scaled, axis=-1, keepdims=True)
    along = jnp.mean(scaled * nv, axis=-1, keepdims=True)
    return root * (scaled - inner - nv * along), cotangent * nv


def gelu_parts(values):
    cdf = 0.5 * (1.0 + lax.erf(values * 0.7071067811865476))
    slope = cdf + values * jnp.exp(-0.5 * values * values) * 0.3989422804014327
    return values * cdf, slope


def column_sum(values):
    return jnp.sum(values, axis=0, keepdims=True)


def encoder_kernel(count, chunks, spacing, *refs):
    (top_ref, pw_ref, qw_ref, ow_ref, uw_ref, dw_ref, vec_ref, ub_ref, qb_ref, og_ref,
     live_ref) = refs[:11]
    enc_ref, dh2_ref, tra_ref, trb_ref, sums_ref, qsum_ref = refs[11:17]
    (emb, inp, midpre, mid, fin, slope, dmid, din, sent, sent_mid, act, d_two, d_up, d_branch,
     d_emb, qkv, attended, probs, d_heads, d_proj, part, grad_all, enc_all, from_left,
     from_right) = refs[17:42]
    line_sems, gather_sems = refs[42:46], refs[46:50]
    me = lax.axis_index("tensor")
    words, features = emb.shape
    heads = attended.shape[1] // HEAD_DIM
    hidden = heads * HEAD_DIM
    scale = HEAD_DIM ** (-0.5)
    own = words // count
    own_tile = pl.ds(pl.multiple_of(me * own, own), own)
    grad_all[own_tile, :] = og_ref[...]
    sums_ref[...] = jnp.zeros_like(sums_ref)
    trb_ref[...] = jnp.zeros_like(trb_ref)
    line_barrier(me, count)

    def line(number, out_ref):
        return LineSum(
            count, me, chunks, spacing, number, part, out_ref, (from_left, from_right), line_sems
        )

    def gather_view(block, chunk):
        return grad_all.at[pl.ds(pl.multiple_of(block * own, own), own)]

    def tiles(size, work):
        def one(index, carry):
            work(pl.ds(pl.multiple_of(index * size, size), size))
            return carry

        lax.fori_loop(0, words // size, one, 0)

    def send_product(lhs, rhs, side, out_ref):
        def work(tile):
            value = dot(lhs[tile, :], rhs[...], 1, side).astype(bf16)
            part[tile, :] = value
            out_ref[tile, :] = value.astype(f32)

        tiles(256, work)

    def grads(lhs, rhs, out_ref, lane):
        def half(k):
            def work():
                depth = features // 2
                value = dot(lhs[:, depth * k : depth * k + depth], rhs[...], 0, 0).astype(bf16)
                for i in range(2):
                    for j in range(2):
                        start = (2 * i + j) * (depth // 4)
                        out_ref[k, i, j, :, lane : lane + rhs.shape[1]] = value[
                            start : start + depth // 4
                        ]

            return work

        return [half(0), half(1)]

    def row(index):
        return vec_ref[index : index + 1, :]

    def add_sum(index, value):
        sums_ref[index : index + 1, :] += column_sum(value)

    send_product(top_ref, pw_ref, 0, emb)

    def first_norm(tile):
        value = emb[tile, :] + row(0)
        emb[tile, :] = value
        value = norm_parts(value)[0] * row(3) + row(6)
        inp[tile, :] = value
        sent[tile, :] = value.astype(bf16)

    line(0, emb).run(first_norm)

    def project(tile):
        qkv[tile, :] = (dot(sent[tile, :], qw_ref[...], 1, 0) + qb_ref[...]).astype(bf16)

    tiles(256, project)

    gather_step(gather_view, 0, 1, me, count, gather_sems)
    for head in range(heads):
        lanes = slice(head * HEAD_DIM, (head + 1) * HEAD_DIM)
        keys = slice(hidden + head * HEAD_DIM, hidden + (head + 1) * HEAD_DIM)
        vals = slice(2 * hidden + head * HEAD_DIM, 2 * hidden + (head + 1) * HEAD_DIM)

        def attend(tile):
            scores = dot(qkv[tile, lanes], qkv[:, keys], 1, 1) * scale
            scores = jnp.where(live_ref[...] > 0.0, scores, big_neg)
            exps = jnp.exp(scores - jnp.max(scores, axis=1, keepdims=True))
            value = exps / jnp.sum(exps, axis=1, keepdims=True)
            probs[head, tile, :] = value
            attended[tile, lanes] = dot(value.astype(bf16), qkv[:, vals], 1, 0).astype(bf16)

        tiles(128, attend)
        if head + 1 < count:
            gather_step(gather_view, head + 1, 1, me, count, gather_sems)
    for step in range(heads + 1, count):
        gather_step(gather_view, step, 1, me, count, gather_sems)
    send_product(attended, ow_ref, 0, midpre)

    def second_norm(tile):
        value = midpre[tile, :] + inp[tile, :] + row(1)
        midpre[tile, :] = value
        value = norm_parts(value)[0] * row(4) + row(7)
        mid[tile, :] = value
        sent_mid[tile, :] = value.astype(bf16)

    line(1, midpre).run(second_norm)

    def feed(tile):
        value, back = gelu_parts(dot(sent_mid[tile, :], uw_ref[...], 1, 0) + ub_ref[...])
        act[tile, :] = value.astype(bf16)
        slope[tile, :] = back

    tiles(128, feed)
    send_product(act, dw_ref, 0, fin)

    def third_norm(tile):
        value = fin[tile, :] + mid[tile, :] + row(2)
        cotangent = grad_all[tile, :].astype(f32)
        enc_all[tile, :] = (norm_parts(value)[0] * row(5) + row(8)).astype(bf16)
        back, gain = norm_back(value, row(5), cotangent)
        fin[tile, :] = back
        low = back.astype(bf16)
        d_two[tile, :] = low
        add_sum(2, low.astype(f32))
        add_sum(5, gain)
        add_sum(8, cotangent)

    line(2, fin).run(third_norm)
    enc_ref[...] = enc_all[own_tile, :]

    def feed_back(tile):
        value = (dot(d_two[tile, :], dw_ref[...], 1, 1) * slope[tile, :]).astype(bf16)
        d_up[tile, :] = value
        add_sum(9, value.astype(f32))

    tiles(128, feed_back)
    send_product(d_up, uw_ref, 1, dmid)
    def second_back(tile):
        cotangent = dmid[tile, :] + fin[tile, :]
        back, gain = norm_back(midpre[tile, :], row(4), cotangent)
        dmid[tile, :] = back
        low = back.astype(bf16)
        d_branch[tile, :] = low
        add_sum(1, low.astype(f32))
        add_sum(4, gain)
        add_sum(7, cotangent)

    work = grads(d_two, act, tra_ref, features) + grads(sent_mid, d_up, tra_ref, 0)
    line(3, dmid).run(second_back, work)

    def heads_back(tile):
        d_heads[tile, :] = dot(d_branch[tile, :], ow_ref[...], 1, 1).astype(bf16)

    tiles(256, heads_back)
    for head in range(heads):
        lanes = slice(head * HEAD_DIM, (head + 1) * HEAD_DIM)
        keys = slice(hidden + head * HEAD_DIM, hidden + (head + 1) * HEAD_DIM)
        vals = slice(2 * hidden + head * HEAD_DIM, 2 * hidden + (head + 1) * HEAD_DIM)
        weights = probs[head]
        d_out = d_heads[:, lanes]
        d_proj[:, vals] = dot(weights.astype(bf16), d_out, 0, 0).astype(bf16)
        d_probs = dot(d_out, qkv[:, vals], 1, 1)
        inner = jnp.sum(d_probs * weights, axis=1, keepdims=True)
        d_scores = (weights * (d_probs - inner)).astype(bf16)
        d_proj[:, lanes] = (dot(d_scores, qkv[:, keys], 1, 0) * scale).astype(bf16)
        d_proj[:, keys] = (dot(d_scores, qkv[:, lanes], 0, 0) * scale).astype(bf16)
    send_product(d_proj, qw_ref, 1, din)
    qsum_ref[...] = column_sum(d_proj[...].astype(f32))

    def first_back(tile):
        cotangent = din[tile, :] + dmid[tile, :]
        back, gain = norm_back(emb[tile, :], row(3), cotangent)
        low = back.astype(bf16)
        d_emb[tile, :] = low
        add_sum(0, low.astype(f32))
        add_sum(3, gain)
        add_sum(6, cotangent)

    work = grads(sent, d_proj, trb_ref, top_ref.shape[1])
    work += grads(d_branch, attended, trb_ref, 1152)
    line(4, din).run(first_back, work)

    def last(tile):
        dh2_ref[tile, :] = dot(d_emb[tile, :], pw_ref[...], 1, 1)

    tiles(256, last)
    for work in grads(d_emb, top_ref, trb_ref, 0):
        work()
    gather_drain(gather_view, 1, me, count, gather_sems)


def encoder(top, weights, vec, up_b, qkv_b, out_grad, live, count, cid):
    words, filters = top.shape
    features = weights[0].shape[1]
    three = weights[1].shape[1]
    units = weights[3].shape[1]
    hidden = three // 3
    chunks, spacing = 16, 3
    shape = jax.ShapeDtypeStruct
    rows = features // 8
    wide = [(words, features)]
    scratch = [pltpu.VMEM((words, n), f32) for n in [features] * 5 + [units] + [features] * 2]
    scratch += [
        pltpu.VMEM((words, n), bf16)
        for n in (features, features, units, features, units, features, features, three, hidden)
    ]
    scratch += [pltpu.VMEM((hidden // HEAD_DIM, words, words), f32)]
    scratch += [pltpu.VMEM((words, n), bf16) for n in (hidden, three, features, features, features)]
    scratch += [pltpu.VMEM((5, words, features), bf16)] * 2
    scratch += [DMA((5, chunks))] * 4 + [DMA((count, 1))] * 4
    return pl.pallas_call(
        functools.partial(encoder_kernel, count, chunks, spacing),
        out_shape=(
            shape((words // count, features), bf16),
            shape((words, filters), f32),
            shape((2, 2, 2, rows, features + units), bf16),
            shape((2, 2, 2, rows, 1408), bf16),
            shape((16, features), f32),
            shape((1, three), f32),
        ),
        in_specs=[VMEM] * 11,
        out_specs=(VMEM,) * 6,
        scratch_shapes=scratch,
        compiler_params=params(cid, 58),
        name="encoder",
    )(top, *weights, vec, up_b, qkv_b, out_grad, live)


class LineScatter:
    def __init__(self, count, me, chunks, spacing, p_ref, out_ref, from_left, from_right, sems):
        self.count, self.me, self.chunks, self.spacing = count, me, chunks, spacing
        self.p_ref, self.out_ref = p_ref, out_ref
        self.from_left, self.from_right, self.sems = from_left, from_right, sems
        self.messages = chunks * (count - 1)
        self.steps = self.messages + spacing * (count - 1)

    def place(self, right, number):
        count, me = self.count, self.me
        lag = me if right else count - 1 - me
        chunk = number // (count - 1)
        far = count - 1 - number % (count - 1)
        block = far if right else count - 1 - far
        words, filters = self.out_ref.shape
        rows = words // self.chunks
        tile = pl.ds(pl.multiple_of(chunk * rows, rows), rows)
        lanes = pl.ds(pl.multiple_of(block * filters, filters), filters)
        buf = self.from_left if right else self.from_right
        send, recv = self.sems[:2] if right else self.sems[2:]
        to = jnp.minimum(me + 1, count - 1) if right else jnp.maximum(me - 1, 0)
        first, passed = [
            functools.partial(
                pltpu.make_async_remote_copy,
                src_ref=src.at[tile, lanes],
                dst_ref=buf.at[tile, lanes],
                send_sem=send.at[block, chunk],
                recv_sem=recv.at[block, chunk],
                device_id={"tensor": to},
                device_id_type=MESH,
            )
            for src in (self.p_ref, buf)
        ]
        return lag, far, tile, lanes, buf, first, passed

    def step(self, step):
        for right in (True, False):
            lag = self.me if right else self.count - 1 - self.me
            number = step - self.spacing * lag
            here = (number >= 0) & (number < self.messages)
            number = jnp.clip(number, 0, self.messages - 1)
            lag, far, tile, lanes, buf, first, passed = self.place(right, number)

            @pl.when(here & (lag == 0))
            def start():
                first().start()

            @pl.when(here & (lag > 0) & (far > lag))
            def middle():
                first().wait_recv()
                buf[tile, lanes] = (
                    buf[tile, lanes].astype(f32) + self.p_ref[tile, lanes].astype(f32)
                ).astype(bf16)
                passed().start()

            @pl.when(here & (lag > 0) & (far == lag))
            def last():
                first().wait_recv()
                self.out_ref[tile, :] += buf[tile, lanes].astype(f32)

    def due(self, chunk):
        return (chunk + self.spacing) * (self.count - 1)

    def finished(self, step, work, after=0):
        each = self.count - 1
        since = step - after - self.spacing * each

        @pl.when((since >= 0) & (since % each == 0) & (since < self.messages))
        def call():
            work(jnp.maximum(since, 0) // each)

    def drain(self):
        def one(number, carry):
            for right in (True, False):
                lag, far, tile, lanes, buf, first, passed = self.place(right, number)

                @pl.when(far > lag)
                def sent():
                    first().wait_send()

            return carry

        lax.fori_loop(0, self.messages, one, 0)


class DpSum:
    def __init__(self, cell, peers, x_first, sems, base):
        self.c, self.x, self.y = cell
        self.peers, self.x_first, self.base = peers, x_first, base
        self.send, self.recv = sems
        self.src = self.half = self.in0 = self.in1 = self.mid = self.in2 = None

    def remote(self, number, src, dst, bit):
        return pltpu.make_async_remote_copy(
            src_ref=src,
            dst_ref=dst,
            send_sem=self.send.at[self.base + number],
            recv_sem=self.recv.at[self.base + number],
            device_id=self.peers[bit],
            device_id_type=MESH,
        )

    def copy0(self):
        return self.remote(0, self.src.at[:, :, 1 - self.c], self.in0, 0)

    def copy1(self):
        if self.x_first:
            return self.remote(1, self.half.at[:, 1 - self.x], self.in1, 1)
        return self.remote(1, self.half.at[1 - self.y], self.in1, 2)

    def copy2(self):
        own = self.y if self.x_first else self.x
        return self.remote(2, self.mid.at[1 - own], self.in2, 2 if self.x_first else 1)

    def finish0(self):
        self.copy0().wait()

        def one(k, carry):
            i, j = k // 2, k % 2
            self.half[i, j] = (self.half[i, j].astype(f32) + self.in0[i, j].astype(f32)).astype(bf16)
            return carry

        lax.fori_loop(0, 4, one, 0)

    def finish1(self):
        self.copy1().wait()

        def one(k, carry):
            kept = self.half[k, self.x] if self.x_first else self.half[self.y, k]
            self.mid[k] = (kept.astype(f32) + self.in1[k].astype(f32)).astype(bf16)
            return carry

        lax.fori_loop(0, 2, one, 0)

    def finish2(self):
        self.copy2().wait()
        own = self.y if self.x_first else self.x
        return self.mid[own].astype(f32) + self.in2[...].astype(f32)


def dp_cell(place):
    cell = [place % 2, (place // 2) % 2, place // 4]
    return cell, [{"dp": place + (1 - 2 * cell[bit]) * 2**bit} for bit in range(3)]


def greet_all(peers):
    barrier = pltpu.get_barrier_semaphore()
    for peer in peers:
        pl.semaphore_signal(barrier, inc=1, device_id=peer, device_id_type=MESH)
    pl.semaphore_wait(barrier, len(peers))


def mix_back(d_hidden, trans, gate_pre, previous):
    gate = jax.nn.sigmoid(gate_pre)
    sig = jax.nn.sigmoid(trans)
    act = trans * sig
    d_trans = (d_hidden * gate * (sig * (1.0 + trans * (1.0 - sig)))).astype(bf16)
    d_gate = (d_hidden * (act - previous) * gate * (1.0 - gate)).astype(bf16)
    return d_trans, d_gate, (1.0 - gate) * d_hidden


def weight_grad_piece(piece, whole_ref, d_refs, outs):
    rows = outs[0].shape[-2]
    lanes = pl.ds(pl.multiple_of(piece * rows, rows), rows)
    index = (piece // 4, (piece // 2) % 2, piece % 2)
    for d_ref, out in zip(d_refs, outs):
        out[index] = dot(whole_ref[:, lanes], d_ref[...], 0, 0).astype(bf16)


def highway_back_kernel(count, chunks, reduce, *refs):
    d_h2_ref, t1_ref, g1_ref, h1_ref = refs[:4]
    late_hbm = refs[4:9]
    refs = refs[9:]
    if reduce:
        tr_hbm = refs[:2]
        refs = refs[2:]
    part0_ref, prev0_ref, dt0_ref, dg0_ref, sums_ref = refs[:5]
    refs = refs[5:]
    if reduce:
        mids = refs[:4]
        hw_refs, tr_half = refs[4:6], refs[6:8]
        in0s, in1s = refs[8:12], refs[12:16]
        dp_sems = refs[16:18]
        refs = refs[18:]
    else:
        hw_refs = refs[:2]
        refs = refs[2:]
    part1_ref, from_left, from_right, d_h1_ref, dt1_ref, dg1_ref = refs[:6]
    t0_ref, g0_ref, h0_ref, whole1_ref, w_ref, late_sem = refs[6:12]
    sems = refs[12:]
    me = lax.axis_index("tensor")
    words, filters = d_h2_ref.shape
    w_hbm = late_hbm[4]
    loads = [
        pltpu.make_async_copy(w_hbm.at[1], w_ref.at[1], late_sem.at[0]),
        pltpu.make_async_copy(late_hbm[3], whole1_ref, late_sem.at[1]),
        pltpu.make_async_copy(w_hbm.at[0], w_ref.at[0], late_sem.at[2]),
        pltpu.make_async_copy(late_hbm[0], t0_ref, late_sem.at[3]),
        pltpu.make_async_copy(late_hbm[1], g0_ref, late_sem.at[4]),
        pltpu.make_async_copy(late_hbm[2], h0_ref, late_sem.at[5]),
    ]
    for copy in loads:
        copy.start()
    items = []
    if reduce:
        cell, peers = dp_cell(lax.axis_index("dp"))
        keep = [
            pltpu.make_async_copy(tr_hbm[k].at[:, :, cell[0]], tr_half[k], late_sem.at[6 + k])
            for k in range(2)
        ]
        for copy in keep:
            copy.start()
    ring = [{"tensor": lax.rem(me + k, count)} for k in range(1, count)]
    sums_ref[...] = jnp.zeros_like(sums_ref)

    def mix(layer, d_h_ref, t_ref, g_ref, h_ref, dt_ref, dg_ref, prev_ref, tile):
        dt, dg, prev = mix_back(d_h_ref[tile, :], t_ref[tile, :], g_ref[tile, :], h_ref[tile, :])
        dt_ref[tile, :] = dt
        dg_ref[tile, :] = dg
        prev_ref[tile, :] = prev
        for j, d in enumerate((dt, dg)):
            sums_ref[2 * layer + j : 2 * layer + j + 1, :] += jnp.sum(
                d.astype(f32), axis=0, keepdims=True
            )

    def products(layer, dt_ref, dg_ref, p_ref, part):
        tile = slice(part * (words // 2), (part + 1) * (words // 2))

        def one(block, carry):
            lanes = pl.ds(pl.multiple_of(block * filters, filters), filters)
            p_ref[tile, lanes] = (
                dot(dt_ref[tile, :], w_ref[layer, 0, lanes, :], 1, 1)
                + dot(dg_ref[tile, :], w_ref[layer, 1, lanes, :], 1, 1)
            ).astype(bf16)
            return carry

        lax.fori_loop(0, count, one, 0)

    rows = words // chunks

    def tile_of(index):
        return pl.ds(pl.multiple_of(index * rows, rows), rows)

    def first(index, carry):
        mix(1, d_h2_ref, t1_ref, g1_ref, h1_ref, dt1_ref, dg1_ref, d_h1_ref, tile_of(index))
        return carry

    def own_part(part):
        tile = slice(part * (words // 2), (part + 1) * (words // 2))
        d_h1_ref[tile, :] += part1_ref[
            tile, pl.ds(pl.multiple_of(me * filters, filters), filters)
        ].astype(f32)

    lax.fori_loop(0, chunks, first, 0)
    loads[0].wait()
    products(1, dt1_ref, dg1_ref, part1_ref, 0)
    own_part(0)
    if reduce:
        greet_all(peers + ring)
        for k in range(4):
            item = DpSum(cell, peers, k % 2 == 0, dp_sems, 3 * k)
            if k < 2:
                item.src, item.half = hw_refs[k], hw_refs[k].at[:, :, cell[0]]
            else:
                item.src, item.half = tr_hbm[k - 2], tr_half[k - 2]
            item.in0, item.in1, item.mid = in0s[k], in1s[k], mids[k]
            items.append(item)
        for item in items[2:]:
            item.copy0().start()
    else:
        greet_all(ring)
    scatter = LineScatter(
        count, me, chunks, 3, part1_ref, d_h1_ref, from_left, from_right, sems
    )

    def step_fn(step, carry):
        scatter.step(step)

        @pl.when(step == 0)
        def rest():
            products(1, dt1_ref, dg1_ref, part1_ref, 1)
            own_part(1)
            loads[1].wait()

        @pl.when((step > 0) & (step <= 8))
        def grads():
            weight_grad_piece(step - 1, whole1_ref, (dt1_ref, dg1_ref), hw_refs)

        @pl.when(step == 9)
        def late():
            for copy in loads[2:]:
                copy.wait()

        if reduce:

            @pl.when(step == 9)
            def start0():
                for item in items[:2]:
                    item.copy0().start()
                for copy in keep:
                    copy.wait()
                for item in items[2:]:
                    item.finish0()
                    item.copy1().start()

            @pl.when(step == 15)
            def start1():
                for item in items[:2]:
                    item.finish0()
                    item.copy1().start()

        scatter.finished(
            step,
            lambda chunk: mix(
                0, d_h1_ref, t0_ref, g0_ref, h0_ref, dt0_ref, dg0_ref, prev0_ref, tile_of(chunk)
            ),
        )

        @pl.when(step == scatter.due(chunks // 2 - 1) + 1)
        def early():
            products(0, dt0_ref, dg0_ref, part0_ref, 0)

        return carry

    lax.fori_loop(0, scatter.steps, step_fn, 0)
    products(0, dt0_ref, dg0_ref, part0_ref, 1)
    for item in items:
        item.finish1()
    scatter.drain()


def highway_back(d_h2, t1, g1, h1, t0, g0, h0, whole1, weight, tra, trb, count, cid):
    words, filters = d_h2.shape
    chunks = 8
    reduce = tra is not None
    rows = whole1.shape[1] // 8
    shape = jax.ShapeDtypeStruct
    out_shape = [
        shape(whole1.shape, bf16),
        shape((words, filters), f32),
        shape((words, filters), bf16),
        shape((words, filters), bf16),
        shape((4, filters), f32),
    ]
    operands = [d_h2, t1, g1, h1, t0, g0, h0, whole1, weight]
    in_specs = [VMEM] * 4 + [ANY] * 5
    hw_shape = (2, 2, 2, rows, filters)
    scratch = []
    if reduce:
        operands += [tra, trb]
        in_specs += [ANY] * 2
        tails = [hw_shape[-2:], hw_shape[-2:], tra.shape[-2:], trb.shape[-2:]]
        out_shape += [shape((2,) + tail, bf16) for tail in tails]
        scratch += [pltpu.VMEM(hw_shape, bf16)] * 2
        scratch += [pltpu.VMEM((2, 2) + tail, bf16) for tail in tails[2:]]
        scratch += [pltpu.VMEM((2, 2) + tail, bf16) for tail in tails]
        scratch += [pltpu.VMEM((2,) + tail, bf16) for tail in tails]
        scratch += [DMA((12,))] * 2
    else:
        out_shape += [shape(hw_shape, bf16)] * 2
    scratch += [pltpu.VMEM(whole1.shape, bf16)] * 3
    scratch += [pltpu.VMEM((words, filters), f32)] + [pltpu.VMEM((words, filters), bf16)] * 2
    scratch += [pltpu.VMEM((words, filters), f32)] * 3
    scratch += [pltpu.VMEM(whole1.shape, bf16), pltpu.VMEM(weight.shape, bf16), DMA((8,))]
    scratch += [DMA((count, chunks))] * 4
    return pl.pallas_call(
        functools.partial(highway_back_kernel, count, chunks, reduce),
        out_shape=tuple(out_shape),
        in_specs=in_specs,
        out_specs=tuple([VMEM] * len(out_shape)),
        scratch_shapes=scratch,
        compiler_params=params(cid, 58),
        name="highway_back",
    )(*operands)


def spread_small(send_recv, in_ref, got, mid, out_ref):
    dp_count, count = out_ref.shape[:2]
    s1, r1, s2, r2, s3, r3 = send_recv
    me = lax.axis_index("tensor")
    place = lax.axis_index("dp")

    def remote(src, dst, send, recv, hop, axis, peer):
        return pltpu.make_async_remote_copy(
            src_ref=src, dst_ref=dst, send_sem=send.at[hop - 1], recv_sem=recv.at[hop - 1],
            device_id={axis: peer}, device_id_type=MESH,
        )

    def scatter(hop):
        peer = lax.rem(place + hop, dp_count)
        return remote(in_ref.at[peer], got.at[hop - 1], s1, r1, hop, "dp", peer)

    def across(hop):
        return remote(mid.at[me], mid.at[me], s2, r2, hop, "tensor", lax.rem(me + hop, count))

    def around(hop):
        return remote(mid, out_ref.at[place], s3, r3, hop, "dp", lax.rem(place + hop, dp_count))

    def loop(fn, stop):
        def one(hop, carry):
            fn(hop)
            return carry

        lax.fori_loop(1, stop, one, 0)

    loop(lambda hop: scatter(hop).start(), dp_count)
    loop(lambda hop: scatter(hop).wait(), dp_count)
    total = lax.fori_loop(0, dp_count - 1, lambda k, acc: acc + got[k], in_ref[place])
    mid[me] = total.astype(bf16)
    loop(lambda hop: across(hop).start(), count)
    loop(lambda hop: across(hop).wait(), count)
    loop(lambda hop: around(hop).start(), dp_count)
    out_ref[place] = mid[...]
    loop(lambda hop: around(hop).wait(), dp_count)


def conv_backward_kernel(count, chars, cuts, *refs):
    (ids_ref, x_hbm, p_hbm, wb_ref, off_ref, log_ref, prev_ref, part_ref, whole_hbm, dt_ref,
     dg_ref) = refs[:11]
    refs = refs[11:]
    if cuts:
        mids_in = refs[:4]
        mask_ref, early_ref = refs[4:6]
        hw_out, up_out, down_out, proj_out, qkv_out, o_out = refs[6:12]
        convw_out, convb_out, table_out, early_out = refs[12:16]
        dw_ref, table_ref, hw_a, hw_b = refs[16:20]
        in0s, in1s, mids, in2s = refs[20:22], refs[22:24], refs[24:26], refs[26:32]
        dp_sems = refs[32:34]
        small_ref, small_got, small_mid, small_all = refs[34:38]
        small_sems = refs[38:44]
        refs = refs[44:]
    else:
        dw_ref, table_ref, hw_a, hw_b = refs[:4]
        refs = refs[4:]
    pad_ref, grad_ref, from_left, from_right, x_buf, p_buf, whole_ref, load_sem, whole_sem = refs[:9]
    line_sems = refs[9:]
    me = lax.axis_index("tensor")
    words, filters = log_ref.shape
    tiles = words // WORD_TILE
    padded = ids_ref.shape[1] // WORD_TILE

    def load(index):
        slot = index % 2
        return [
            pltpu.make_async_copy(hbm.at[index], buf.at[slot], load_sem.at[k, slot])
            for k, (buf, hbm) in enumerate(((x_buf, x_hbm), (p_buf, p_hbm)))
        ]

    whole_copy = pltpu.make_async_copy(whole_hbm, whole_ref, whole_sem)
    whole_copy.start()
    for index in range(2):
        for copy in load(index):
            copy.start()
    ring = [{"tensor": lax.rem(me + k, count)} for k in range(1, count)]
    items = []
    if cuts:
        place = lax.axis_index("dp")
        dp_count = small_all.shape[0]
        cell, dp_peers = dp_cell(place)
        greet_all([{"dp": lax.rem(place + k, dp_count)} for k in range(1, dp_count)] + ring)
        for k in range(6):
            item = DpSum(cell, dp_peers, k % 2 == 0, dp_sems, 3 * k)
            item.in2 = in2s[k]
            if k < 2:
                item.src = (hw_a, hw_b)[k]
                item.half = item.src.at[:, :, cell[0]]
                item.in0, item.in1, item.mid = in0s[k], in1s[k], mids[k]
            else:
                item.mid = mids_in[k - 2]
            items.append(item)
        for item in items[2:]:
            item.copy2().start()
    else:
        greet_all(ring)

    dw_ref[...] = jnp.zeros_like(dw_ref)
    table_ref[...] = jnp.zeros_like(table_ref)
    pad_ref[...] = jnp.zeros_like(pad_ref)
    grad_ref[...] = prev_ref[...] + part_ref[
        :, pl.ds(pl.multiple_of(me * filters, filters), filters)
    ].astype(f32)
    chunks = line_sems[0].shape[1]
    per = words // chunks // WORD_TILE
    scatter = LineScatter(
        count, me, chunks, 3, part_ref, grad_ref, from_left, from_right, line_sems
    )
    group = lax.broadcasted_iota(jnp.int32, (1, WORD_TILE, LANES), 2) // 16
    vocab = lax.broadcasted_iota(jnp.int32, (table_ref.shape[0], padded * WORD_TILE), 0)

    def tile_step(index):
        slot = index % 2
        for copy in load(index):
            copy.wait()
        tile = pl.ds(pl.multiple_of(index * WORD_TILE, WORD_TILE), WORD_TILE)
        pooled = log_ref[tile, :] - off_ref[...]
        sig = jax.nn.sigmoid(pooled)
        grad = grad_ref[tile, :] * (sig * (1.0 + pooled * (1.0 - sig)))
        d_conv = (grad[None] * p_buf[slot].astype(f32)).astype(bf16)
        d_conv = d_conv.reshape(chars * WORD_TILE, filters)
        dw_ref[...] += dot(x_buf[slot], d_conv, 0, 0)
        d_win = dot(d_conv, wb_ref[...], 1, 1).astype(bf16)
        pad_ref[6 : 6 + chars] = d_win.reshape(chars, WORD_TILE, LANES)
        d_emb = pad_ref[6 : 6 + padded]
        for tap in range(1, 7):
            d_emb = jnp.where(group == tap, pad_ref[6 - tap : 6 - tap + padded], d_emb)
        one_hot = jnp.where(vocab == ids_ref[pl.ds(index, 1), :], 1.0, 0.0).astype(bf16)
        table_ref[...] += dot(one_hot, d_emb.reshape(padded * WORD_TILE, LANES), 1, 0)

        @pl.when(index + 2 < tiles)
        def more():
            for copy in load(index + 2):
                copy.start()

    def step_fn(step, carry):
        scatter.step(step)

        @pl.when(step == 0)
        def whole():
            whole_copy.wait()

        @pl.when(step < 8)
        def grads():
            weight_grad_piece(step, whole_ref, (dt_ref, dg_ref), (hw_a, hw_b))

        if cuts:

            @pl.when(step == 8)
            def start0():
                for item in items[:2]:
                    item.copy0().start()

            @pl.when(step == cuts[0])
            def start1():
                for item in items[:2]:
                    item.finish0()
                    item.copy1().start()

            @pl.when(step == cuts[1])
            def start2():
                for item in items[:2]:
                    item.finish1()
                    item.copy2().start()

        for k in range(per):
            scatter.finished(step, lambda chunk: tile_step(chunk * per + k), k)
        return carry

    lax.fori_loop(0, scatter.due(chunks - 1) + per, step_fn, 0)
    if cuts:
        for i in range(8):
            small_ref[i, :, 0:filters] = dw_ref[16 * i : 16 * i + 16, :]
            small_ref[i, :, filters : filters + 3 * LANES] = jnp.zeros((16, 3 * LANES), f32)
            for k in range(3):
                lane = filters + k * LANES
                small_ref[i, 0:11, lane : lane + LANES] = table_ref[
                    33 * i + 11 * k : 33 * i + 11 * k + 11, :
                ]
            small_ref[i, :, filters + 3 * LANES :] = early_ref[i]
        spread_small(small_sems, small_ref, small_got, small_mid, small_all)
        for t in range(count):
            lanes = slice(t * filters, (t + 1) * filters)
            for i in range(7):
                band = slice(16 * i, 16 * i + 16)
                convw_out[band, lanes] = small_all[i, t, :, 0:filters].astype(f32) * mask_ref[band, :]
            convb_out[:, lanes] = small_all[7, t, :, 0:filters].astype(f32)[0:1]
        for i in range(8):
            total = small_all[i, 0, :, filters : filters + 3 * LANES].astype(f32)
            for t in range(1, count):
                total += small_all[i, t, :, filters : filters + 3 * LANES].astype(f32)
            for k in range(3):
                table_out[33 * i + 11 * k : 33 * i + 11 * k + 11, :] = total[
                    0:11, k * LANES : (k + 1) * LANES
                ]
            for t in range(count):
                early_out[t, i] = small_all[i, t, :, filters + 3 * LANES :].astype(f32)
        for k in range(4):
            hw_out[k // 2, k % 2] = items[k].finish2()
        total = items[4].finish2()
        units = up_out.shape[1]
        up_out[...] = total[:, :units]
        down_out[...] = total[:, units:].T
        total = items[5].finish2()
        three = qkv_out.shape[1]
        proj_out[...] = total[:, :filters].T
        qkv_out[...] = total[:, filters : filters + three]
        o_out[...] = total[:, 1152 : 1152 + three // 3].T
    scatter.drain()


def conv_backward(ids, x, p, wb, off, logs, prev, part, whole, dt, dg, rest, count, cid):
    words, filters = logs.shape
    chars = p.shape[1]
    chunks = 8
    shape = jax.ShapeDtypeStruct
    hw_shape = (2, 2, 2, whole.shape[1] // 8, filters)
    operands = [ids, x, p, wb, off, logs, prev, part, whole, dt, dg]
    in_specs = [VMEM, ANY, ANY] + [VMEM] * 5 + [ANY, VMEM, VMEM]
    sums = [(LANES, filters), (264, LANES)]
    scratch = []
    cuts = None
    if rest:
        mids, mask, early, units, three = rest
        cuts = (14, 26)
        operands += list(mids) + [mask, early]
        in_specs += [VMEM] * 6
        own = [hw_shape[-2:]] * 2
        tails = own + [mid.shape[-2:] for mid in mids]
        rows = mids[2].shape[-2]
        out_shape = [
            shape((2, 2) + own[0], f32),
            shape((rows, units), f32),
            shape((mids[2].shape[-1] - units, rows), f32),
            shape((filters, rows), f32),
            shape((rows, three), f32),
            shape((three // 3, rows), f32),
            shape((112, count * filters), f32),
            shape((1, count * filters), f32),
            shape(sums[1], f32),
            shape((count,) + early.shape, f32),
        ]
        small = (16, filters + 4 * LANES)
        scratch += [pltpu.VMEM(tail, f32) for tail in sums]
        scratch += [pltpu.VMEM(hw_shape, bf16)] * 2
        scratch += [pltpu.VMEM((2, 2) + tail, bf16) for tail in own]
        scratch += [pltpu.VMEM((2,) + tail, bf16) for tail in own + own]
        scratch += [pltpu.VMEM(tail, bf16) for tail in tails]
        scratch += [DMA((18,))] * 2
        scratch += [
            pltpu.VMEM((8,) + small, f32),
            pltpu.VMEM((7,) + small, f32),
            pltpu.VMEM((count,) + small, bf16),
            pltpu.VMEM((8, count) + small, bf16),
        ]
        scratch += [DMA((7,))] * 2 + [DMA((count - 1,))] * 2 + [DMA((7,))] * 2
    else:
        out_shape = [shape(tail, f32) for tail in sums] + [shape(hw_shape, bf16)] * 2
    scratch += [
        pltpu.VMEM((68, WORD_TILE, LANES), bf16),
        pltpu.VMEM((words, filters), f32),
        pltpu.VMEM(part.shape, bf16),
        pltpu.VMEM(part.shape, bf16),
        pltpu.VMEM((2,) + x.shape[1:], bf16),
        pltpu.VMEM((2,) + p.shape[1:], bf16),
        pltpu.VMEM(whole.shape, bf16),
        DMA((2, 2)),
        DMA,
    ]
    scratch += [DMA((count, chunks))] * 4
    return pl.pallas_call(
        functools.partial(conv_backward_kernel, count, chars, cuts),
        out_shape=tuple(out_shape),
        in_specs=in_specs,
        out_specs=tuple([VMEM] * len(out_shape)),
        scratch_shapes=scratch,
        compiler_params=params(cid, 58),
        name="conv_backward",
    )(*operands)


def small_kernel(dp_count, count, in_ref, out_ref, got, mid, *sems):
    me = lax.axis_index("tensor")
    place = lax.axis_index("dp")
    barrier = pltpu.get_barrier_semaphore()

    def greet(hop, carry):
        peer = lax.rem(place + hop, dp_count)
        pl.semaphore_signal(barrier, inc=1, device_id={"dp": peer}, device_id_type=MESH)
        return carry

    lax.fori_loop(1, dp_count, greet, 0)
    for hop in range(1, count):
        pl.semaphore_signal(
            barrier, inc=1, device_id={"tensor": lax.rem(me + hop, count)}, device_id_type=MESH
        )
    pl.semaphore_wait(barrier, dp_count + count - 2)
    spread_small(sems, in_ref, got, mid, out_ref)


def sum_small(packed, dp_count, count, cid):
    shape = packed.shape[1:]
    return pl.pallas_call(
        functools.partial(small_kernel, dp_count, count),
        out_shape=jax.ShapeDtypeStruct((dp_count, count) + shape, bf16),
        in_specs=[VMEM],
        out_specs=VMEM,
        scratch_shapes=[
            pltpu.VMEM((dp_count - 1,) + shape, f32),
            pltpu.VMEM((count,) + shape, bf16),
            DMA((dp_count - 1,)),
            DMA((dp_count - 1,)),
            DMA((count - 1,)),
            DMA((count - 1,)),
            DMA((dp_count - 1,)),
            DMA((dp_count - 1,)),
        ],
        compiler_params=params(cid, 32),
        name="sum_small",
    )(packed)


def mm(spec, *operands):
    return jnp.einsum(spec, *operands, preferred_element_type=f32)


def body(
    char_ids,
    seq_lengths,
    char_table,
    conv_weight,
    conv_bias,
    highway_weight,
    highway_bias,
    proj_weight,
    proj_bias,
    norm_gain,
    norm_shift,
    qkv_weight,
    qv_bias,
    output_projection_weight,
    out_bias,
    up_weight,
    up_bias,
    down_weight,
    down_bias,
    out_grad,
):
    words, nseq, chars = char_ids.shape
    assert nseq == 1
    count = lax.axis_size("tensor")
    dp_count = lax.axis_size("dp")
    rank = lax.axis_index("tensor")
    vocab, char_dim = char_table.shape
    taps_dim, filters = conv_weight.shape
    features = proj_weight.shape[1]
    heads = qkv_weight.shape[2] // HEAD_DIM

    padded = chars + 6
    ids = jnp.pad(char_ids[:, 0], ((0, 0), (0, 6)), constant_values=-1)
    ids_tiles = jnp.swapaxes(ids.reshape(words // WORD_TILE, WORD_TILE, padded), 1, 2)
    ids_tiles = ids_tiles.reshape(words // WORD_TILE, padded * WORD_TILE)
    table_wide = jnp.pad(jnp.tile(char_table, (1, 7)), ((0, 0), (0, LANES - taps_dim)))
    one_hot = (ids.T[:, :, None] == lax.broadcasted_iota(jnp.int32, (1, 1, vocab), 2)).astype(bf16)
    pattern = np.zeros((padded, LANES), np.float32)
    pattern[:, taps_dim] = 1.0
    for k in range(1, 7):
        pattern[chars - k, taps_dim + k] = 1.0
    y = (mm("qwv,vl->qwl", one_hot, table_wide) + pattern[:, None, :]).astype(bf16)

    widths = filter_widths(filters)
    off = jnp.asarray(np.log((chars - widths + 1).astype(np.float64)).astype(np.float32))[None]
    tap_of = np.arange(taps_dim)[:, None] // char_dim
    w_taps = jnp.where(tap_of < widths[None], conv_weight, 0).astype(bf16)
    ends = np.where(widths[None] > np.arange(1, 7)[:, None], big_neg, 0.0).astype(np.float32)
    tail = LANES - taps_dim - 7
    w_all = jnp.concatenate(
        [w_taps, conv_bias[None], jnp.asarray(ends, bf16), jnp.zeros((tail, filters), bf16)], axis=0
    )
    w_back = jnp.pad(w_taps, ((0, LANES - taps_dim), (0, 0)))

    logs, whole, x_tiles, p_tiles = conv_forward(y, w_all, off, count, chars, 1)
    hidden = jax.nn.silu(logs - off)
    kept_layers = []
    for layer in range(highway_weight.shape[0]):
        if layer > 0:
            whole = gather_features(hidden.astype(bf16), count, 1 + layer)
        trans, gate_pre = [
            mm("rk,kf->rf", whole, highway_weight[layer, j]) + highway_bias[layer, j].astype(f32)
            for j in range(2)
        ]
        kept_layers.append((hidden, whole, trans, gate_pre))
        gate = jax.nn.sigmoid(gate_pre)
        hidden = gate * jax.nn.silu(trans) + (1.0 - gate) * hidden
    vec = jnp.concatenate(
        [jnp.stack([proj_bias, out_bias, down_bias]), norm_gain, norm_shift], axis=0
    ).astype(f32)
    qkv_b = jnp.stack([qv_bias[0], jnp.zeros_like(qv_bias[0]), qv_bias[1]]).reshape(1, -1)
    place = lax.broadcasted_iota(jnp.int32, (1, words), 1)
    live = jnp.where(place < seq_lengths[0], 1.0, 0.0).astype(f32)
    encoded, d_hidden, tr_a, tr_b, row_sums, proj_sums = encoder(
        hidden.astype(bf16),
        (
            proj_weight,
            qkv_weight.reshape(features, -1),
            output_projection_weight,
            up_weight,
            down_weight,
        ),
        jnp.pad(vec, ((0, 7), (0, 0))),
        up_bias.astype(f32)[None],
        qkv_b.astype(f32),
        out_grad[:, 0],
        live,
        count,
        4,
    )
    encoded = encoded[:, None]

    (h0, whole0, t0, g0), (h1, whole1, t1, g1) = kept_layers
    back_args = (d_hidden, t1, g1, h1, t0, g0, h0, whole1, highway_weight)
    conv_args = (ids_tiles, x_tiles, p_tiles, w_back, off, logs)
    taps_mask = tap_of < widths[None]
    three = 3 * heads * HEAD_DIM
    if dp_count == 8 and (features // dp_count) % 16 == 0:
        part0, prev0, dt0, dg0, hw_bias_part, *mids = highway_back(
            *back_args, tr_a, tr_b, count, 9
        )
        early = jnp.concatenate(
            [part.reshape(-1) for part in (hw_bias_part, proj_sums, row_sums[:10])]
        )
        early = jnp.pad(early, (0, 8 * 16 * LANES - early.size)).reshape(8, 16, LANES)
        (hw_w_grad, up_w_grad, down_w_grad, proj_w_grad, qkv_w_grad, out_w_grad, conv_w_grad,
         conv_b_grad, table_all, early) = conv_backward(
            *conv_args, prev0, part0, whole0, dt0, dg0,
            (mids, jnp.asarray(taps_mask, f32), early, up_weight.shape[1], three), count, 10,
        )
        conv_b_grad = conv_b_grad[0]
        early = early.reshape(count, -1)
    else:
        part0, prev0, dt0, dg0, hw_bias_part, *hw1 = highway_back(*back_args, None, None, count, 9)
        d_w_all, table_all, *hw0 = conv_backward(
            *conv_args, prev0, part0, whole0, dt0, dg0, (), count, 10
        )
        hw_sum = jnp.stack([part.reshape(-1, filters) for part in hw0 + hw1])
        hw_sum = lax.psum_scatter(hw_sum, "dp", scatter_dimension=1, tiled=True).astype(f32)
        tr_a, tr_b = [
            lax.psum_scatter(
                part.reshape(features, -1), "dp", scatter_dimension=0, tiled=True
            ).astype(f32)
            for part in (tr_a, tr_b)
        ]
        hw_w_grad = hw_sum.reshape(2, 2, -1, filters)
        units = up_weight.shape[1]
        up_w_grad = tr_a[:, :units]
        down_w_grad = tr_a[:, units:].T
        proj_w_grad = tr_b[:, :filters].T
        qkv_w_grad = tr_b[:, filters : filters + three]
        out_w_grad = tr_b[:, 1152 : 1152 + heads * HEAD_DIM].T
        pieces = [d_w_all[: taps_dim + 1], table_all, hw_bias_part, proj_sums, row_sums[:10]]
        flat = jnp.concatenate([part.reshape(-1) for part in pieces])
        width = -(-flat.size // (dp_count * 16 * LANES)) * LANES
        flat = jnp.pad(flat, (0, dp_count * 16 * width - flat.size))
        summed = sum_small(flat.reshape(dp_count, 16, width), dp_count, count, 11)
        summed = jnp.swapaxes(summed, 0, 1).reshape(count, -1).astype(f32)
        conv_size, table_size = pieces[0].size, table_all.size
        conv_all = summed[:, :conv_size].reshape(count, taps_dim + 1, filters)
        conv_all = jnp.swapaxes(conv_all, 0, 1)
        conv_w_grad = jnp.where(taps_mask[:, None], conv_all[:taps_dim], 0.0)
        conv_w_grad = conv_w_grad.reshape(taps_dim, -1)
        conv_b_grad = conv_all[taps_dim].reshape(-1)
        table_all = jnp.sum(summed[:, conv_size : conv_size + table_size], axis=0)
        table_all = table_all.reshape(-1, LANES)
        early = summed[:, conv_size + table_size :]

    qkv_w_grad = qkv_w_grad.reshape(-1, 3, heads * HEAD_DIM)
    table_grad = jnp.sum(
        table_all[:vocab, :taps_dim].reshape(vocab, taps_dim // char_dim, char_dim), axis=1
    )
    hw_b_grad = jnp.swapaxes(early[:, : 4 * filters].reshape(count, 4, filters), 0, 1)
    hw_b_grad = hw_b_grad.reshape(2, 2, -1)
    early = early[:, 4 * filters :]
    qv_grad = jnp.swapaxes(early[:, :three].reshape(count, 3, -1), 0, 1)[::2].reshape(2, -1)
    rows = early[:, three : three + 10 * features].reshape(count, 10, features)
    proj_b_grad, out_b_grad, down_b_grad = rows[0, 0], rows[0, 1], rows[0, 2]
    gain_grad = rows[0, 3:6]
    shift_grad = rows[0, 6:9]
    up_b_grad = rows[:, 9].reshape(-1)
    return (
        encoded,
        table_grad,
        conv_w_grad,
        conv_b_grad,
        hw_w_grad,
        hw_b_grad,
        proj_w_grad,
        proj_b_grad,
        gain_grad,
        shift_grad,
        qkv_w_grad,
        qv_grad,
        out_w_grad,
        out_b_grad,
        up_w_grad,
        up_b_grad,
        down_w_grad,
        down_b_grad,
    )


def solution(mesh):
    return jax.shard_map(
        body,
        mesh=mesh,
        in_specs=(
            P(None, "dp", None),
            P("dp"),
            P(),
            P(None, "tensor"),
            P("tensor"),
            P(None, None, None, "tensor"),
            P(None, None, "tensor"),
            P("tensor", None),
            P(),
            P(),
            P(),
            P(None, None, "tensor"),
            P(None, "tensor"),
            P("tensor", None),
            P(),
            P(None, "tensor"),
            P("tensor"),
            P("tensor", None),
            P(),
            P("tensor", "dp", None),
        ),
        out_specs=(
            P("tensor", "dp", None),
            P(),
            P(),
            P(),
            P(None, None, "dp", "tensor"),
            P(),
            P("tensor", "dp"),
            P(),
            P(),
            P(),
            P("dp", None, "tensor"),
            P(),
            P("tensor", "dp"),
            P(),
            P("dp", "tensor"),
            P(),
            P("tensor", "dp"),
            P(),
        ),
        check_vma=False,
    )
```

time: 506 us -> 451 us (0.89); the launches traced: 498 us -> 450 us
  Pallas kernels: 354 us -> 390 us
  matrix products: 50.2 us -> 24.9 us
  other arithmetic: 29.7 us -> 5.01 us
  blocking collectives: 18 us -> 0 us
  local copies, waits for them, and re-layouts: 42.6 us -> 29.3 us
    pallas_call x7 -> x2, Pallas kernels: 193 us -> 227 us  [the longest x1 145 us: encoder(): pl.pallas_call(functools.partial(encoder_kernel, count, chunks, spacing),...]
    dot_general x24 -> x5, matrix products: 44.7 us -> 24.9 us  [mm(): return jnp.einsum(spec, *operands, preferred_element_type=f32)]
    all_gather x1 -> x0, blocking collectives: 18 us -> none  [body(): lax.all_gather(out_grad[:, 0], 'tensor', axis=0, tiled=True).astype(f32)]
    reduce_sum x20 -> x0, other arithmetic: 14.2 us -> none  [the longest x5 7.26 us: layer_norm(): return centered * lax.rsqrt(variance + norm_eps) * gain + shift]
    concatenate x4 -> x2, local copies, waits for them, and re-layouts: 11 us -> 1.62 us  [the longest x1 1.53 us: body(): jnp.concatenate([jnp.stack([proj_bias, out_bias, down_bias]), norm_gain,...]
    convert_element_type x8 -> x1, other arithmetic: 6.84 us -> 0.07 us  [body(): qkv_b.astype(f32)]
    pallas_call x1, Pallas kernels: 87.3 us -> 80.7 us  [highway_back(): pl.pallas_call(functools.partial(highway_back_kernel, count, chunks, redu...]
    pallas_call x1, Pallas kernels: 40.8 us -> 46 us  [conv_forward(): pl.pallas_call(functools.partial(conv_forward_kernel, count, chars, chunk...]
where the time goes in v3:
time: 451 us; the launch traced here: 450 us
  Pallas kernels  390 us (86%)
  local copies, waits for them, and re-layouts  29.3 us (6%)
  matrix products  24.9 us (6%)
  other arithmetic  5.01 us (1%)
    pallas_call x1, Pallas kernels, encoder(): pl.pallas_call(functools.partial(encoder_kernel, count, chunks, spacing),...  145 us
    pallas_call x1, Pallas kernels, conv_backward(): pl.pallas_call(functools.partial(conv_backward_kernel, count, chars, cuts...  82.7 us
    pallas_call x1, Pallas kernels, highway_back(): pl.pallas_call(functools.partial(highway_back_kernel, count, chunks, redu...  80.7 us
    pallas_call x1, Pallas kernels, conv_forward(): pl.pallas_call(functools.partial(conv_forward_kernel, count, chars, chunk...  46 us
    pallas_call x1, Pallas kernels, gather_features(): pl.pallas_call(functools.partial(gather_kernel, count, chunks), out_shape...  35.4 us
    dot_general x5, matrix products, mm(): return jnp.einsum(spec, *operands, preferred_element_type=f32)  24.9 us
    unnamed x52, local copies, waits for them, and re-layouts  13.4 us

profile of v3, /device:TPU:1, one launch (start us, length us, event | category | flops | bytes accessed | tf_op | source)
XLA Modules:
  0.0 450.4 jit_solution(3249300448012189124)
XLA Ops:
  1.5 0.6 compare_select_fusion.refs_10_
  2.1 0.7 broadcast_in_dim.35
  2.8 0.8 fusion.32
  3.6 0.7 reshape.162.refs_8_
  4.3 0.7 stack.12
  5.0 0.7 stack.13
  5.7 1.3 reshape.161.refs_7_
  6.9 0.7 stack.14
  7.6 0.8 slice_convert_fusion.1
  8.4 1.5 concatenate.10
  9.9 0.6 pad_convert_fusion.refs_6_
  10.6 0.7 tile.4
  11.4 1.0 broadcast_select_fusion
  12.4 1.4 fusion.31
  13.7 1.0 copy.62
  14.9 0.2 copy.66
  15.1 0.8 reshape.144.refs_0_
  15.9 1.3 copy.65.refs_2_
  17.3 13.8 %add_convert_fusion.y_ref = bf16[56,512,128]{2,1,0:T(8,128)(2,1)} fusion(s32[56,512]{1,0:T(8,128)S(1)} %copy.63, f32[56,128]{1,0:T(8,128)S(1)} %copy-done.16, bf16[262,112]{1,0:T(8,128)(2,1)S(1)} %copy.64), kind=kOutput, calls=%fused_computation.3 | convolution fusion | flops 1937940480 | bytes 7542080 | tf_op jit(solution)/shard_map/qwv,vl->qwl/dot_general | solution.py:1290
  31.1 46.0 %conv_forward.1 = (f32[512,512]{1,0:T(8,128)S(1)}, bf16[512,2048]{1,0:T(8,128)(2,1)S(1)}, bf16[16,1600,128]{2,1,0:T(8,128)(2,1)}, bf16[16,50,32,512]{3,2,1,0:T(8,128)(2,1)}) custom-call(bf16[56,512,128]{2,1,0:T(8,128)(2,1)} %add_convert_fusion.y_ref, bf16[128,512]{1,0:T(8,128)(2,1)S(1)} %get-tuple-element.141.w_ref, f32[1,512]{1,0:T(1,128)S(1)} %copy-done.3), custom_call_target="tpu_custom_call" | custom-call | tf_op jit(solution)/shard_map/conv_forward/pallas_call | solution.py:192
  77.2 4.0 fusion.14.refs_5_
  81.3 3.1 fusion.29
  84.4 35.4 %gather_features.1.refs_7_ = bf16[512,2048]{1,0:T(8,128)(2,1)S(1)} custom-call(bf16[512,512]{1,0:T(8,128)(2,1)S(1)} %get-tuple-element.133.x_ref), custom_call_target="tpu_custom_call" | custom-call | tf_op jit(solution)/shard_map/gather_features/pallas_call | solution.py:236
  119.8 1.2 fusion.20.refs_2_
  121.1 2.7 add_convert_fusion.1
  123.8 144.8 %encoder.1 = (bf16[128,768]{1,0:T(8,128)(2,1)}, f32[512,512]{1,0:T(8,128)}, bf16[2,2,2,96,1536]{4,3,2,1,0:T(8,128)(2,1)}, bf16[2,2,2,96,1408]{4,3,2,1,0:T(8,128)...) custom-call(bf16[512,512]{1,0:T(8,128)(2,1)} %get-tuple-element.149.refs_0_, bf16[512,768]{1,0:T(8,128)(2,1)} %refs_1_.1, ...), custom_call_target="tpu_custom_call" | custom-call | tf_op jit(solution)/shard_map/encoder/pallas_call | solution.py:571
  268.6 80.7 %highway_back.1 = (bf16[512,2048]{1,0:T(8,128)(2,1)}, f32[512,512]{1,0:T(8,128)}, bf16[512,512]{1,0:T(8,128)(2,1)}, bf16[512,512]{1,0:T(8,128)(2,1)}, f32[4,512]...) custom-call(f32[512,512]{1,0:T(8,128)} %get-tuple-element.52.refs_0_, ...), custom_call_target="tpu_custom_call" | custom-call | tf_op jit(solution)/shard_map/highway_back/pallas_call | solution.py:954
  349.3 0.7 copy.74
  350.1 0.6 pad.27
  350.8 82.7 %conv_backward.1 = (f32[2,2,256,512]{3,2,1,0:T(8,128)}, f32[96,768]{1,0:T(8,128)}, f32[768,96]{1,0:T(8,128)}, f32[512,96]{1,0:T(8,128)}, f32[96,576]{1,0:T(8,128...) custom-call(s32[16,1792]{1,0:T(8,128)} %reshape.144.refs_0_, ...), custom_call_target="tpu_custom_call" | custom-call | tf_op jit(solution)/shard_map/conv_backward/pallas_call | solution.py:1237
  433.5 1.1 copy.67
  434.5 0.6 reduce_sum.9
  435.2 1.8 copy.71
  437.0 1.1 copy.77
  438.3 0.7 reshape.156
  439.1 0.7 reshape.152
  439.8 0.6 slice.98
  440.4 0.6 slice_reduce_fusion
  441.1 0.6 slice_bitcast_fusion
  441.7 0.1 copy.69
  441.8 0.9 copy.72
  442.7 1.9 copy.73
  444.6 1.6 copy.85
  446.2 0.9 copy.86
  447.1 0.6 copy.87
  447.7 1.3 copy.88
  449.0 0.6 copy.89
  449.7 0.7 copy.90
  (58 shorter events, 1.1 us)
Async XLA Ops:
  0.7 15.3 %copy-start.9 = (bf16[768,3,192]{0,2,1:T(8,128)(2,1)S(1)}, bf16[768,3,192]{0,2,1:T(8,128)(2,1)}, u32[]{:S(2)}) copy-start(bf16[768,3,192]{0,2,1:T(8,128)(2,1)} %param.36) | copy-start | bytes 2654212
  14.7 2.5 copy-start.16
  17.3 13.8 %copy-start.3 = (f32[1,512]{1,0:T(1,128)S(1)}, f32[1,512]{1,0:T(1,128)}, u32[]{:S(2)}) copy-start(f32[1,512]{1,0:T(1,128)} %constant.47.off_ref.refs_4_) | copy-start | bytes 6148
  31.1 50.1 %slice-start = ((s8[8388608]{0:T(1024)(128)(4,1)}), s8[4194304]{0:T(1024)(128)(4,1)S(1)}, s32[]{:S(2)}) async-start(s8[8388608]{0:T(1024)(128)(4,1)} %bitcast.70), calls=%async_computation | async-start | bytes 8388608
  77.1 4.1 copy-start.1
  77.2 4.1 copy-start.2
  77.2 4.1 slice-start.1
  77.2 4.1 copy-start.17
  81.3 3.2 copy-start.5
  84.4 36.7 %copy-start.6 = (f32[512,512]{1,0:T(8,128)}, f32[512,512]{1,0:T(8,128)S(1)}, u32[]{:S(2)}) copy-start(f32[512,512]{1,0:T(8,128)S(1)} %get-tuple-element.134.refs_3_) | copy-start | bytes 3145732
  119.8 1.3 copy-start
  121.1 2.7 copy-start.7
  268.6 80.7 %copy-start.15 = (f32[1,576]{1,0:T(1,128)S(1)}, f32[1,576]{1,0:T(1,128)}, u32[]{:S(2)}) copy-start(f32[1,576]{1,0:T(1,128)} %get-tuple-element.64) | copy-start | bytes 6916
  268.6 81.4 %copy-start.13 = (f32[16,768]{1,0:T(8,128)S(1)}, f32[16,768]{1,0:T(8,128)}, u32[]{:S(2)}) copy-start(f32[16,768]{1,0:T(8,128)} %get-tuple-element.65) | copy-start | bytes 147460
  433.5 8.2 %copy-start.11 = (f32[96,576]{1,0:T(8,128)S(1)}, f32[96,576]{1,0:T(8,128)}, u32[]{:S(2)}) copy-start(f32[96,576]{1,0:T(8,128)} %get-tuple-element.72) | copy-start | bytes 663556
  435.2 11.0 %copy-start.8 = (f32[112,2048]{1,0:T(8,128)S(1)}, f32[112,2048]{1,0:T(8,128)}, u32[]{:S(2)}) copy-start(f32[112,2048]{1,0:T(8,128)} %get-tuple-element.171) | copy-start | bytes 2752516
  439.8 7.9 %copy-start.4 = (f32[2,2,256,512]{3,2,1,0:T(8,128)S(1)}, f32[2,2,256,512]{3,2,1,0:T(8,128)}, u32[]{:S(2)}) copy-start(f32[2,2,256,512]{3,2,1,0:T(8,128)} %get-tuple-element.173) | copy-start | bytes 6291460
  441.8 5.3 %copy-start.14 = (f32[1,2048]{1,0:T(1,128)S(1)}, f32[1,2048]{1,0:T(1,128)}, u32[]{:S(2)}) copy-start(f32[1,2048]{1,0:T(1,128)} %get-tuple-element.68) | copy-start | bytes 24580
  447.7 1.3 copy-start.12
  447.7 2.0 copy-start.10

commit v4 on v3

--- a/solution.py
+++ b/solution.py
@@ -111,28 +111,61 @@
     lax.fori_loop(0, chunks, one, 0)
 
 
-def windows(y_ref, start, chars):
-    group = lax.broadcasted_iota(jnp.int32, (1, WORD_TILE, LANES), 2) // 16
-    tile = pl.ds(start, WORD_TILE)
-    value = y_ref[0:chars, tile, :]
-    for tap in range(1, 7):
-        value = jnp.where(group == tap, y_ref[tap : chars + tap, tile, :], value)
-    return value.reshape(chars * WORD_TILE, LANES)
-
-
-def conv_forward_kernel(count, chars, chunks, y_ref, w_ref, off_ref, log_ref, whole_ref, x_hbm,
-                        p_hbm, x_buf, p_buf, keep_sem, *sems):
+FLAT_QV = 60
+FLAT_HIGHWAY = 63
+
+
+def flat_row(ref, start, blocks):
+    return jnp.concatenate(
+        [ref[start + k : start + k + 1, :] for k in range(blocks)], axis=1
+    ).astype(f32)
+
+
+def embed_forward_kernel(count, chars, *refs):
+    (ids_ref, chars_ref, pattern_ref, w_ref, off_ref, flat_ref, hw_hbm) = refs[:7]
+    log_ref, whole0_ref, whole1_ref, top_ref, x_hbm, p_hbm = refs[7:13]
+    kept = refs[13:19]
+    y_buf, x_buf, p_buf, hw_ref, table_ref, hb_ref, keep_sem, late_sem = refs[19:27]
+    bufs = refs[27:33]
+    sems0, sems1 = refs[33:37], refs[37:41]
+    t_refs, g_refs, h_refs = (bufs[0], bufs[3]), (bufs[1], bufs[4]), (bufs[2], bufs[5])
+    wholes = (whole0_ref, whole1_ref)
     me = lax.axis_index("tensor")
     words, filters = log_ref.shape
-    rows = words // chunks
     tiles = words // WORD_TILE
+    half = words // 2
+    padded = ids_ref.shape[1] // WORD_TILE
+    own = pl.ds(pl.multiple_of(me * filters, filters), filters)
+    loads = [
+        pltpu.make_async_copy(hw_hbm.at[layer], hw_ref.at[layer], late_sem.at[layer])
+        for layer in range(2)
+    ]
+    for copy in loads:
+        copy.start()
+    stores = [
+        pltpu.make_async_copy(buf, out, late_sem.at[2 + k])
+        for k, (buf, out) in enumerate(zip(bufs, kept))
+    ]
+    y_buf[...] = jnp.zeros_like(y_buf)
+    table_ref[...] = jnp.zeros_like(table_ref)
+    depth, vocab_size = chars_ref.shape
+    for tap in range(7):
+        table_ref[depth * tap : depth * tap + depth, 0:vocab_size] = chars_ref[...]
+    for k in range(4):
+        start = FLAT_HIGHWAY + k * (filters // LANES)
+        hb_ref[k : k + 1, :] = flat_row(flat_ref, start, filters // LANES)
     line_barrier(me, count)
 
-    def view(block, chunk):
-        return whole_ref.at[
-            pl.ds(pl.multiple_of(chunk * rows, rows), rows),
-            pl.ds(pl.multiple_of(block * filters, filters), filters),
-        ]
+    def view_of(whole):
+        def view(block, chunk):
+            return whole.at[
+                pl.ds(pl.multiple_of(chunk * WORD_TILE, WORD_TILE), WORD_TILE),
+                pl.ds(pl.multiple_of(block * filters, filters), filters),
+            ]
+
+        return view
+
+    views = [view_of(whole) for whole in wholes]
 
     def keep(index):
         slot = index % 2
@@ -141,7 +174,10 @@
             for k, (buf, hbm) in enumerate(((x_buf, x_hbm), (p_buf, p_hbm)))
         ]
 
-    def tile_step(index, carry):
+    group = lax.broadcasted_iota(jnp.int32, (1, WORD_TILE, LANES), 2) // 16
+    vocab = lax.broadcasted_iota(jnp.int32, (table_ref.shape[1], padded * WORD_TILE), 0)
+
+    def tile_step(index):
         slot = index % 2
 
         @pl.when(index >= 2)
@@ -149,8 +185,13 @@
             for copy in keep(index - 2):
                 copy.wait()
 
-        start = pl.multiple_of(index * WORD_TILE, WORD_TILE)
-        x2 = windows(y_ref, start, chars)
+        one_hot = jnp.where(vocab == ids_ref[pl.ds(index, 1), :], 1.0, 0.0).astype(bf16)
+        found = dot(table_ref[...], one_hot, 1, 0).astype(bf16).T
+        y_buf[0:padded] = found.reshape(padded, WORD_TILE, LANES)
+        value = jnp.where(group == 7, pattern_ref[...], y_buf[0:chars])
+        for tap in range(1, 7):
+            value = jnp.where(group == tap, y_buf[tap : chars + tap], value)
+        x2 = value.reshape(chars * WORD_TILE, LANES)
         x_buf[slot] = x2
         conv = dot(x2, w_ref[...], 1, 0).reshape(chars, WORD_TILE, filters)
         top = jnp.max(conv, axis=0)
@@ -159,89 +200,115 @@
         p_buf[slot] = (exps * (1.0 / sums)[None]).astype(bf16)
         for copy in keep(index):
             copy.start()
+        tile = pl.ds(pl.multiple_of(index * WORD_TILE, WORD_TILE), WORD_TILE)
         total = top + jnp.log(sums)
-        log_ref[pl.ds(start, WORD_TILE), :] = total
+        log_ref[tile, :] = total
         pooled = total - off_ref[...]
-        whole_ref[
-            pl.ds(start, WORD_TILE), pl.ds(pl.multiple_of(me * filters, filters), filters)
-        ] = (pooled * jax.nn.sigmoid(pooled)).astype(bf16)
+        hidden = pooled * jax.nn.sigmoid(pooled)
+        h_refs[0][tile, :] = hidden
+        whole0_ref[tile, own] = hidden.astype(bf16)
+
+    def layer_step(layer, part):
+        rows = slice(part * half, (part + 1) * half)
+        for j, out in enumerate((t_refs[layer], g_refs[layer])):
+            bias = hb_ref[2 * layer + j : 2 * layer + j + 1, :]
+            out[rows, :] = dot(wholes[layer][rows, :], hw_ref[layer, j], 1, 0) + bias
+
+        def mix(index, carry):
+            tile = pl.ds(pl.multiple_of(part * half + index * WORD_TILE, WORD_TILE), WORD_TILE)
+            trans = t_refs[layer][tile, :]
+            gate = jax.nn.sigmoid(g_refs[layer][tile, :])
+            hidden = gate * (trans * jax.nn.sigmoid(trans)) + (1.0 - gate) * h_refs[layer][tile, :]
+            if layer == 0:
+                h_refs[1][tile, :] = hidden
+                whole1_ref[tile, own] = hidden.astype(bf16)
+            else:
+                top_ref[tile, :] = hidden.astype(bf16)
+            return carry
+
+        lax.fori_loop(0, half // WORD_TILE, mix, 0)
+
+    shift = tiles // 2 + count - 1
+    last = shift + tiles + count - 1
+
+    def step_fn(step, carry):
+        @pl.when(step < tiles)
+        def convolve():
+            tile_step(step)
+
+        @pl.when(step < tiles + count - 1)
+        def first_gather():
+            gather_step(views[0], step, tiles, me, count, sems0)
+
+        @pl.when(step == shift)
+        def first_half():
+            loads[0].wait()
+            layer_step(0, 0)
+
+        @pl.when(step == shift + tiles // 2)
+        def second_half():
+            layer_step(0, 1)
+            for copy in stores[:3]:
+                copy.start()
+
+        @pl.when(step >= shift)
+        def second_gather():
+            gather_step(views[1], step - shift, tiles, me, count, sems1)
+
+        @pl.when(step == 2 * shift - 1)
+        def third_half():
+            loads[1].wait()
+            layer_step(1, 0)
+
         return carry
 
-    per = rows // WORD_TILE
-
-    def chunk_step(step, carry):
-        @pl.when(step < chunks)
-        def work():
-            lax.fori_loop(step * per, step * per + per, tile_step, 0)
-
-        gather_step(view, step, chunks, me, count, sems)
-        return carry
-
-    lax.fori_loop(0, chunks + count - 1, chunk_step, 0)
+    lax.fori_loop(0, last, step_fn, 0)
+    layer_step(1, 1)
+    for copy in stores[3:]:
+        copy.start()
     for index in (tiles - 2, tiles - 1):
         for copy in keep(index):
             copy.wait()
-    gather_drain(view, chunks, me, count, sems)
-
-
-def conv_forward(y, w, off, count, chars, cid):
-    words, filters = y.shape[1], w.shape[1]
-    chunks = 8
-    tiles = words // WORD_TILE
+    for sems, view in zip((sems0, sems1), views):
+        gather_drain(view, tiles, me, count, sems)
+    for copy in stores:
+        copy.wait()
+
+
+def embed_forward(ids, table, pattern, w, off, flat_vec, weight, count, chars, cid):
+    filters = w.shape[1]
+    tiles = ids.shape[0]
+    words = tiles * WORD_TILE
     shape = jax.ShapeDtypeStruct
+    flat = (words, filters)
     return pl.pallas_call(
-        functools.partial(conv_forward_kernel, count, chars, chunks),
+        functools.partial(embed_forward_kernel, count, chars),
         out_shape=(
-            shape((words, filters), f32),
+            shape(flat, f32),
             shape((words, count * filters), bf16),
+            shape((words, count * filters), bf16),
+            shape(flat, bf16),
             shape((tiles, chars * WORD_TILE, LANES), bf16),
             shape((tiles, chars, WORD_TILE, filters), bf16),
-        ),
-        in_specs=[VMEM] * 3,
-        out_specs=(VMEM, VMEM, ANY, ANY),
+        )
+        + (shape(flat, f32),) * 6,
+        in_specs=[VMEM] * 6 + [ANY],
+        out_specs=(VMEM,) * 4 + (ANY,) * 8,
         scratch_shapes=[
+            pltpu.VMEM((chars + 6, WORD_TILE, LANES), bf16),
             pltpu.VMEM((2, chars * WORD_TILE, LANES), bf16),
             pltpu.VMEM((2, chars, WORD_TILE, filters), bf16),
+            pltpu.VMEM(weight.shape, bf16),
+            pltpu.VMEM((LANES, 264), bf16),
+            pltpu.VMEM((8, filters), f32),
             DMA((2, 2)),
+            DMA((8,)),
         ]
-        + [DMA((count, chunks))] * 4,
-        compiler_params=params(cid, 50),
-        name="conv_forward",
-    )(y, w, off)
-
-
-def gather_kernel(count, chunks, x_ref, whole_ref, *sems):
-    me = lax.axis_index("tensor")
-    words, filters = x_ref.shape
-    rows = words // chunks
-    whole_ref[:, pl.ds(pl.multiple_of(me * filters, filters), filters)] = x_ref[...]
-    line_barrier(me, count)
-
-    def view(block, chunk):
-        return whole_ref.at[
-            pl.ds(pl.multiple_of(chunk * rows, rows), rows),
-            pl.ds(pl.multiple_of(block * filters, filters), filters),
-        ]
-
-    def chunk_step(step, carry):
-        gather_step(view, step, chunks, me, count, sems)
-        return carry
-
-    lax.fori_loop(0, chunks + count - 1, chunk_step, 0)
-    gather_drain(view, chunks, me, count, sems)
-
-
-def gather_features(x, count, cid):
-    chunks = 4
-    return pl.pallas_call(
-        functools.partial(gather_kernel, count, chunks),
-        out_shape=jax.ShapeDtypeStruct((x.shape[0], count * x.shape[1]), bf16),
-        in_specs=[VMEM],
-        out_specs=VMEM,
-        scratch_shapes=[DMA((count, chunks))] * 4,
-        compiler_params=params(cid, 16),
-        name="gather_features",
-    )(x)
+        + [pltpu.VMEM(flat, f32)] * 6
+        + [DMA((count, tiles))] * 8,
+        compiler_params=params(cid, 58),
+        name="embed_forward",
+    )(ids, table, pattern, w, off, flat_vec, weight)
 
 
 class LineSum:
@@ -355,9 +422,8 @@
 
 
 def encoder_kernel(count, chunks, spacing, *refs):
-    (top_ref, pw_ref, qw_ref, ow_ref, uw_ref, dw_ref, vec_ref, ub_ref, qb_ref, og_ref,
-     live_ref) = refs[:11]
-    enc_ref, dh2_ref, tra_ref, trb_ref, sums_ref, qsum_ref = refs[11:17]
+    top_ref, pw_ref, qw_ref, ow_ref, uw_ref, dw_ref, flat_ref, og_ref, len_ref = refs[:9]
+    enc_ref, dh2_ref, tra_ref, trb_ref, sums_ref, qsum_ref, vec_ref, qb_ref = refs[9:17]
     (emb, inp, midpre, mid, fin, slope, dmid, din, sent, sent_mid, act, d_two, d_up, d_branch,
      d_emb, qkv, attended, probs, d_heads, d_proj, part, grad_all, enc_all, from_left,
      from_right) = refs[17:42]
@@ -372,6 +438,15 @@
     grad_all[own_tile, :] = og_ref[...]
     sums_ref[...] = jnp.zeros_like(sums_ref)
     trb_ref[...] = jnp.zeros_like(trb_ref)
+    for k in range(10):
+        vec_ref[k : k + 1, :] = flat_row(flat_ref, k * (features // LANES), features // LANES)
+    ends = [flat_ref[FLAT_QV + k : FLAT_QV + k + 1, :].astype(f32) for k in range(3)]
+    qb_ref[...] = jnp.zeros_like(qb_ref)
+    qb_ref[:, 0:128] = ends[0]
+    qb_ref[:, 128:192] = ends[1][:, 0:64]
+    qb_ref[:, 384:448] = ends[1][:, 64:128]
+    qb_ref[:, 448:576] = ends[2]
+    live = lax.broadcasted_iota(jnp.int32, (1, words), 1) < len_ref[0]
     line_barrier(me, count)
 
     def line(number, out_ref):
@@ -431,7 +506,7 @@
     line(0, emb).run(first_norm)
 
     def project(tile):
-        qkv[tile, :] = (dot(sent[tile, :], qw_ref[...], 1, 0) + qb_ref[...]).astype(bf16)
+        qkv[tile, :] = (dot(sent[tile, :], qw_ref[...], 1, 1) + qb_ref[...]).astype(bf16)
 
     tiles(256, project)
 
@@ -443,7 +518,7 @@
 
         def attend(tile):
             scores = dot(qkv[tile, lanes], qkv[:, keys], 1, 1) * scale
-            scores = jnp.where(live_ref[...] > 0.0, scores, big_neg)
+            scores = jnp.where(live, scores, big_neg)
             exps = jnp.exp(scores - jnp.max(scores, axis=1, keepdims=True))
             value = exps / jnp.sum(exps, axis=1, keepdims=True)
             probs[head, tile, :] = value
@@ -466,7 +541,7 @@
     line(1, midpre).run(second_norm)
 
     def feed(tile):
-        value, back = gelu_parts(dot(sent_mid[tile, :], uw_ref[...], 1, 0) + ub_ref[...])
+        value, back = gelu_parts(dot(sent_mid[tile, :], uw_ref[...], 1, 0) + row(9))
         act[tile, :] = value.astype(bf16)
         slope[tile, :] = back
 
@@ -524,7 +599,7 @@
         d_scores = (weights * (d_probs - inner)).astype(bf16)
         d_proj[:, lanes] = (dot(d_scores, qkv[:, keys], 1, 0) * scale).astype(bf16)
         d_proj[:, keys] = (dot(d_scores, qkv[:, lanes], 0, 0) * scale).astype(bf16)
-    send_product(d_proj, qw_ref, 1, din)
+    send_product(d_proj, qw_ref, 0, din)
     qsum_ref[...] = column_sum(d_proj[...].astype(f32))
 
     def first_back(tile):
@@ -549,17 +624,17 @@
     gather_drain(gather_view, 1, me, count, gather_sems)
 
 
-def encoder(top, weights, vec, up_b, qkv_b, out_grad, live, count, cid):
+def encoder(top, weights, flat, out_grad, lengths, count, cid):
     words, filters = top.shape
     features = weights[0].shape[1]
-    three = weights[1].shape[1]
+    three = weights[1].shape[0]
     units = weights[3].shape[1]
     hidden = three // 3
     chunks, spacing = 16, 3
     shape = jax.ShapeDtypeStruct
     rows = features // 8
-    wide = [(words, features)]
-    scratch = [pltpu.VMEM((words, n), f32) for n in [features] * 5 + [units] + [features] * 2]
+    scratch = [pltpu.VMEM((16, features), f32), pltpu.VMEM((1, three), f32)]
+    scratch += [pltpu.VMEM((words, n), f32) for n in [features] * 5 + [units] + [features] * 2]
     scratch += [
         pltpu.VMEM((words, n), bf16)
         for n in (features, features, units, features, units, features, features, three, hidden)
@@ -578,12 +653,12 @@
             shape((16, features), f32),
             shape((1, three), f32),
         ),
-        in_specs=[VMEM] * 11,
+        in_specs=[VMEM] * 8 + [pl.BlockSpec(memory_space=pltpu.SMEM)],
         out_specs=(VMEM,) * 6,
         scratch_shapes=scratch,
         compiler_params=params(cid, 58),
         name="encoder",
-    )(top, *weights, vec, up_b, qkv_b, out_grad, live)
+    )(top, *weights, flat, out_grad, lengths)
 
 
 class LineScatter:
@@ -765,11 +840,12 @@
     part0_ref, prev0_ref, dt0_ref, dg0_ref, sums_ref = refs[:5]
     refs = refs[5:]
     if reduce:
-        mids = refs[:4]
+        tr_outs = refs[2:4]
         hw_refs, tr_half = refs[4:6], refs[6:8]
         in0s, in1s = refs[8:12], refs[12:16]
-        dp_sems = refs[16:18]
-        refs = refs[18:]
+        mids, in2s = list(refs[:2]) + list(refs[16:18]), refs[18:20]
+        dp_sems = refs[20:22]
+        refs = refs[22:]
     else:
         hw_refs = refs[:2]
         refs = refs[2:]
@@ -852,6 +928,8 @@
             else:
                 item.src, item.half = tr_hbm[k - 2], tr_half[k - 2]
             item.in0, item.in1, item.mid = in0s[k], in1s[k], mids[k]
+            if k >= 2:
+                item.in2 = in2s[k - 2]
             items.append(item)
         for item in items[2:]:
             item.copy0().start()
@@ -881,21 +959,30 @@
 
         if reduce:
 
-            @pl.when(step == 9)
-            def start0():
-                for item in items[:2]:
-                    item.copy0().start()
+            @pl.when(step == 4)
+            def encoder1():
                 for copy in keep:
                     copy.wait()
                 for item in items[2:]:
                     item.finish0()
                     item.copy1().start()
 
+            @pl.when(step == 9)
+            def highway0():
+                for item in items[:2]:
+                    item.copy0().start()
+
             @pl.when(step == 15)
-            def start1():
+            def highway1():
                 for item in items[:2]:
                     item.finish0()
                     item.copy1().start()
+
+            @pl.when(step == 20)
+            def encoder2():
+                for item in items[2:]:
+                    item.finish1()
+                    item.copy2().start()
 
         scatter.finished(
             step,
@@ -912,8 +999,10 @@
 
     lax.fori_loop(0, scatter.steps, step_fn, 0)
     products(0, dt0_ref, dg0_ref, part0_ref, 1)
-    for item in items:
+    for item in items[:2]:
         item.finish1()
+    for item, out in zip(items[2:], tr_outs if reduce else ()):
+        out[...] = item.finish2().astype(bf16)
     scatter.drain()
 
 
@@ -938,11 +1027,13 @@
         operands += [tra, trb]
         in_specs += [ANY] * 2
         tails = [hw_shape[-2:], hw_shape[-2:], tra.shape[-2:], trb.shape[-2:]]
-        out_shape += [shape((2,) + tail, bf16) for tail in tails]
+        out_shape += [shape((2,) + tail, bf16) for tail in tails[:2]]
+        out_shape += [shape(tail, bf16) for tail in tails[2:]]
         scratch += [pltpu.VMEM(hw_shape, bf16)] * 2
         scratch += [pltpu.VMEM((2, 2) + tail, bf16) for tail in tails[2:]]
         scratch += [pltpu.VMEM((2, 2) + tail, bf16) for tail in tails]
-        scratch += [pltpu.VMEM((2,) + tail, bf16) for tail in tails]
+        scratch += [pltpu.VMEM((2,) + tail, bf16) for tail in tails + tails[2:]]
+        scratch += [pltpu.VMEM(tail, bf16) for tail in tails[2:]]
         scratch += [DMA((12,))] * 2
     else:
         out_shape += [shape(hw_shape, bf16)] * 2
@@ -962,66 +1053,125 @@
     )(*operands)
 
 
-def spread_small(send_recv, in_ref, got, mid, out_ref):
-    dp_count, count = out_ref.shape[:2]
-    s1, r1, s2, r2, s3, r3 = send_recv
-    me = lax.axis_index("tensor")
-    place = lax.axis_index("dp")
-
-    def remote(src, dst, send, recv, hop, axis, peer):
+class Spread:
+    def __init__(self, sems, in_ref, got, mid, out_ref):
+        self.dp_count, self.count = out_ref.shape[:2]
+        self.sems, self.in_ref, self.got, self.mid, self.out_ref = sems, in_ref, got, mid, out_ref
+        self.me = lax.axis_index("tensor")
+        self.place = lax.axis_index("dp")
+
+    def remote(self, src, dst, phase, hop, axis, peer):
+        send, recv = self.sems[2 * phase : 2 * phase + 2]
         return pltpu.make_async_remote_copy(
             src_ref=src, dst_ref=dst, send_sem=send.at[hop - 1], recv_sem=recv.at[hop - 1],
             device_id={axis: peer}, device_id_type=MESH,
         )
 
-    def scatter(hop):
-        peer = lax.rem(place + hop, dp_count)
-        return remote(in_ref.at[peer], got.at[hop - 1], s1, r1, hop, "dp", peer)
-
-    def across(hop):
-        return remote(mid.at[me], mid.at[me], s2, r2, hop, "tensor", lax.rem(me + hop, count))
-
-    def around(hop):
-        return remote(mid, out_ref.at[place], s3, r3, hop, "dp", lax.rem(place + hop, dp_count))
-
-    def loop(fn, stop):
+    def scatter(self, hop):
+        peer = lax.rem(self.place + hop, self.dp_count)
+        return self.remote(self.in_ref.at[peer], self.got.at[hop - 1], 0, hop, "dp", peer)
+
+    def across(self, hop):
+        peer = lax.rem(self.me + hop, self.count)
+        return self.remote(self.mid.at[self.me], self.mid.at[self.me], 1, hop, "tensor", peer)
+
+    def around(self, hop):
+        peer = lax.rem(self.place + hop, self.dp_count)
+        return self.remote(self.mid, self.out_ref.at[self.place], 2, hop, "dp", peer)
+
+    def loop(self, fn, stop):
         def one(hop, carry):
             fn(hop)
             return carry
 
         lax.fori_loop(1, stop, one, 0)
 
-    loop(lambda hop: scatter(hop).start(), dp_count)
-    loop(lambda hop: scatter(hop).wait(), dp_count)
-    total = lax.fori_loop(0, dp_count - 1, lambda k, acc: acc + got[k], in_ref[place])
-    mid[me] = total.astype(bf16)
-    loop(lambda hop: across(hop).start(), count)
-    loop(lambda hop: across(hop).wait(), count)
-    loop(lambda hop: around(hop).start(), dp_count)
-    out_ref[place] = mid[...]
-    loop(lambda hop: around(hop).wait(), dp_count)
+    def first(self):
+        self.loop(lambda hop: self.scatter(hop).start(), self.dp_count)
+
+    def second(self):
+        self.loop(lambda hop: self.scatter(hop).wait(), self.dp_count)
+        total = lax.fori_loop(
+            0,
+            self.dp_count - 1,
+            lambda k, acc: acc + self.got[k].astype(f32),
+            self.in_ref[self.place].astype(f32),
+        )
+        self.mid[self.me] = total.astype(bf16)
+        self.loop(lambda hop: self.across(hop).start(), self.count)
+
+    def third(self):
+        self.loop(lambda hop: self.across(hop).wait(), self.count)
+        self.loop(lambda hop: self.around(hop).start(), self.dp_count)
+        self.out_ref[self.place] = self.mid[...]
+
+    def finish(self):
+        self.loop(lambda hop: self.around(hop).wait(), self.dp_count)
+
+
+def early_parts(rows):
+    start = 0
+    for source, (count, width) in enumerate(rows):
+        for block in range(-(-width // LANES)):
+            yield source, block, start, count, min(LANES, width - block * LANES)
+            start += count
+
+
+EARLY = ((4, 512), (1, 576), (10, 768))
+
+
+def pack_early(ref, *sources):
+    ref[...] = jnp.zeros_like(ref)
+    for source, block, start, count, width in early_parts(EARLY):
+        value = sources[source][0:count, block * LANES : block * LANES + width]
+        for k in range(count):
+            place = start + k
+            ref[place // 16, place % 16 : place % 16 + 1, 0:width] = value[k : k + 1]
+
+
+def unpack_early(ref, hwb_out, vec_out, upb_out, qv_out):
+    for t in range(ref.shape[1]):
+        for source, block, start, count, width in early_parts(EARLY):
+            for k in range(count):
+                place = start + k
+                row = ref[place // 16, t, :, :].astype(f32)[place % 16 : place % 16 + 1, 0:width]
+                lane = block * LANES
+                if source == 0:
+                    hwb_out[k : k + 1, t * 512 + lane : t * 512 + lane + width] = row
+                elif source == 2 and k == 9:
+                    upb_out[:, t * 768 + lane : t * 768 + lane + width] = row
+                elif source == 2 and t == 0:
+                    vec_out[k : k + 1, lane : lane + width] = row
+                elif source == 1:
+                    for out, low in ((0, 0), (1, 384)):
+                        left, right = max(lane, low), min(lane + width, low + 192)
+                        if left < right:
+                            place_at = t * 192 + left - low
+                            qv_out[out : out + 1, place_at : place_at + right - left] = row[
+                                :, left - lane : right - lane
+                            ]
 
 
 def conv_backward_kernel(count, chars, cuts, *refs):
-    (ids_ref, x_hbm, p_hbm, wb_ref, off_ref, log_ref, prev_ref, part_ref, whole_hbm, dt_ref,
+    (ids_ref, x_hbm, p_hbm, w_ref, off_ref, log_ref, prev_ref, part_ref, whole_hbm, dt_ref,
      dg_ref) = refs[:11]
     refs = refs[11:]
     if cuts:
-        mids_in = refs[:4]
-        mask_ref, early_ref = refs[4:6]
-        hw_out, up_out, down_out, proj_out, qkv_out, o_out = refs[6:12]
-        convw_out, convb_out, table_out, early_out = refs[12:16]
-        dw_ref, table_ref, hw_a, hw_b = refs[16:20]
-        in0s, in1s, mids, in2s = refs[20:22], refs[22:24], refs[24:26], refs[26:32]
-        dp_sems = refs[32:34]
-        small_ref, small_got, small_mid, small_all = refs[34:38]
-        small_sems = refs[38:44]
-        refs = refs[44:]
+        mids_in = refs[:2]
+        hb_sums, proj_sums, row_sums = refs[2:5]
+        hw_out, convw_out, convb_out, table_out, hwb_out, vec_out, upb_out, qv_out = refs[5:13]
+        dw_ref, table_ref, hw_a, hw_b = refs[13:17]
+        in0s, in1s, mids, in2s = refs[17:19], refs[19:21], refs[21:23], refs[23:27]
+        dp_sems = refs[27:29]
+        spreads = [Spread(refs[33 + 10 * k : 39 + 10 * k], *refs[29 + 10 * k : 33 + 10 * k])
+                   for k in range(2)]
+        refs = refs[49:]
     else:
         dw_ref, table_ref, hw_a, hw_b = refs[:4]
         refs = refs[4:]
-    pad_ref, grad_ref, from_left, from_right, x_buf, p_buf, whole_ref, load_sem, whole_sem = refs[:9]
-    line_sems = refs[9:]
+    (pad_ref, stage_ref, grad_ref, from_left, from_right, x_buf, p_buf, whole_ref, wb_ref,
+     load_sem, whole_sem) = refs[:11]
+    line_sems = refs[11:]
     me = lax.axis_index("tensor")
     words, filters = log_ref.shape
     tiles = words // WORD_TILE
@@ -1043,10 +1193,10 @@
     items = []
     if cuts:
         place = lax.axis_index("dp")
-        dp_count = small_all.shape[0]
+        dp_count = spreads[0].dp_count
         cell, dp_peers = dp_cell(place)
         greet_all([{"dp": lax.rem(place + k, dp_count)} for k in range(1, dp_count)] + ring)
-        for k in range(6):
+        for k in range(4):
             item = DpSum(cell, dp_peers, k % 2 == 0, dp_sems, 3 * k)
             item.in2 = in2s[k]
             if k < 2:
@@ -1058,9 +1208,13 @@
             items.append(item)
         for item in items[2:]:
             item.copy2().start()
+        pack_early(spreads[0].in_ref, hb_sums, proj_sums, row_sums)
+        spreads[0].first()
     else:
         greet_all(ring)
 
+    row_of = lax.broadcasted_iota(jnp.int32, w_ref.shape, 0)
+    wb_ref[...] = jnp.where(row_of < 112, w_ref[...].astype(f32), 0.0).astype(bf16)
     dw_ref[...] = jnp.zeros_like(dw_ref)
     table_ref[...] = jnp.zeros_like(table_ref)
     pad_ref[...] = jnp.zeros_like(pad_ref)
@@ -1112,6 +1266,14 @@
 
         if cuts:
 
+            @pl.when(step == 4)
+            def early2():
+                spreads[0].second()
+
+            @pl.when(step == 7)
+            def early3():
+                spreads[0].third()
+
             @pl.when(step == 8)
             def start0():
                 for item in items[:2]:
@@ -1135,101 +1297,96 @@
 
     lax.fori_loop(0, scatter.due(chunks - 1) + per, step_fn, 0)
     if cuts:
+        late = spreads[1]
+        taps = table_ref[:, 0:16]
+        for tap in range(1, 7):
+            taps += table_ref[:, 16 * tap : 16 * tap + 16]
+        stage_ref[...] = jnp.zeros_like(stage_ref)
+        table_ref[:, 0:16] = taps
         for i in range(8):
-            small_ref[i, :, 0:filters] = dw_ref[16 * i : 16 * i + 16, :]
-            small_ref[i, :, filters : filters + 3 * LANES] = jnp.zeros((16, 3 * LANES), f32)
+            late.in_ref[i, :, 0:filters] = dw_ref[16 * i : 16 * i + 16, :].astype(bf16)
             for k in range(3):
-                lane = filters + k * LANES
-                small_ref[i, 0:11, lane : lane + LANES] = table_ref[
-                    33 * i + 11 * k : 33 * i + 11 * k + 11, :
+                size = 16 if k < 2 else 1
+                stage_ref[0:size, 16 * k : 16 * k + 16] = table_ref[
+                    33 * i + 16 * k : 33 * i + 16 * k + size, 0:16
                 ]
-            small_ref[i, :, filters + 3 * LANES :] = early_ref[i]
-        spread_small(small_sems, small_ref, small_got, small_mid, small_all)
+            late.in_ref[i, :, filters:] = stage_ref[...].astype(bf16)
+        late.first()
+        spreads[0].finish()
+        unpack_early(spreads[0].out_ref, hwb_out, vec_out, upb_out, qv_out)
+        late.second()
+        late.third()
+        for k in range(4):
+            hw_out[k // 2, k % 2] = items[k].finish2().astype(bf16)
+        late.finish()
         for t in range(count):
             lanes = slice(t * filters, (t + 1) * filters)
             for i in range(7):
-                band = slice(16 * i, 16 * i + 16)
-                convw_out[band, lanes] = small_all[i, t, :, 0:filters].astype(f32) * mask_ref[band, :]
-            convb_out[:, lanes] = small_all[7, t, :, 0:filters].astype(f32)[0:1]
+                convw_out[16 * i : 16 * i + 16, lanes] = late.out_ref[i, t, :, 0:filters]
+            convb_out[:, lanes] = late.out_ref[7, t, :, 0:filters].astype(f32)[0:1]
         for i in range(8):
-            total = small_all[i, 0, :, filters : filters + 3 * LANES].astype(f32)
+            total = late.out_ref[i, 0, :, filters:].astype(f32)
             for t in range(1, count):
-                total += small_all[i, t, :, filters : filters + 3 * LANES].astype(f32)
+                total += late.out_ref[i, t, :, filters:].astype(f32)
             for k in range(3):
-                table_out[33 * i + 11 * k : 33 * i + 11 * k + 11, :] = total[
-                    0:11, k * LANES : (k + 1) * LANES
+                size = 16 if k < 2 else 1
+                table_out[33 * i + 16 * k : 33 * i + 16 * k + size, :] = total[
+                    0:size, 16 * k : 16 * k + 16
                 ]
-            for t in range(count):
-                early_out[t, i] = small_all[i, t, :, filters + 3 * LANES :].astype(f32)
-        for k in range(4):
-            hw_out[k // 2, k % 2] = items[k].finish2()
-        total = items[4].finish2()
-        units = up_out.shape[1]
-        up_out[...] = total[:, :units]
-        down_out[...] = total[:, units:].T
-        total = items[5].finish2()
-        three = qkv_out.shape[1]
-        proj_out[...] = total[:, :filters].T
-        qkv_out[...] = total[:, filters : filters + three]
-        o_out[...] = total[:, 1152 : 1152 + three // 3].T
     scatter.drain()
 
 
-def conv_backward(ids, x, p, wb, off, logs, prev, part, whole, dt, dg, rest, count, cid):
+def conv_backward(ids, x, p, w, off, logs, prev, part, whole, dt, dg, rest, count, cid):
     words, filters = logs.shape
     chars = p.shape[1]
     chunks = 8
     shape = jax.ShapeDtypeStruct
     hw_shape = (2, 2, 2, whole.shape[1] // 8, filters)
-    operands = [ids, x, p, wb, off, logs, prev, part, whole, dt, dg]
-    in_specs = [VMEM, ANY, ANY] + [VMEM] * 5 + [ANY, VMEM, VMEM]
+    operands = [ids, x, p, w, off, logs, prev, part, whole, dt, dg] + list(rest)
+    in_specs = [VMEM, ANY, ANY] + [VMEM] * 5 + [ANY, VMEM, VMEM] + [VMEM] * len(rest)
     sums = [(LANES, filters), (264, LANES)]
     scratch = []
     cuts = None
     if rest:
-        mids, mask, early, units, three = rest
-        cuts = (14, 26)
-        operands += list(mids) + [mask, early]
-        in_specs += [VMEM] * 6
-        own = [hw_shape[-2:]] * 2
-        tails = own + [mid.shape[-2:] for mid in mids]
-        rows = mids[2].shape[-2]
+        cuts = (17, 28)
+        tail = hw_shape[-2:]
+        features = rest[-1].shape[-1]
         out_shape = [
-            shape((2, 2) + own[0], f32),
-            shape((rows, units), f32),
-            shape((mids[2].shape[-1] - units, rows), f32),
-            shape((filters, rows), f32),
-            shape((rows, three), f32),
-            shape((three // 3, rows), f32),
-            shape((112, count * filters), f32),
+            shape((2, 2) + tail, bf16),
+            shape((112, count * filters), bf16),
             shape((1, count * filters), f32),
-            shape(sums[1], f32),
-            shape((count,) + early.shape, f32),
+            shape((264, 16), f32),
+            shape((4, count * filters), f32),
+            shape((9, features), f32),
+            shape((1, count * features), f32),
+            shape((2, features), f32),
         ]
-        small = (16, filters + 4 * LANES)
-        scratch += [pltpu.VMEM(tail, f32) for tail in sums]
+        scratch += [pltpu.VMEM(shape_of, f32) for shape_of in sums]
         scratch += [pltpu.VMEM(hw_shape, bf16)] * 2
-        scratch += [pltpu.VMEM((2, 2) + tail, bf16) for tail in own]
-        scratch += [pltpu.VMEM((2,) + tail, bf16) for tail in own + own]
-        scratch += [pltpu.VMEM(tail, bf16) for tail in tails]
-        scratch += [DMA((18,))] * 2
-        scratch += [
-            pltpu.VMEM((8,) + small, f32),
-            pltpu.VMEM((7,) + small, f32),
-            pltpu.VMEM((count,) + small, bf16),
-            pltpu.VMEM((8, count) + small, bf16),
-        ]
-        scratch += [DMA((7,))] * 2 + [DMA((count - 1,))] * 2 + [DMA((7,))] * 2
+        scratch += [pltpu.VMEM((2, 2) + tail, bf16)] * 2
+        scratch += [pltpu.VMEM((2,) + tail, bf16)] * 4
+        scratch += [pltpu.VMEM(tail, bf16)] * 4
+        scratch += [DMA((12,))] * 2
+        for small, kind in (((16, LANES), f32), ((16, filters + LANES), bf16)):
+            scratch += [
+                pltpu.VMEM((8,) + small, kind),
+                pltpu.VMEM((7,) + small, kind),
+                pltpu.VMEM((count,) + small, bf16),
+                pltpu.VMEM((8, count) + small, bf16),
+            ]
+            scratch += [DMA((7,))] * 2 + [DMA((count - 1,))] * 2 + [DMA((7,))] * 2
     else:
-        out_shape = [shape(tail, f32) for tail in sums] + [shape(hw_shape, bf16)] * 2
+        out_shape = [shape(shape_of, f32) for shape_of in sums] + [shape(hw_shape, bf16)] * 2
     scratch += [
         pltpu.VMEM((68, WORD_TILE, LANES), bf16),
+        pltpu.VMEM((16, LANES), f32),
         pltpu.VMEM((words, filters), f32),
         pltpu.VMEM(part.shape, bf16),
         pltpu.VMEM(part.shape, bf16),
         pltpu.VMEM((2,) + x.shape[1:], bf16),
         pltpu.VMEM((2,) + p.shape[1:], bf16),
         pltpu.VMEM(whole.shape, bf16),
+        pltpu.VMEM(w.shape, bf16),
         DMA((2, 2)),
         DMA,
     ]
@@ -1261,7 +1418,11 @@
             barrier, inc=1, device_id={"tensor": lax.rem(me + hop, count)}, device_id_type=MESH
         )
     pl.semaphore_wait(barrier, dp_count + count - 2)
-    spread_small(sems, in_ref, got, mid, out_ref)
+    spread = Spread(sems, in_ref, got, mid, out_ref)
+    spread.first()
+    spread.second()
+    spread.third()
+    spread.finish()
 
 
 def sum_small(packed, dp_count, count, cid):
@@ -1284,10 +1445,6 @@
         compiler_params=params(cid, 32),
         name="sum_small",
     )(packed)
-
-
-def mm(spec, *operands):
-    return jnp.einsum(spec, *operands, preferred_element_type=f32)
 
 
 def body(
@@ -1322,17 +1479,16 @@
     features = proj_weight.shape[1]
     heads = qkv_weight.shape[2] // HEAD_DIM
 
-    padded = chars + 6
-    ids = jnp.pad(char_ids[:, 0], ((0, 0), (0, 6)), constant_values=-1)
-    ids_tiles = jnp.swapaxes(ids.reshape(words // WORD_TILE, WORD_TILE, padded), 1, 2)
-    ids_tiles = ids_tiles.reshape(words // WORD_TILE, padded * WORD_TILE)
-    table_wide = jnp.pad(jnp.tile(char_table, (1, 7)), ((0, 0), (0, LANES - taps_dim)))
-    one_hot = (ids.T[:, :, None] == lax.broadcasted_iota(jnp.int32, (1, 1, vocab), 2)).astype(bf16)
-    pattern = np.zeros((padded, LANES), np.float32)
-    pattern[:, taps_dim] = 1.0
+    tiles = words // WORD_TILE
+    ids_tiles = jnp.swapaxes(char_ids[:, 0].reshape(tiles, WORD_TILE, chars), 1, 2)
+    ids_tiles = ids_tiles.reshape(tiles, chars * WORD_TILE)
+    flat = [proj_bias, out_bias, down_bias, norm_gain, norm_shift, up_bias, qv_bias, highway_bias]
+    flat = jnp.concatenate([part.reshape(-1) for part in flat]).reshape(-1, LANES)
+
+    pattern = np.zeros((chars, WORD_TILE, LANES), np.float32)
+    pattern[:, :, taps_dim] = 1.0
     for k in range(1, 7):
-        pattern[chars - k, taps_dim + k] = 1.0
-    y = (mm("qwv,vl->qwl", one_hot, table_wide) + pattern[:, None, :]).astype(bf16)
+        pattern[chars - k, :, taps_dim + k] = 1.0
 
     widths = filter_widths(filters)
     off = jnp.asarray(np.log((chars - widths + 1).astype(np.float64)).astype(np.float32))[None]
@@ -1343,66 +1499,55 @@
     w_all = jnp.concatenate(
         [w_taps, conv_bias[None], jnp.asarray(ends, bf16), jnp.zeros((tail, filters), bf16)], axis=0
     )
-    w_back = jnp.pad(w_taps, ((0, LANES - taps_dim), (0, 0)))
-
-    logs, whole, x_tiles, p_tiles = conv_forward(y, w_all, off, count, chars, 1)
-    hidden = jax.nn.silu(logs - off)
-    kept_layers = []
-    for layer in range(highway_weight.shape[0]):
-        if layer > 0:
-            whole = gather_features(hidden.astype(bf16), count, 1 + layer)
-        trans, gate_pre = [
-            mm("rk,kf->rf", whole, highway_weight[layer, j]) + highway_bias[layer, j].astype(f32)
-            for j in range(2)
-        ]
-        kept_layers.append((hidden, whole, trans, gate_pre))
-        gate = jax.nn.sigmoid(gate_pre)
-        hidden = gate * jax.nn.silu(trans) + (1.0 - gate) * hidden
-    vec = jnp.concatenate(
-        [jnp.stack([proj_bias, out_bias, down_bias]), norm_gain, norm_shift], axis=0
-    ).astype(f32)
-    qkv_b = jnp.stack([qv_bias[0], jnp.zeros_like(qv_bias[0]), qv_bias[1]]).reshape(1, -1)
-    place = lax.broadcasted_iota(jnp.int32, (1, words), 1)
-    live = jnp.where(place < seq_lengths[0], 1.0, 0.0).astype(f32)
+
+    logs, whole0, whole1, top, x_tiles, p_tiles, t0, g0, h0, t1, g1, h1 = embed_forward(
+        ids_tiles,
+        char_table.T,
+        jnp.asarray(pattern, bf16),
+        w_all,
+        off,
+        flat,
+        highway_weight,
+        count,
+        chars,
+        1,
+    )
     encoded, d_hidden, tr_a, tr_b, row_sums, proj_sums = encoder(
-        hidden.astype(bf16),
+        top,
         (
             proj_weight,
-            qkv_weight.reshape(features, -1),
+            jnp.transpose(qkv_weight, (1, 2, 0)).reshape(-1, features),
             output_projection_weight,
             up_weight,
             down_weight,
         ),
-        jnp.pad(vec, ((0, 7), (0, 0))),
-        up_bias.astype(f32)[None],
-        qkv_b.astype(f32),
+        flat,
         out_grad[:, 0],
-        live,
+        seq_lengths,
         count,
         4,
     )
     encoded = encoded[:, None]
 
-    (h0, whole0, t0, g0), (h1, whole1, t1, g1) = kept_layers
     back_args = (d_hidden, t1, g1, h1, t0, g0, h0, whole1, highway_weight)
-    conv_args = (ids_tiles, x_tiles, p_tiles, w_back, off, logs)
-    taps_mask = tap_of < widths[None]
+    conv_args = (ids_tiles, x_tiles, p_tiles, w_all, off, logs)
+    taps_mask = np.tile(tap_of < widths[None], (1, count))
     three = 3 * heads * HEAD_DIM
+    units = up_weight.shape[1]
     if dp_count == 8 and (features // dp_count) % 16 == 0:
-        part0, prev0, dt0, dg0, hw_bias_part, *mids = highway_back(
+        part0, prev0, dt0, dg0, hw_bias_part, mid_a, mid_b, tr_a, tr_b = highway_back(
             *back_args, tr_a, tr_b, count, 9
         )
-        early = jnp.concatenate(
-            [part.reshape(-1) for part in (hw_bias_part, proj_sums, row_sums[:10])]
+        (hw_w_grad, conv_w_grad, conv_b_grad, table_grad, hw_b_grad, rows, up_b_grad,
+         qv_grad) = conv_backward(
+            *conv_args, prev0, part0, whole0, dt0, dg0,
+            (mid_a, mid_b, hw_bias_part, proj_sums, row_sums), count, 10,
         )
-        early = jnp.pad(early, (0, 8 * 16 * LANES - early.size)).reshape(8, 16, LANES)
-        (hw_w_grad, up_w_grad, down_w_grad, proj_w_grad, qkv_w_grad, out_w_grad, conv_w_grad,
-         conv_b_grad, table_all, early) = conv_backward(
-            *conv_args, prev0, part0, whole0, dt0, dg0,
-            (mids, jnp.asarray(taps_mask, f32), early, up_weight.shape[1], three), count, 10,
-        )
-        conv_b_grad = conv_b_grad[0]
-        early = early.reshape(count, -1)
+        conv_w_grad, conv_b_grad = conv_w_grad.astype(f32), conv_b_grad[0]
+        hw_w_grad = hw_w_grad.astype(f32)
+        tr_a, tr_b = tr_a.astype(f32), tr_b.astype(f32)
+        table_grad = table_grad[:vocab]
+        up_b_grad = up_b_grad[0]
     else:
         part0, prev0, dt0, dg0, hw_bias_part, *hw1 = highway_back(*back_args, None, None, count, 9)
         d_w_all, table_all, *hw0 = conv_backward(
@@ -1417,12 +1562,6 @@
             for part in (tr_a, tr_b)
         ]
         hw_w_grad = hw_sum.reshape(2, 2, -1, filters)
-        units = up_weight.shape[1]
-        up_w_grad = tr_a[:, :units]
-        down_w_grad = tr_a[:, units:].T
-        proj_w_grad = tr_b[:, :filters].T
-        qkv_w_grad = tr_b[:, filters : filters + three]
-        out_w_grad = tr_b[:, 1152 : 1152 + heads * HEAD_DIM].T
         pieces = [d_w_all[: taps_dim + 1], table_all, hw_bias_part, proj_sums, row_sums[:10]]
         flat = jnp.concatenate([part.reshape(-1) for part in pieces])
         width = -(-flat.size // (dp_count * 16 * LANES)) * LANES
@@ -1432,26 +1571,30 @@
         conv_size, table_size = pieces[0].size, table_all.size
         conv_all = summed[:, :conv_size].reshape(count, taps_dim + 1, filters)
         conv_all = jnp.swapaxes(conv_all, 0, 1)
-        conv_w_grad = jnp.where(taps_mask[:, None], conv_all[:taps_dim], 0.0)
-        conv_w_grad = conv_w_grad.reshape(taps_dim, -1)
+        conv_w_grad = conv_all[:taps_dim].reshape(taps_dim, -1)
         conv_b_grad = conv_all[taps_dim].reshape(-1)
         table_all = jnp.sum(summed[:, conv_size : conv_size + table_size], axis=0)
         table_all = table_all.reshape(-1, LANES)
         early = summed[:, conv_size + table_size :]
-
-    qkv_w_grad = qkv_w_grad.reshape(-1, 3, heads * HEAD_DIM)
-    table_grad = jnp.sum(
-        table_all[:vocab, :taps_dim].reshape(vocab, taps_dim // char_dim, char_dim), axis=1
-    )
-    hw_b_grad = jnp.swapaxes(early[:, : 4 * filters].reshape(count, 4, filters), 0, 1)
+        table_grad = jnp.sum(
+            table_all[:vocab, :taps_dim].reshape(vocab, taps_dim // char_dim, char_dim), axis=1
+        )
+        hw_b_grad = jnp.swapaxes(early[:, : 4 * filters].reshape(count, 4, filters), 0, 1)
+        early = early[:, 4 * filters :]
+        qv_grad = jnp.swapaxes(early[:, :three].reshape(count, 3, -1), 0, 1)[::2].reshape(2, -1)
+        rows = early[:, three : three + 10 * features].reshape(count, 10, features)
+        up_b_grad = rows[:, 9].reshape(-1)
+        rows = rows[0]
+
+    conv_w_grad = jnp.where(taps_mask, conv_w_grad, 0.0)
     hw_b_grad = hw_b_grad.reshape(2, 2, -1)
-    early = early[:, 4 * filters :]
-    qv_grad = jnp.swapaxes(early[:, :three].reshape(count, 3, -1), 0, 1)[::2].reshape(2, -1)
-    rows = early[:, three : three + 10 * features].reshape(count, 10, features)
-    proj_b_grad, out_b_grad, down_b_grad = rows[0, 0], rows[0, 1], rows[0, 2]
-    gain_grad = rows[0, 3:6]
-    shift_grad = rows[0, 6:9]
-    up_b_grad = rows[:, 9].reshape(-1)
+    up_w_grad = tr_a[:, :units]
+    down_w_grad = tr_a[:, units:].T
+    proj_w_grad = tr_b[:, :filters].T
+    qkv_w_grad = tr_b[:, filters : filters + three].reshape(-1, 3, heads * HEAD_DIM)
+    out_w_grad = tr_b[:, 1152 : 1152 + heads * HEAD_DIM].T
+    proj_b_grad, out_b_grad, down_b_grad = rows[0], rows[1], rows[2]
+    gain_grad, shift_grad = rows[3:6], rows[6:9]
     return (
         encoded,
         table_grad,

time: 451 us -> 429 us (0.951)
  matrix products: 24.9 us -> 0 us
  Pallas kernels: 390 us -> 399 us
  local copies, waits for them, and re-layouts: 29.3 us -> 22.5 us
    dot_general x5 -> x0, matrix products: 24.9 us -> none  [mm(): return jnp.einsum(spec, *operands, preferred_element_type=f32)]
    pallas_call x2 -> x1, Pallas kernels: 81.4 us -> 89.6 us  [embed_forward(): pl.pallas_call(functools.partial(embed_forward_kernel, count, chars), out...]
    pallas_call x1, Pallas kernels: 82.7 us -> 75.1 us  [conv_backward(): pl.pallas_call(functools.partial(conv_backward_kernel, count, chars, cuts...]
    pallas_call x1, Pallas kernels: 145 us -> 151 us  [encoder(): pl.pallas_call(functools.partial(encoder_kernel, count, chunks, spacing),...]
    unnamed x52 -> x36, local copies, waits for them, and re-layouts: 13.4 us -> 11.7 us
where the time goes in v4:
time: 429 us; the launch traced here: 428 us
  Pallas kernels  399 us (93%)
  local copies, waits for them, and re-layouts  22.5 us (5%)
  other arithmetic  5.15 us (1%)
    pallas_call x1, Pallas kernels, encoder(): pl.pallas_call(functools.partial(encoder_kernel, count, chunks, spacing),...  151 us
    pallas_call x1, Pallas kernels, embed_forward(): pl.pallas_call(functools.partial(embed_forward_kernel, count, chars), out...  89.6 us
    pallas_call x1, Pallas kernels, highway_back(): pl.pallas_call(functools.partial(highway_back_kernel, count, chunks, redu...  83.4 us
    pallas_call x1, Pallas kernels, conv_backward(): pl.pallas_call(functools.partial(conv_backward_kernel, count, chars, cuts...  75.1 us
    unnamed x36, local copies, waits for them, and re-layouts  11.7 us

profile of v4, /device:TPU:1, one launch (start us, length us, event | category | flops | bytes accessed | tf_op | source)
XLA Modules:
  0.0 428.3 jit_solution(655903841552381738)
XLA Ops:
  1.3 0.1 pad.3.clone
  1.4 0.8 reshape.66
  2.2 0.7 broadcast_in_dim.21
  2.8 0.7 copy.53
  3.5 0.7 reshape.64
  4.2 0.7 reshape.65
  4.9 0.9 dynamic-update-slice
  5.8 0.8 dynamic-update-slice.1
  6.6 0.9 dynamic-update-slice.2
  7.5 0.3 dynamic-update-slice.3
  7.8 0.3 dynamic-update-slice.4
  8.1 0.9 dynamic-update-slice.5
  8.9 0.2 dynamic-update-slice.6
  9.1 0.2 dynamic-update-slice.7
  9.4 1.0 broadcast_select_fusion
  10.3 1.4 maximum_maximum_fusion.refs_3_
  11.8 1.0 copy.47
  12.8 0.2 copy.48
  13.0 0.8 reshape.63.refs_0_
  13.8 0.0 copy-done.6
  13.8 89.6 %embed_forward.1 = (f32[512,512]{1,0:T(8,128)}, bf16[512,2048]{1,0:T(8,128)(2,1)}, bf16[512,2048]{1,0:T(8,128)(2,1)}, bf16[512,512]{1,0:T(8,128)(2,1)}, bf16[16,...) custom-call(s32[16,1600]{1,0:T(8,128)} %reshape.63.refs_0_, ...), custom_call_target="tpu_custom_call" | custom-call | tf_op jit(solution)/shard_map/embed_forward/pallas_call | solution.py:284
  103.4 151.2 %encoder.1 = (bf16[128,768]{1,0:T(8,128)(2,1)}, f32[512,512]{1,0:T(8,128)}, bf16[2,2,2,96,1536]{4,3,2,1,0:T(8,128)(2,1)}, bf16[2,2,2,96,1408]{4,3,2,1,0:T(8,128)...) custom-call(bf16[512,512]{1,0:T(8,128)(2,1)} %get-tuple-element.53.refs_0_, bf16[512,768]{1,0:T(8,128)(2,1)} %refs_1_.1, ...), custom_call_target="tpu_custom_call" | custom-call | tf_op jit(solution)/shard_map/encoder/pallas_call | solution.py:646
  254.6 83.4 %highway_back.1 = (bf16[512,2048]{1,0:T(8,128)(2,1)}, f32[512,512]{1,0:T(8,128)}, bf16[512,512]{1,0:T(8,128)(2,1)}, bf16[512,512]{1,0:T(8,128)(2,1)}, f32[4,512]...) custom-call(f32[512,512]{1,0:T(8,128)} %get-tuple-element.58.refs_0_, ...), custom_call_target="tpu_custom_call" | custom-call | tf_op jit(solution)/shard_map/highway_back/pallas_call | solution.py:1045
  338.0 0.0 copy-start.2
  338.0 75.1 %conv_backward.1 = (bf16[2,2,256,512]{3,2,1,0:T(8,128)(2,1)}, bf16[112,2048]{1,0:T(8,128)(2,1)}, f32[1,2048]{1,0:T(1,128)}, f32[264,16]{1,0:T(8,128)}, f32[4,204...) custom-call(s32[16,1600]{1,0:T(8,128)} %reshape.63.refs_0_, ...), custom_call_target="tpu_custom_call" | custom-call | tf_op jit(solution)/shard_map/conv_backward/pallas_call | solution.py:1394
  413.1 0.0 copy-start
  413.1 1.7 copy.50
  414.8 1.5 slice_reduce_fusion
  416.2 1.4 fusion
  417.7 1.4 reshape.70
  419.1 0.0 copy-done.2
  419.1 0.1 copy.49
  419.2 0.0 copy-start.3
  419.3 0.0 copy-start.4
  419.3 0.9 copy.51
  420.2 0.7 slice_bitcast_fusion.1
  420.9 0.7 copy.52
  421.6 0.0 copy-done
  421.6 0.7 slice.47
  422.4 0.7 slice_bitcast_fusion
  423.2 0.0 copy-done.4
  423.2 1.1 convert_select_fusion
  424.2 1.6 convert_element_type.15
  425.9 0.7 copy.67
  426.5 0.6 copy.68
  427.1 0.0 copy-done.9
  427.1 0.6 copy.69
  427.7 0.6 copy.70
  (17 shorter events, 0.1 us)
Async XLA Ops:
  9.4 4.5 %copy-start.6 = (bf16[10112]{0:T(1024)(128)(2,1)}, bf16[10112]{0:T(1024)(128)(2,1)S(1)}, u32[]{:S(2)}) copy-start(bf16[10112]{0:T(1024)(128)(2,1)S(1)} %dynamic-update-slice.7) | copy-start | bytes 60676
  338.0 81.1 %copy-start.2 = (bf16[96,1408]{1,0:T(8,128)(2,1)S(1)}, bf16[96,1408]{1,0:T(8,128)(2,1)}, u32[]{:S(2)}) copy-start(bf16[96,1408]{1,0:T(8,128)(2,1)} %get-tuple-element.83) | copy-start | bytes 811012
  413.1 8.5 %copy-start = (bf16[96,1536]{1,0:T(8,128)(2,1)S(1)}, bf16[96,1536]{1,0:T(8,128)(2,1)}, u32[]{:S(2)}) copy-start(bf16[96,1536]{1,0:T(8,128)(2,1)} %get-tuple-element.86) | copy-start | bytes 884740
  419.2 3.9 copy-start.3
  419.3 3.9 copy-start.4
  420.2 4.0 copy-start.1
  423.2 2.7 copy-start.5
  424.2 2.3 copy-start.8
  424.2 2.9 copy-start.9
  424.2 3.5 copy-start.7

commit v5 on v4

--- a/solution.py
+++ b/solution.py
@@ -45,7 +45,7 @@
     return lax.dot_general(a, b, (((ca,), (cb,)), ((), ())), preferred_element_type=f32)
 
 
-def line_barrier(me, count):
+def line_greet(me, count):
     barrier = pltpu.get_barrier_semaphore()
     for there, ok in ((me - 1, me > 0), (me + 1, me < count - 1)):
 
@@ -53,7 +53,11 @@
         def greet():
             pl.semaphore_signal(barrier, inc=1, device_id={"tensor": there}, device_id_type=MESH)
 
-    pl.semaphore_wait(barrier, jnp.minimum(me, 1) + jnp.minimum(count - 1 - me, 1))
+
+def line_meet(me, count):
+    pl.semaphore_wait(
+        pltpu.get_barrier_semaphore(), jnp.minimum(me, 1) + jnp.minimum(count - 1 - me, 1)
+    )
 
 
 def line_copy(view, me, count, right, block, chunk, sems):
@@ -70,9 +74,9 @@
     )
 
 
-def gather_step(view, step, chunks, me, count, sems):
+def gather_step(view, step, chunks, me, count, sems, spacing=1):
     for hop in range(count):
-        chunk = step - hop
+        chunk = step - spacing * hop
         here = (chunk >= 0) & (chunk < chunks)
         safe = jnp.clip(chunk, 0, chunks - 1)
         for right in (True, False):
@@ -111,26 +115,18 @@
     lax.fori_loop(0, chunks, one, 0)
 
 
-FLAT_QV = 60
-FLAT_HIGHWAY = 63
-
-
-def flat_row(ref, start, blocks):
-    return jnp.concatenate(
-        [ref[start + k : start + k + 1, :] for k in range(blocks)], axis=1
-    ).astype(f32)
-
-
 def embed_forward_kernel(count, chars, *refs):
-    (ids_ref, chars_ref, pattern_ref, w_ref, off_ref, flat_ref, hw_hbm) = refs[:7]
-    log_ref, whole0_ref, whole1_ref, top_ref, x_hbm, p_hbm = refs[7:13]
-    kept = refs[13:19]
-    y_buf, x_buf, p_buf, hw_ref, table_ref, hb_ref, keep_sem, late_sem = refs[19:27]
-    bufs = refs[27:33]
-    sems0, sems1 = refs[33:37], refs[37:41]
+    (ids_ref, chars_ref, pattern_ref, cw_ref, cb_ref, mask_ref, ends_ref, off_ref, bias_ref,
+     hw_hbm) = refs[:10]
+    log_ref, whole0_ref, whole1_ref, top_ref, x_hbm, p_hbm = refs[10:16]
+    kept = refs[16:22]
+    y_buf, x_buf, p_buf, hw_ref, table_ref, w_ref, hb_ref, keep_sem, late_sem = refs[22:31]
+    bufs = refs[31:37]
+    sems0, sems1 = refs[37:41], refs[41:45]
     t_refs, g_refs, h_refs = (bufs[0], bufs[3]), (bufs[1], bufs[4]), (bufs[2], bufs[5])
     wholes = (whole0_ref, whole1_ref)
     me = lax.axis_index("tensor")
+    line_greet(me, count)
     words, filters = log_ref.shape
     tiles = words // WORD_TILE
     half = words // 2
@@ -151,10 +147,14 @@
     depth, vocab_size = chars_ref.shape
     for tap in range(7):
         table_ref[depth * tap : depth * tap + depth, 0:vocab_size] = chars_ref[...]
-    for k in range(4):
-        start = FLAT_HIGHWAY + k * (filters // LANES)
-        hb_ref[k : k + 1, :] = flat_row(flat_ref, start, filters // LANES)
-    line_barrier(me, count)
+    for layer in range(2):
+        hb_ref[2 * layer : 2 * layer + 2, :] = bias_ref[layer].astype(f32)
+    taps = cw_ref.shape[0]
+    w_ref[0:taps, :] = (cw_ref[...].astype(f32) * mask_ref[...]).astype(bf16)
+    first = lax.broadcasted_iota(jnp.int32, ends_ref.shape, 0) == 0
+    bias = cb_ref[...].astype(f32).reshape(1, filters)
+    w_ref[taps:, :] = jnp.where(first, bias, ends_ref[...]).astype(bf16)
+    line_meet(me, count)
 
     def view_of(whole):
         def view(block, chunk):
@@ -228,17 +228,19 @@
 
         lax.fori_loop(0, half // WORD_TILE, mix, 0)
 
-    shift = tiles // 2 + count - 1
-    last = shift + tiles + count - 1
+    spacing = 2
+    fill = spacing * (count - 1)
+    shift = tiles // 2 + fill
+    last = shift + tiles + fill
 
     def step_fn(step, carry):
         @pl.when(step < tiles)
         def convolve():
             tile_step(step)
 
-        @pl.when(step < tiles + count - 1)
+        @pl.when(step < tiles + fill)
         def first_gather():
-            gather_step(views[0], step, tiles, me, count, sems0)
+            gather_step(views[0], step, tiles, me, count, sems0, spacing)
 
         @pl.when(step == shift)
         def first_half():
@@ -253,7 +255,7 @@
 
         @pl.when(step >= shift)
         def second_gather():
-            gather_step(views[1], step - shift, tiles, me, count, sems1)
+            gather_step(views[1], step - shift, tiles, me, count, sems1, spacing)
 
         @pl.when(step == 2 * shift - 1)
         def third_half():
@@ -275,8 +277,8 @@
         copy.wait()
 
 
-def embed_forward(ids, table, pattern, w, off, flat_vec, weight, count, chars, cid):
-    filters = w.shape[1]
+def embed_forward(ids, table, pattern, conv, off, bias, weight, count, chars, cid):
+    filters = conv[0].shape[1]
     tiles = ids.shape[0]
     words = tiles * WORD_TILE
     shape = jax.ShapeDtypeStruct
@@ -292,7 +294,7 @@
             shape((tiles, chars, WORD_TILE, filters), bf16),
         )
         + (shape(flat, f32),) * 6,
-        in_specs=[VMEM] * 6 + [ANY],
+        in_specs=[VMEM] * 9 + [ANY],
         out_specs=(VMEM,) * 4 + (ANY,) * 8,
         scratch_shapes=[
             pltpu.VMEM((chars + 6, WORD_TILE, LANES), bf16),
@@ -300,6 +302,7 @@
             pltpu.VMEM((2, chars, WORD_TILE, filters), bf16),
             pltpu.VMEM(weight.shape, bf16),
             pltpu.VMEM((LANES, 264), bf16),
+            pltpu.VMEM((LANES, filters), bf16),
             pltpu.VMEM((8, filters), f32),
             DMA((2, 2)),
             DMA((8,)),
@@ -308,7 +311,7 @@
         + [DMA((count, tiles))] * 8,
         compiler_params=params(cid, 58),
         name="embed_forward",
-    )(ids, table, pattern, w, off, flat_vec, weight)
+    )(ids, table, pattern, *conv, off, bias, weight)
 
 
 class LineSum:
@@ -422,13 +425,15 @@
 
 
 def encoder_kernel(count, chunks, spacing, *refs):
-    top_ref, pw_ref, qw_ref, ow_ref, uw_ref, dw_ref, flat_ref, og_ref, len_ref = refs[:9]
-    enc_ref, dh2_ref, tra_ref, trb_ref, sums_ref, qsum_ref, vec_ref, qb_ref = refs[9:17]
+    top_ref, pw_ref, qw_ref, ow_ref, uw_ref, dw_ref = refs[:6]
+    bias_refs, norm_refs, qv_ref, og_ref, len_ref = refs[6:10], refs[10:12], *refs[12:15]
+    enc_ref, dh2_ref, tra_ref, trb_ref, sums_ref, qsum_ref, vec_ref, qb_ref = refs[15:23]
     (emb, inp, midpre, mid, fin, slope, dmid, din, sent, sent_mid, act, d_two, d_up, d_branch,
      d_emb, qkv, attended, probs, d_heads, d_proj, part, grad_all, enc_all, from_left,
-     from_right) = refs[17:42]
-    line_sems, gather_sems = refs[42:46], refs[46:50]
+     from_right) = refs[23:48]
+    line_sems, gather_sems = refs[48:52], refs[52:56]
     me = lax.axis_index("tensor")
+    line_greet(me, count)
     words, features = emb.shape
     heads = attended.shape[1] // HEAD_DIM
     hidden = heads * HEAD_DIM
@@ -438,16 +443,15 @@
     grad_all[own_tile, :] = og_ref[...]
     sums_ref[...] = jnp.zeros_like(sums_ref)
     trb_ref[...] = jnp.zeros_like(trb_ref)
-    for k in range(10):
-        vec_ref[k : k + 1, :] = flat_row(flat_ref, k * (features // LANES), features // LANES)
-    ends = [flat_ref[FLAT_QV + k : FLAT_QV + k + 1, :].astype(f32) for k in range(3)]
+    for k, bias_ref in zip((0, 1, 2, 9), bias_refs):
+        vec_ref[k : k + 1, :] = bias_ref[...].astype(f32).reshape(1, features)
+    for k, norm_ref in zip((3, 6), norm_refs):
+        vec_ref[k : k + 3, :] = norm_ref[...].astype(f32)
     qb_ref[...] = jnp.zeros_like(qb_ref)
-    qb_ref[:, 0:128] = ends[0]
-    qb_ref[:, 128:192] = ends[1][:, 0:64]
-    qb_ref[:, 384:448] = ends[1][:, 64:128]
-    qb_ref[:, 448:576] = ends[2]
+    ends = qv_ref[...].astype(f32)
+    qb_ref[:, 0:hidden] = ends[0:1]
+    qb_ref[:, 2 * hidden : 3 * hidden] = ends[1:2]
     live = lax.broadcasted_iota(jnp.int32, (1, words), 1) < len_ref[0]
-    line_barrier(me, count)
 
     def line(number, out_ref):
         return LineSum(
@@ -495,6 +499,7 @@
         sums_ref[index : index + 1, :] += column_sum(value)
 
     send_product(top_ref, pw_ref, 0, emb)
+    line_meet(me, count)
 
     def first_norm(tile):
         value = emb[tile, :] + row(0)
@@ -508,9 +513,9 @@
     def project(tile):
         qkv[tile, :] = (dot(sent[tile, :], qw_ref[...], 1, 1) + qb_ref[...]).astype(bf16)
 
+    gather_step(gather_view, 0, 1, me, count, gather_sems)
     tiles(256, project)
 
-    gather_step(gather_view, 0, 1, me, count, gather_sems)
     for head in range(heads):
         lanes = slice(head * HEAD_DIM, (head + 1) * HEAD_DIM)
         keys = slice(hidden + head * HEAD_DIM, hidden + (head + 1) * HEAD_DIM)
@@ -525,11 +530,13 @@
             attended[tile, lanes] = dot(value.astype(bf16), qkv[:, vals], 1, 0).astype(bf16)
 
         tiles(128, attend)
-        if head + 1 < count:
-            gather_step(gather_view, head + 1, 1, me, count, gather_sems)
-    for step in range(heads + 1, count):
-        gather_step(gather_view, step, 1, me, count, gather_sems)
+        if head == heads - 2:
+            gather_step(gather_view, 1, 1, me, count, gather_sems)
     send_product(attended, ow_ref, 0, midpre)
+
+    def pass_grads():
+        for step in range(2, count - 1):
+            gather_step(gather_view, step, 1, me, count, gather_sems)
 
     def second_norm(tile):
         value = midpre[tile, :] + inp[tile, :] + row(1)
@@ -538,7 +545,8 @@
         mid[tile, :] = value
         sent_mid[tile, :] = value.astype(bf16)
 
-    line(1, midpre).run(second_norm)
+    line(1, midpre).run(second_norm, [lambda: None, lambda: None, pass_grads])
+    gather_step(gather_view, count - 1, 1, me, count, gather_sems)
 
     def feed(tile):
         value, back = gelu_parts(dot(sent_mid[tile, :], uw_ref[...], 1, 0) + row(9))
@@ -624,13 +632,13 @@
     gather_drain(gather_view, 1, me, count, gather_sems)
 
 
-def encoder(top, weights, flat, out_grad, lengths, count, cid):
+def encoder(top, weights, biases, out_grad, lengths, count, cid):
     words, filters = top.shape
     features = weights[0].shape[1]
     three = weights[1].shape[0]
     units = weights[3].shape[1]
     hidden = three // 3
-    chunks, spacing = 16, 3
+    chunks, spacing = 16, 4
     shape = jax.ShapeDtypeStruct
     rows = features // 8
     scratch = [pltpu.VMEM((16, features), f32), pltpu.VMEM((1, three), f32)]
@@ -653,12 +661,12 @@
             shape((16, features), f32),
             shape((1, three), f32),
         ),
-        in_specs=[VMEM] * 8 + [pl.BlockSpec(memory_space=pltpu.SMEM)],
+        in_specs=[VMEM] * 14 + [pl.BlockSpec(memory_space=pltpu.SMEM)],
         out_specs=(VMEM,) * 6,
         scratch_shapes=scratch,
         compiler_params=params(cid, 58),
         name="encoder",
-    )(top, *weights, flat, out_grad, lengths)
+    )(top, *weights, *biases, out_grad, lengths)
 
 
 class LineScatter:
@@ -810,7 +818,10 @@
     barrier = pltpu.get_barrier_semaphore()
     for peer in peers:
         pl.semaphore_signal(barrier, inc=1, device_id=peer, device_id_type=MESH)
-    pl.semaphore_wait(barrier, len(peers))
+
+
+def meet_all(peers):
+    pl.semaphore_wait(pltpu.get_barrier_semaphore(), len(peers))
 
 
 def mix_back(d_hidden, trans, gate_pre, previous):
@@ -875,6 +886,8 @@
         for copy in keep:
             copy.start()
     ring = [{"tensor": lax.rem(me + k, count)} for k in range(1, count)]
+    everyone = (peers if reduce else []) + ring
+    greet_all(everyone)
     sums_ref[...] = jnp.zeros_like(sums_ref)
 
     def mix(layer, d_h_ref, t_ref, g_ref, h_ref, dt_ref, dg_ref, prev_ref, tile):
@@ -915,12 +928,12 @@
             tile, pl.ds(pl.multiple_of(me * filters, filters), filters)
         ].astype(f32)
 
-    lax.fori_loop(0, chunks, first, 0)
+    lax.fori_loop(0, chunks // 2, first, 0)
     loads[0].wait()
     products(1, dt1_ref, dg1_ref, part1_ref, 0)
     own_part(0)
+    meet_all(everyone)
     if reduce:
-        greet_all(peers + ring)
         for k in range(4):
             item = DpSum(cell, peers, k % 2 == 0, dp_sems, 3 * k)
             if k < 2:
@@ -933,8 +946,6 @@
             items.append(item)
         for item in items[2:]:
             item.copy0().start()
-    else:
-        greet_all(ring)
     scatter = LineScatter(
         count, me, chunks, 3, part1_ref, d_h1_ref, from_left, from_right, sems
     )
@@ -944,6 +955,7 @@
 
         @pl.when(step == 0)
         def rest():
+            lax.fori_loop(chunks // 2, chunks, first, 0)
             products(1, dt1_ref, dg1_ref, part1_ref, 1)
             own_part(1)
             loads[1].wait()
@@ -1153,9 +1165,9 @@
 
 
 def conv_backward_kernel(count, chars, cuts, *refs):
-    (ids_ref, x_hbm, p_hbm, w_ref, off_ref, log_ref, prev_ref, part_ref, whole_hbm, dt_ref,
-     dg_ref) = refs[:11]
-    refs = refs[11:]
+    (ids_ref, x_hbm, p_hbm, cw_ref, mask_ref, off_ref, log_ref, prev_ref, part_ref, whole_hbm,
+     dt_ref, dg_ref) = refs[:12]
+    refs = refs[12:]
     if cuts:
         mids_in = refs[:2]
         hb_sums, proj_sums, row_sums = refs[2:5]
@@ -1195,7 +1207,7 @@
         place = lax.axis_index("dp")
         dp_count = spreads[0].dp_count
         cell, dp_peers = dp_cell(place)
-        greet_all([{"dp": lax.rem(place + k, dp_count)} for k in range(1, dp_count)] + ring)
+        ring += [{"dp": lax.rem(place + k, dp_count)} for k in range(1, dp_count)]
         for k in range(4):
             item = DpSum(cell, dp_peers, k % 2 == 0, dp_sems, 3 * k)
             item.in2 = in2s[k]
@@ -1206,21 +1218,22 @@
             else:
                 item.mid = mids_in[k - 2]
             items.append(item)
-        for item in items[2:]:
-            item.copy2().start()
         pack_early(spreads[0].in_ref, hb_sums, proj_sums, row_sums)
-        spreads[0].first()
-    else:
-        greet_all(ring)
-
-    row_of = lax.broadcasted_iota(jnp.int32, w_ref.shape, 0)
-    wb_ref[...] = jnp.where(row_of < 112, w_ref[...].astype(f32), 0.0).astype(bf16)
+    greet_all(ring)
+    taps = cw_ref.shape[0]
+    wb_ref[...] = jnp.zeros_like(wb_ref)
+    wb_ref[0:taps, :] = (cw_ref[...].astype(f32) * mask_ref[...]).astype(bf16)
     dw_ref[...] = jnp.zeros_like(dw_ref)
     table_ref[...] = jnp.zeros_like(table_ref)
     pad_ref[...] = jnp.zeros_like(pad_ref)
     grad_ref[...] = prev_ref[...] + part_ref[
         :, pl.ds(pl.multiple_of(me * filters, filters), filters)
     ].astype(f32)
+    meet_all(ring)
+    for item in items[2:]:
+        item.copy2().start()
+    if cuts:
+        spreads[0].first()
     chunks = line_sems[0].shape[1]
     per = words // chunks // WORD_TILE
     scatter = LineScatter(
@@ -1336,14 +1349,14 @@
     scatter.drain()
 
 
-def conv_backward(ids, x, p, w, off, logs, prev, part, whole, dt, dg, rest, count, cid):
+def conv_backward(ids, x, p, w, mask, off, logs, prev, part, whole, dt, dg, rest, count, cid):
     words, filters = logs.shape
     chars = p.shape[1]
     chunks = 8
     shape = jax.ShapeDtypeStruct
     hw_shape = (2, 2, 2, whole.shape[1] // 8, filters)
-    operands = [ids, x, p, w, off, logs, prev, part, whole, dt, dg] + list(rest)
-    in_specs = [VMEM, ANY, ANY] + [VMEM] * 5 + [ANY, VMEM, VMEM] + [VMEM] * len(rest)
+    operands = [ids, x, p, w, mask, off, logs, prev, part, whole, dt, dg] + list(rest)
+    in_specs = [VMEM, ANY, ANY] + [VMEM] * 6 + [ANY, VMEM, VMEM] + [VMEM] * len(rest)
     sums = [(LANES, filters), (264, LANES)]
     scratch = []
     cuts = None
@@ -1386,7 +1399,7 @@
         pltpu.VMEM((2,) + x.shape[1:], bf16),
         pltpu.VMEM((2,) + p.shape[1:], bf16),
         pltpu.VMEM(whole.shape, bf16),
-        pltpu.VMEM(w.shape, bf16),
+        pltpu.VMEM((LANES, filters), bf16),
         DMA((2, 2)),
         DMA,
     ]
@@ -1445,6 +1458,64 @@
         compiler_params=params(cid, 32),
         name="sum_small",
     )(packed)
+
+
+def finish_kernel(units, three, *refs):
+    (enc, table, conv_w, mask, conv_b, hw, hw_b, rows, qv, up_b, tr_a, tr_b) = refs[:12]
+    (enc_out, table_out, conv_w_out, conv_b_out, hw_out, hw_b_out, proj_out, proj_b_out, gain_out,
+     shift_out, qkv_out, qv_out, o_out, o_b_out, up_out, up_b_out, down_out, down_b_out) = refs[12:]
+    filters = mask.shape[1]
+    enc_out[0] = enc[...]
+    table_out[...] = table[...].T[:, 0 : table_out.shape[1]]
+    for start in range(0, conv_w.shape[1], filters):
+        lanes = slice(start, start + filters)
+        conv_w_out[:, lanes] = conv_w[:, lanes].astype(f32) * mask[...]
+    conv_b_out[...] = conv_b[...].reshape(conv_b_out.shape)
+    for layer in range(2):
+        hw_b_out[layer] = hw_b[2 * layer : 2 * layer + 2, :]
+        for j in range(2):
+            hw_out[layer, j] = hw[layer, j].astype(f32)
+    for k, out in enumerate((proj_b_out, o_b_out, down_b_out)):
+        out[...] = rows[k : k + 1, :].reshape(out.shape)
+    gain_out[...] = rows[3:6, :]
+    shift_out[...] = rows[6:9, :]
+    qv_out[...] = qv[...]
+    up_b_out[...] = up_b[...].reshape(up_b_out.shape)
+    up_out[...] = tr_a[:, 0:units].astype(f32)
+    down_out[...] = tr_a[:, units:].astype(f32)
+    proj_out[...] = tr_b[:, 0:filters].astype(f32)
+    hidden = three // 3
+    qkv = tr_b[:, filters : filters + three].astype(f32)
+    for k in range(3):
+        qkv_out[k] = qkv[:, k * hidden : (k + 1) * hidden]
+    o_out[...] = tr_b[:, 1152 : 1152 + hidden].astype(f32).T
+
+
+def finish(encoded, table, conv_w, mask, conv_b, hw, hw_b, rows, qv, up_b, tr_a, tr_b, vocab,
+           units, three):
+    features, depth, filters = rows.shape[1], tr_a.shape[0], mask.shape[1]
+    shapes = [
+        (table.shape[1], vocab), conv_w.shape, (conv_w.shape[1],), hw.shape,
+        (2, 2, hw_b.shape[1]), (depth, filters), (features,), (3, features), (3, features),
+        (3, depth, three // 3), qv.shape, (three // 3, depth), (features,), (depth, units),
+        (up_b.shape[1],), (depth, tr_a.shape[1] - units), (features,),
+    ]
+    (encoded, table, conv_w, conv_b, hw, hw_b, proj, proj_b, gain, shift, qkv, qv, o, o_b, up, up_b,
+     down, down_b) = pl.pallas_call(
+        functools.partial(finish_kernel, units, three),
+        out_shape=tuple(
+            [jax.ShapeDtypeStruct((1,) + encoded.shape, bf16)]
+            + [jax.ShapeDtypeStruct(shape, f32) for shape in shapes]
+        ),
+        in_specs=[VMEM] * 12,
+        out_specs=(VMEM,) * 18,
+        compiler_params=pltpu.CompilerParams(vmem_limit_bytes=32 * MIB),
+        name="finish",
+    )(encoded, table, conv_w, mask, conv_b, hw, hw_b, rows, qv, up_b, tr_a, tr_b)
+    return (
+        jnp.transpose(encoded, (1, 0, 2)), table.T, conv_w, conv_b, hw, hw_b, proj.T, proj_b, gain,
+        shift, jnp.transpose(qkv, (1, 0, 2)), qv, o, o_b, up, up_b, down.T, down_b,
+    )
 
 
 def body(
@@ -1482,9 +1553,6 @@
     tiles = words // WORD_TILE
     ids_tiles = jnp.swapaxes(char_ids[:, 0].reshape(tiles, WORD_TILE, chars), 1, 2)
     ids_tiles = ids_tiles.reshape(tiles, chars * WORD_TILE)
-    flat = [proj_bias, out_bias, down_bias, norm_gain, norm_shift, up_bias, qv_bias, highway_bias]
-    flat = jnp.concatenate([part.reshape(-1) for part in flat]).reshape(-1, LANES)
-
     pattern = np.zeros((chars, WORD_TILE, LANES), np.float32)
     pattern[:, :, taps_dim] = 1.0
     for k in range(1, 7):
@@ -1493,20 +1561,18 @@
     widths = filter_widths(filters)
     off = jnp.asarray(np.log((chars - widths + 1).astype(np.float64)).astype(np.float32))[None]
     tap_of = np.arange(taps_dim)[:, None] // char_dim
-    w_taps = jnp.where(tap_of < widths[None], conv_weight, 0).astype(bf16)
-    ends = np.where(widths[None] > np.arange(1, 7)[:, None], big_neg, 0.0).astype(np.float32)
-    tail = LANES - taps_dim - 7
-    w_all = jnp.concatenate(
-        [w_taps, conv_bias[None], jnp.asarray(ends, bf16), jnp.zeros((tail, filters), bf16)], axis=0
-    )
+    taps_mask = tap_of < widths[None]
+    mask = jnp.asarray(taps_mask, f32)
+    ends = np.zeros((LANES - taps_dim, filters), np.float32)
+    ends[1:7] = np.where(widths[None] > np.arange(1, 7)[:, None], big_neg, 0.0)
 
     logs, whole0, whole1, top, x_tiles, p_tiles, t0, g0, h0, t1, g1, h1 = embed_forward(
         ids_tiles,
         char_table.T,
         jnp.asarray(pattern, bf16),
-        w_all,
+        (conv_weight, conv_bias, mask, jnp.asarray(ends)),
         off,
-        flat,
+        highway_bias,
         highway_weight,
         count,
         chars,
@@ -1521,17 +1587,15 @@
             up_weight,
             down_weight,
         ),
-        flat,
+        (proj_bias, out_bias, down_bias, up_bias, norm_gain, norm_shift, qv_bias),
         out_grad[:, 0],
         seq_lengths,
         count,
         4,
     )
-    encoded = encoded[:, None]
 
     back_args = (d_hidden, t1, g1, h1, t0, g0, h0, whole1, highway_weight)
-    conv_args = (ids_tiles, x_tiles, p_tiles, w_all, off, logs)
-    taps_mask = np.tile(tap_of < widths[None], (1, count))
+    conv_args = (ids_tiles, x_tiles, p_tiles, conv_weight, mask, off, logs)
     three = 3 * heads * HEAD_DIM
     units = up_weight.shape[1]
     if dp_count == 8 and (features // dp_count) % 16 == 0:
@@ -1543,11 +1607,10 @@
             *conv_args, prev0, part0, whole0, dt0, dg0,
             (mid_a, mid_b, hw_bias_part, proj_sums, row_sums), count, 10,
         )
-        conv_w_grad, conv_b_grad = conv_w_grad.astype(f32), conv_b_grad[0]
-        hw_w_grad = hw_w_grad.astype(f32)
-        tr_a, tr_b = tr_a.astype(f32), tr_b.astype(f32)
-        table_grad = table_grad[:vocab]
-        up_b_grad = up_b_grad[0]
+        return finish(
+            encoded, table_grad, conv_w_grad, mask, conv_b_grad, hw_w_grad, hw_b_grad, rows,
+            qv_grad, up_b_grad, tr_a, tr_b, vocab, units, three,
+        )
     else:
         part0, prev0, dt0, dg0, hw_bias_part, *hw1 = highway_back(*back_args, None, None, count, 9)
         d_w_all, table_all, *hw0 = conv_backward(
@@ -1586,7 +1649,7 @@
         up_b_grad = rows[:, 9].reshape(-1)
         rows = rows[0]
 
-    conv_w_grad = jnp.where(taps_mask, conv_w_grad, 0.0)
+    conv_w_grad = jnp.where(np.tile(taps_mask, (1, count)), conv_w_grad, 0.0)
     hw_b_grad = hw_b_grad.reshape(2, 2, -1)
     up_w_grad = tr_a[:, :units]
     down_w_grad = tr_a[:, units:].T
@@ -1596,7 +1659,7 @@
     proj_b_grad, out_b_grad, down_b_grad = rows[0], rows[1], rows[2]
     gain_grad, shift_grad = rows[3:6], rows[6:9]
     return (
-        encoded,
+        encoded[:, None],
         table_grad,
         conv_w_grad,
         conv_b_grad,

time: 429 us -> 377 us (0.88)
  Pallas kernels: 399 us -> 366 us
  local copies, waits for them, and re-layouts: 22.5 us -> 8.88 us
  other arithmetic: 5.15 us -> 0 us
    pallas_call x1, Pallas kernels: 83.4 us -> 60.6 us  [highway_back(): pl.pallas_call(functools.partial(highway_back_kernel, count, chunks, redu...]
    pallas_call x1, Pallas kernels: 151 us -> 141 us  [encoder(): pl.pallas_call(functools.partial(encoder_kernel, count, chunks, spacing),...]
    unnamed x36 -> x25, local copies, waits for them, and re-layouts: 11.7 us -> 7.83 us
where the time goes in v5:
time: 377 us; the launch traced here: 376 us
  Pallas kernels  366 us (97%)
  local copies, waits for them, and re-layouts  8.88 us (2%)
    pallas_call x1, Pallas kernels, encoder(): pl.pallas_call(functools.partial(encoder_kernel, count, chunks, spacing),...  141 us
    pallas_call x1, Pallas kernels, embed_forward(): pl.pallas_call(functools.partial(embed_forward_kernel, count, chars), out...  88.1 us
    pallas_call x1, Pallas kernels, conv_backward(): pl.pallas_call(functools.partial(conv_backward_kernel, count, chars, cuts...  74.1 us
    pallas_call x1, Pallas kernels, highway_back(): pl.pallas_call(functools.partial(highway_back_kernel, count, chunks, redu...  60.6 us
    unnamed x25, local copies, waits for them, and re-layouts  7.83 us

profile of v5, /device:TPU:1, one launch (start us, length us, event | category | flops | bytes accessed | tf_op | source)
XLA Modules:
  0.0 376.3 jit_solution(16547403617623766085)
XLA Ops:
  1.3 1.0 copy.43
  2.3 0.2 copy.44
  2.6 0.8 reshape.42.refs_0_
  3.4 88.1 %embed_forward.1 = (f32[512,512]{1,0:T(8,128)}, bf16[512,2048]{1,0:T(8,128)(2,1)}, bf16[512,2048]{1,0:T(8,128)(2,1)}, bf16[512,512]{1,0:T(8,128)(2,1)}, bf16[16,...) custom-call(s32[16,1600]{1,0:T(8,128)} %reshape.42.refs_0_, ...), custom_call_target="tpu_custom_call" | custom-call | tf_op jit(solution)/shard_map/embed_forward/pallas_call | solution.py:286
  91.5 141.0 %encoder.1 = (bf16[128,768]{1,0:T(8,128)(2,1)}, f32[512,512]{1,0:T(8,128)}, bf16[2,2,2,96,1536]{4,3,2,1,0:T(8,128)(2,1)}, bf16[2,2,2,96,1408]{4,3,2,1,0:T(8,128)...) custom-call(bf16[512,512]{1,0:T(8,128)(2,1)} %get-tuple-element.71.refs_0_, bf16[512,768]{1,0:T(8,128)(2,1)} %refs_1_.1, ...), custom_call_target="tpu_custom_call" | custom-call | tf_op jit(solution)/shard_map/encoder/pallas_call | solution.py:654
  232.5 60.6 %highway_back.1 = (bf16[512,2048]{1,0:T(8,128)(2,1)}, f32[512,512]{1,0:T(8,128)}, bf16[512,512]{1,0:T(8,128)(2,1)}, bf16[512,512]{1,0:T(8,128)(2,1)}, f32[4,512]...) custom-call(f32[512,512]{1,0:T(8,128)} %get-tuple-element.76.refs_0_, ...), custom_call_target="tpu_custom_call" | custom-call | tf_op jit(solution)/shard_map/highway_back/pallas_call | solution.py:1057
  293.2 0.0 copy-start
  293.2 0.0 copy-start.3
  293.2 0.0 copy-start.4
  293.2 0.0 copy-start.5
  293.2 74.1 %conv_backward.1 = (bf16[2,2,256,512]{3,2,1,0:T(8,128)(2,1)}, bf16[112,2048]{1,0:T(8,128)(2,1)}, f32[1,2048]{1,0:T(1,128)}, f32[264,16]{1,0:T(8,128)}, f32[4,204...) custom-call(s32[16,1600]{1,0:T(8,128)} %reshape.42.refs_0_, ...), custom_call_target="tpu_custom_call" | custom-call | tf_op jit(solution)/shard_map/conv_backward/pallas_call | solution.py:1407
  367.3 0.0 copy-done
  367.3 0.0 copy-done.3
  367.3 0.0 copy-done.4
  367.3 0.0 copy-done.5
  367.3 0.0 copy-start.1
  367.3 1.2 copy-done.1
  368.5 0.0 copy-start.2
  368.5 1.0 copy-done.2
  369.6 0.0 copy-start.6
  369.6 0.9 copy-done.6
  370.5 0.0 copy-start.7
  370.5 0.8 copy-done.7
  371.3 0.0 copy-start.8
  371.3 0.8 copy-done.8
  372.0 0.0 copy-start.9
  372.0 0.7 copy-done.9
  372.7 0.0 copy-start.10
  372.7 0.7 copy-done.10
  373.4 0.0 copy-start.11
  373.4 0.7 copy-done.11
  374.1 2.2 finish.1
Async XLA Ops:
  293.2 74.1 %copy-start = (f32[112,512]{1,0:T(8,128)S(1)}, f32[112,512]{1,0:T(8,128)}, u32[]{:S(2)}) copy-start(f32[112,512]{1,0:T(8,128)} %constant.9.clone.refs_5_.refs_4_.refs_3_) | copy-start | bytes 688132
  293.2 74.1 %copy-start.3 = (bf16[96,1536]{1,0:T(8,128)(2,1)S(1)}, bf16[96,1536]{1,0:T(8,128)(2,1)}, u32[]{:S(2)}) copy-start(bf16[96,1536]{1,0:T(8,128)(2,1)} %get-tuple-element.104.refs_10_) | copy-start | bytes 884740
  293.2 74.1 %copy-start.4 = (bf16[96,1408]{1,0:T(8,128)(2,1)S(1)}, bf16[96,1408]{1,0:T(8,128)(2,1)}, u32[]{:S(2)}) copy-start(bf16[96,1408]{1,0:T(8,128)(2,1)} %get-tuple-element.105.refs_11_) | copy-start | bytes 811012
  293.2 74.1 %copy-start.5 = (bf16[128,768]{1,0:T(8,128)(2,1)S(1)}, bf16[128,768]{1,0:T(8,128)(2,1)}, u32[]{:S(2)}) copy-start(bf16[128,768]{1,0:T(8,128)(2,1)} %get-tuple-element.72.refs_0_) | copy-start | bytes 589828
  367.3 1.2 copy-start.1
  368.5 1.0 copy-start.2
  369.6 0.9 copy-start.6
  370.5 0.8 copy-start.7
  371.3 0.8 copy-start.8
  372.0 0.7 copy-start.9
  372.7 0.7 copy-start.10
  373.4 0.7 copy-start.11

commit v6 on v5

--- a/solution.py
+++ b/solution.py
@@ -315,41 +315,43 @@
 
 
 class LineSum:
-    def __init__(self, count, me, chunks, spacing, number, p_ref, out_ref, buffers, sems):
+    def __init__(self, count, me, chunks, spacing, first, sums, parts, outs, buffers, sems):
         self.count, self.me, self.chunks, self.spacing = count, me, chunks, spacing
-        self.number, self.p_ref, self.out_ref = number, p_ref, out_ref
+        self.first, self.messages, self.parts, self.outs = first, sums * chunks, parts, outs
         self.buffers, self.sems = buffers, sems
-        self.steps = chunks + spacing * (count - 1)
-
-    def place(self, right, chunk):
-        count, me, number = self.count, self.me, self.number
-        lag = me if right else count - 1 - me
-        rows = self.p_ref.shape[0] // self.chunks
-        tile = pl.ds(pl.multiple_of(chunk * rows, rows), rows)
+        self.fill = spacing * (count - 1)
+
+    def tile(self, number, size=1):
+        rows = self.parts.shape[1] // self.chunks * size
+        return pl.ds(pl.multiple_of(number % self.chunks // size * rows, rows), rows)
+
+    def place(self, right, number):
+        count, me = self.count, self.me
+        k, chunk, tile = self.first + number // self.chunks, number % self.chunks, self.tile(number)
         buf = self.buffers[0 if right else 1]
         send, recv = self.sems[:2] if right else self.sems[2:]
         to = jnp.minimum(me + 1, count - 1) if right else jnp.maximum(me - 1, 0)
         first, passed = [
             functools.partial(
                 pltpu.make_async_remote_copy,
-                src_ref=src,
-                dst_ref=buf.at[number, tile],
-                send_sem=send.at[number, chunk],
-                recv_sem=recv.at[number, chunk],
+                src_ref=src.at[k, tile],
+                dst_ref=buf.at[k, tile],
+                send_sem=send.at[k, chunk],
+                recv_sem=recv.at[k, chunk],
                 device_id={"tensor": to},
                 device_id_type=MESH,
             )
-            for src in (self.p_ref.at[tile], buf.at[number, tile])
+            for src in (self.parts, buf)
         ]
-        return lag, tile, buf, first, passed
+        return k, tile, buf, first, passed
 
     def step(self, step):
         for right in (True, False):
             lag = self.me if right else self.count - 1 - self.me
-            chunk = step - self.spacing * lag
-            here = (chunk >= 0) & (chunk < self.chunks)
-            chunk = jnp.clip(chunk, 0, self.chunks - 1)
-            lag, tile, buf, first, passed = self.place(right, chunk)
+            number = step - self.spacing * lag
+            here = (number >= 0) & (number < self.messages)
+            number = jnp.clip(number, 0, self.messages - 1)
+            k, tile, buf, first, passed = self.place(right, number)
 
             @pl.when(here & (lag == 0))
             def start():
@@ -358,19 +360,20 @@
             @pl.when(here & (lag > 0))
             def middle():
                 first().wait_recv()
-                got = buf[self.number, tile, :].astype(f32)
+                got = buf[k, tile, :].astype(f32)
 
                 @pl.when(lag < self.count - 1)
                 def forward():
-                    buf[self.number, tile, :] = (got + self.p_ref[tile, :].astype(f32)).astype(bf16)
+                    buf[k, tile, :] = (got + self.parts[k, tile, :].astype(f32)).astype(bf16)
                     passed().start()
 
-                self.out_ref[tile, :] += got
+                self.outs[k, tile, :] += got
 
     def drain(self):
-        def one(chunk, carry):
+        def one(number, carry):
             for right in (True, False):
-                lag, tile, buf, first, passed = self.place(right, chunk)
+                lag = self.me if right else self.count - 1 - self.me
+                k, tile, buf, first, passed = self.place(right, number)
 
                 @pl.when(lag < self.count - 1)
                 def sent():
@@ -378,25 +381,29 @@
 
             return carry
 
-        lax.fori_loop(0, self.chunks, one, 0)
-
-    def run(self, done, extra=()):
-        rows = self.p_ref.shape[0] // self.chunks
-        fill = self.spacing * (self.count - 1)
+        lax.fori_loop(0, self.messages, one, 0)
+
+    def run(self, done, after, extra):
+        size = self.chunks // 4
 
         def one(step, carry):
             self.step(step)
-            for k, work in enumerate(extra):
+            for k, work in extra.items():
                 pl.when(step == k)(work)
-
-            @pl.when(step >= fill)
-            def finish():
-                chunk = jnp.maximum(step - fill, 0)
-                done(pl.ds(pl.multiple_of(chunk * rows, rows), rows))
+            number = step - self.fill
+            for k in range(len(done)):
+
+                @pl.when((number >= k * self.chunks) & (number < (k + 1) * self.chunks))
+                def finish():
+                    done[k](self.tile(jnp.maximum(number, 0)))
+
+                    @pl.when(number % size == size - 1)
+                    def quarter():
+                        after[k](self.tile(jnp.maximum(number, 0), size))
 
             return carry
 
-        lax.fori_loop(0, self.steps, one, 0)
+        lax.fori_loop(0, self.messages + self.fill, one, 0)
         self.drain()
 
 
@@ -428,13 +435,13 @@
     top_ref, pw_ref, qw_ref, ow_ref, uw_ref, dw_ref = refs[:6]
     bias_refs, norm_refs, qv_ref, og_ref, len_ref = refs[6:10], refs[10:12], *refs[12:15]
     enc_ref, dh2_ref, tra_ref, trb_ref, sums_ref, qsum_ref, vec_ref, qb_ref = refs[15:23]
-    (emb, inp, midpre, mid, fin, slope, dmid, din, sent, sent_mid, act, d_two, d_up, d_branch,
-     d_emb, qkv, attended, probs, d_heads, d_proj, part, grad_all, enc_all, from_left,
-     from_right) = refs[23:48]
-    line_sems, gather_sems = refs[48:52], refs[52:56]
+    (inp, mid, slope, sent, sent_mid, act, d_two, d_up, d_branch, d_emb, qkv, attended, probs,
+     d_heads, d_proj, grad_all, enc_all, outs, parts, from_left, from_right) = refs[23:44]
+    line_sems, gather_sems = refs[44:48], refs[48:52]
+    emb, midpre, fin, dmid, din = [outs.at[k] for k in range(5)]
     me = lax.axis_index("tensor")
     line_greet(me, count)
-    words, features = emb.shape
+    words, features = inp.shape
     heads = attended.shape[1] // HEAD_DIM
     hidden = heads * HEAD_DIM
     scale = HEAD_DIM ** (-0.5)
@@ -453,9 +460,9 @@
     qb_ref[:, 2 * hidden : 3 * hidden] = ends[1:2]
     live = lax.broadcasted_iota(jnp.int32, (1, words), 1) < len_ref[0]
 
-    def line(number, out_ref):
+    def line(first, sums):
         return LineSum(
-            count, me, chunks, spacing, number, part, out_ref, (from_left, from_right), line_sems
+            count, me, chunks, spacing, first, sums, parts, outs, (from_left, from_right), line_sems
         )
 
     def gather_view(block, chunk):
@@ -468,13 +475,13 @@
 
         lax.fori_loop(0, words // size, one, 0)
 
-    def send_product(lhs, rhs, side, out_ref):
+    def product(lhs, rhs, side, k):
         def work(tile):
             value = dot(lhs[tile, :], rhs[...], 1, side).astype(bf16)
-            part[tile, :] = value
-            out_ref[tile, :] = value.astype(f32)
-
-        tiles(256, work)
+            parts[k, tile, :] = value
+            outs[k, tile, :] = value.astype(f32)
+
+        return work
 
     def grads(lhs, rhs, out_ref, lane):
         def half(k):
@@ -498,7 +505,7 @@
     def add_sum(index, value):
         sums_ref[index : index + 1, :] += column_sum(value)
 
-    send_product(top_ref, pw_ref, 0, emb)
+    tiles(256, product(top_ref, pw_ref, 0, 0))
     line_meet(me, count)
 
     def first_norm(tile):
@@ -508,13 +515,11 @@
         inp[tile, :] = value
         sent[tile, :] = value.astype(bf16)
 
-    line(0, emb).run(first_norm)
-
     def project(tile):
         qkv[tile, :] = (dot(sent[tile, :], qw_ref[...], 1, 1) + qb_ref[...]).astype(bf16)
 
+    line(0, 1).run([first_norm], [project], {})
     gather_step(gather_view, 0, 1, me, count, gather_sems)
-    tiles(256, project)
 
     for head in range(heads):
         lanes = slice(head * HEAD_DIM, (head + 1) * HEAD_DIM)
@@ -532,7 +537,7 @@
         tiles(128, attend)
         if head == heads - 2:
             gather_step(gather_view, 1, 1, me, count, gather_sems)
-    send_product(attended, ow_ref, 0, midpre)
+    tiles(256, product(attended, ow_ref, 0, 1))
 
     def pass_grads():
         for step in range(2, count - 1):
@@ -545,16 +550,15 @@
         mid[tile, :] = value
         sent_mid[tile, :] = value.astype(bf16)
 
-    line(1, midpre).run(second_norm, [lambda: None, lambda: None, pass_grads])
-    gather_step(gather_view, count - 1, 1, me, count, gather_sems)
+
+    send_down = product(act, dw_ref, 0, 2)
+    send_up = product(d_up, uw_ref, 1, 3)
 
     def feed(tile):
         value, back = gelu_parts(dot(sent_mid[tile, :], uw_ref[...], 1, 0) + row(9))
         act[tile, :] = value.astype(bf16)
         slope[tile, :] = back
-
-    tiles(128, feed)
-    send_product(act, dw_ref, 0, fin)
+        send_down(tile)
 
     def third_norm(tile):
         value = fin[tile, :] + mid[tile, :] + row(2)
@@ -568,16 +572,12 @@
         add_sum(5, gain)
         add_sum(8, cotangent)
 
-    line(2, fin).run(third_norm)
-    enc_ref[...] = enc_all[own_tile, :]
-
     def feed_back(tile):
         value = (dot(d_two[tile, :], dw_ref[...], 1, 1) * slope[tile, :]).astype(bf16)
         d_up[tile, :] = value
         add_sum(9, value.astype(f32))
-
-    tiles(128, feed_back)
-    send_product(d_up, uw_ref, 1, dmid)
+        send_up(tile)
+
     def second_back(tile):
         cotangent = dmid[tile, :] + fin[tile, :]
         back, gain = norm_back(midpre[tile, :], row(4), cotangent)
@@ -588,13 +588,20 @@
         add_sum(4, gain)
         add_sum(7, cotangent)
 
-    work = grads(d_two, act, tra_ref, features) + grads(sent_mid, d_up, tra_ref, 0)
-    line(3, dmid).run(second_back, work)
-
     def heads_back(tile):
         d_heads[tile, :] = dot(d_branch[tile, :], ow_ref[...], 1, 1).astype(bf16)
 
-    tiles(256, heads_back)
+    extra = {2: pass_grads}
+    extra[chunks + 4] = lambda: gather_step(
+        gather_view, count - 1, 1, me, count, gather_sems
+    )
+    work = grads(d_two, act, tra_ref, features) + grads(sent_mid, d_up, tra_ref, 0)
+    extra.update({2 * chunks + spacing * (count - 1) + k: w for k, w in enumerate(work)})
+    line(1, 3).run(
+        [second_norm, third_norm, second_back], [feed, feed_back, heads_back], extra
+    )
+    enc_ref[...] = enc_all[own_tile, :]
+
     for head in range(heads):
         lanes = slice(head * HEAD_DIM, (head + 1) * HEAD_DIM)
         keys = slice(hidden + head * HEAD_DIM, hidden + (head + 1) * HEAD_DIM)
@@ -607,7 +614,7 @@
         d_scores = (weights * (d_probs - inner)).astype(bf16)
         d_proj[:, lanes] = (dot(d_scores, qkv[:, keys], 1, 0) * scale).astype(bf16)
         d_proj[:, keys] = (dot(d_scores, qkv[:, lanes], 0, 0) * scale).astype(bf16)
-    send_product(d_proj, qw_ref, 0, din)
+    tiles(256, product(d_proj, qw_ref, 0, 4))
     qsum_ref[...] = column_sum(d_proj[...].astype(f32))
 
     def first_back(tile):
@@ -619,14 +626,12 @@
         add_sum(3, gain)
         add_sum(6, cotangent)
 
+    def last(tile):
+        dh2_ref[tile, :] = dot(d_emb[tile, :], pw_ref[...], 1, 1)
+
     work = grads(sent, d_proj, trb_ref, top_ref.shape[1])
     work += grads(d_branch, attended, trb_ref, 1152)
-    line(4, din).run(first_back, work)
-
-    def last(tile):
-        dh2_ref[tile, :] = dot(d_emb[tile, :], pw_ref[...], 1, 1)
-
-    tiles(256, last)
+    line(4, 1).run([first_back], [last], dict(enumerate(work)))
     for work in grads(d_emb, top_ref, trb_ref, 0):
         work()
     gather_drain(gather_view, 1, me, count, gather_sems)
@@ -638,18 +643,20 @@
     three = weights[1].shape[0]
     units = weights[3].shape[1]
     hidden = three // 3
-    chunks, spacing = 16, 4
+    chunks = 16
+    spacing = (chunks - chunks // 4) // (count - 1)
     shape = jax.ShapeDtypeStruct
     rows = features // 8
     scratch = [pltpu.VMEM((16, features), f32), pltpu.VMEM((1, three), f32)]
-    scratch += [pltpu.VMEM((words, n), f32) for n in [features] * 5 + [units] + [features] * 2]
+    scratch += [pltpu.VMEM((words, n), f32) for n in (features, features, units)]
     scratch += [
         pltpu.VMEM((words, n), bf16)
         for n in (features, features, units, features, units, features, features, three, hidden)
     ]
     scratch += [pltpu.VMEM((hidden // HEAD_DIM, words, words), f32)]
-    scratch += [pltpu.VMEM((words, n), bf16) for n in (hidden, three, features, features, features)]
-    scratch += [pltpu.VMEM((5, words, features), bf16)] * 2
+    scratch += [pltpu.VMEM((words, n), bf16) for n in (hidden, three, features, features)]
+    scratch += [pltpu.VMEM((5, words, features), f32)]
+    scratch += [pltpu.VMEM((5, words, features), bf16)] * 3
     scratch += [DMA((5, chunks))] * 4 + [DMA((count, 1))] * 4
     return pl.pallas_call(
         functools.partial(encoder_kernel, count, chunks, spacing),
@@ -1461,9 +1468,19 @@
 
 
 def finish_kernel(units, three, *refs):
-    (enc, table, conv_w, mask, conv_b, hw, hw_b, rows, qv, up_b, tr_a, tr_b) = refs[:12]
     (enc_out, table_out, conv_w_out, conv_b_out, hw_out, hw_b_out, proj_out, proj_b_out, gain_out,
-     shift_out, qkv_out, qv_out, o_out, o_b_out, up_out, up_b_out, down_out, down_b_out) = refs[12:]
+     shift_out, qkv_out, qv_out, o_out, o_b_out, up_out, up_b_out, down_out,
+     down_b_out) = refs[12:30]
+    bufs, sem = refs[30:42], refs[42]
+    loads = [
+        pltpu.make_async_copy(src, dst, sem.at[k])
+        for k, (src, dst) in enumerate(zip(refs[:12], bufs))
+    ]
+    for copy in loads:
+        copy.start()
+    for copy in loads:
+        copy.wait()
+    (enc, table, conv_w, mask, conv_b, hw, hw_b, rows, qv, up_b, tr_a, tr_b) = bufs
     filters = mask.shape[1]
     enc_out[0] = enc[...]
     table_out[...] = table[...].T[:, 0 : table_out.shape[1]]
@@ -1500,6 +1517,7 @@
         (3, depth, three // 3), qv.shape, (three // 3, depth), (features,), (depth, units),
         (up_b.shape[1],), (depth, tr_a.shape[1] - units), (features,),
     ]
+    operands = (encoded, table, conv_w, mask, conv_b, hw, hw_b, rows, qv, up_b, tr_a, tr_b)
     (encoded, table, conv_w, conv_b, hw, hw_b, proj, proj_b, gain, shift, qkv, qv, o, o_b, up, up_b,
      down, down_b) = pl.pallas_call(
         functools.partial(finish_kernel, units, three),
@@ -1507,11 +1525,12 @@
             [jax.ShapeDtypeStruct((1,) + encoded.shape, bf16)]
             + [jax.ShapeDtypeStruct(shape, f32) for shape in shapes]
         ),
-        in_specs=[VMEM] * 12,
+        in_specs=[ANY] * 12,
         out_specs=(VMEM,) * 18,
-        compiler_params=pltpu.CompilerParams(vmem_limit_bytes=32 * MIB),
+        scratch_shapes=[pltpu.VMEM(part.shape, part.dtype) for part in operands] + [DMA((12,))],
+        compiler_params=pltpu.CompilerParams(vmem_limit_bytes=58 * MIB),
         name="finish",
-    )(encoded, table, conv_w, mask, conv_b, hw, hw_b, rows, qv, up_b, tr_a, tr_b)
+    )(*operands)
     return (
         jnp.transpose(encoded, (1, 0, 2)), table.T, conv_w, conv_b, hw, hw_b, proj.T, proj_b, gain,
         shift, jnp.transpose(qkv, (1, 0, 2)), qv, o, o_b, up, up_b, down.T, down_b,

time: 377 us -> 354 us (0.939)
  Pallas kernels: 366 us -> 351 us
  local copies, waits for them, and re-layouts: 8.88 us -> 2.07 us
    pallas_call x1, Pallas kernels: 141 us -> 127 us  [encoder(): pl.pallas_call(functools.partial(encoder_kernel, count, chunks, spacing),...]
    unnamed x25 -> x1, local copies, waits for them, and re-layouts: 7.83 us -> 1.02 us
    pallas_call x1, Pallas kernels: 60.6 us -> 56.6 us  [highway_back(): pl.pallas_call(functools.partial(highway_back_kernel, count, chunks, redu...]
where the time goes in v6:
time: 354 us
  Pallas kernels  351 us (99%)
    pallas_call x1, Pallas kernels, encoder(): pl.pallas_call(functools.partial(encoder_kernel, count, chunks, spacing),...  127 us
    pallas_call x1, Pallas kernels, embed_forward(): pl.pallas_call(functools.partial(embed_forward_kernel, count, chars), out...  88.1 us
    pallas_call x1, Pallas kernels, conv_backward(): pl.pallas_call(functools.partial(conv_backward_kernel, count, chars, cuts...  74.5 us
    pallas_call x1, Pallas kernels, highway_back(): pl.pallas_call(functools.partial(highway_back_kernel, count, chunks, redu...  56.6 us

profile of v6, /device:TPU:1, one launch (start us, length us, event | category | flops | bytes accessed | tf_op | source)
XLA Modules:
  0.0 354.2 jit_solution(12838498346493739174)
XLA Ops:
  1.3 1.0 copy.43
  2.3 0.2 copy.44
  2.6 0.8 reshape.42.refs_0_
  3.4 88.1 %embed_forward.1 = (f32[512,512]{1,0:T(8,128)}, bf16[512,2048]{1,0:T(8,128)(2,1)}, bf16[512,2048]{1,0:T(8,128)(2,1)}, bf16[512,512]{1,0:T(8,128)(2,1)}, bf16[16,...) custom-call(s32[16,1600]{1,0:T(8,128)} %reshape.42.refs_0_, ...), custom_call_target="tpu_custom_call" | custom-call | tf_op jit(solution)/shard_map/embed_forward/pallas_call | solution.py:286
  91.5 127.3 %encoder.1 = (bf16[128,768]{1,0:T(8,128)(2,1)}, f32[512,512]{1,0:T(8,128)}, bf16[2,2,2,96,1536]{4,3,2,1,0:T(8,128)(2,1)}, bf16[2,2,2,96,1408]{4,3,2,1,0:T(8,128)...) custom-call(bf16[512,512]{1,0:T(8,128)(2,1)} %get-tuple-element.71.refs_0_, bf16[512,768]{1,0:T(8,128)(2,1)} %refs_1_.1, ...), custom_call_target="tpu_custom_call" | custom-call | tf_op jit(solution)/shard_map/encoder/pallas_call | solution.py:661
  218.7 56.6 %highway_back.1 = (bf16[512,2048]{1,0:T(8,128)(2,1)}, f32[512,512]{1,0:T(8,128)}, bf16[512,512]{1,0:T(8,128)(2,1)}, bf16[512,512]{1,0:T(8,128)(2,1)}, f32[4,512]...) custom-call(f32[512,512]{1,0:T(8,128)} %get-tuple-element.76.refs_0_, ...), custom_call_target="tpu_custom_call" | custom-call | tf_op jit(solution)/shard_map/highway_back/pallas_call | solution.py:1064
  275.3 74.5 %conv_backward.1 = (bf16[2,2,256,512]{3,2,1,0:T(8,128)(2,1)}, bf16[112,2048]{1,0:T(8,128)(2,1)}, f32[1,2048]{1,0:T(1,128)}, f32[264,16]{1,0:T(8,128)}, f32[4,204...) custom-call(s32[16,1600]{1,0:T(8,128)} %reshape.42.refs_0_, ...), custom_call_target="tpu_custom_call" | custom-call | tf_op jit(solution)/shard_map/conv_backward/pallas_call | solution.py:1414
  349.8 4.1 %finish.1 = (bf16[1,128,768]{2,1,0:T(8,128)(2,1)}, f32[16,262]{1,0:T(8,128)}, f32[112,2048]{1,0:T(8,128)}, f32[2048]{0:T(1024)}, f32[2,2,256,512]{3,2,1,0:T(8,12...) custom-call(bf16[128,768]{1,0:T(8,128)(2,1)} %get-tuple-element.72.r, ...), custom_call_target="tpu_custom_call" | custom-call | tf_op jit(solution)/shard_map/finish/pallas_call | solution.py:1522

commit v7 on v6

--- a/solution.py
+++ b/solution.py
@@ -118,18 +118,18 @@
 def embed_forward_kernel(count, chars, *refs):
     (ids_ref, chars_ref, pattern_ref, cw_ref, cb_ref, mask_ref, ends_ref, off_ref, bias_ref,
      hw_hbm) = refs[:10]
-    log_ref, whole0_ref, whole1_ref, top_ref, x_hbm, p_hbm = refs[10:16]
+    log_out, whole0_out, whole1_ref, top_ref, x_hbm, p_hbm = refs[10:16]
     kept = refs[16:22]
     y_buf, x_buf, p_buf, hw_ref, table_ref, w_ref, hb_ref, keep_sem, late_sem = refs[22:31]
     bufs = refs[31:37]
     sems0, sems1 = refs[37:41], refs[41:45]
+    log_ref, whole0_ref = refs[45:47]
     t_refs, g_refs, h_refs = (bufs[0], bufs[3]), (bufs[1], bufs[4]), (bufs[2], bufs[5])
     wholes = (whole0_ref, whole1_ref)
     me = lax.axis_index("tensor")
     line_greet(me, count)
     words, filters = log_ref.shape
     tiles = words // WORD_TILE
-    half = words // 2
     padded = ids_ref.shape[1] // WORD_TILE
     own = pl.ds(pl.multiple_of(me * filters, filters), filters)
     loads = [
@@ -142,6 +142,8 @@
         pltpu.make_async_copy(buf, out, late_sem.at[2 + k])
         for k, (buf, out) in enumerate(zip(bufs, kept))
     ]
+    logs_copy = pltpu.make_async_copy(log_ref, log_out, late_sem.at[8])
+    whole_copy = pltpu.make_async_copy(whole0_ref, whole0_out, late_sem.at[9])
     y_buf[...] = jnp.zeros_like(y_buf)
     table_ref[...] = jnp.zeros_like(table_ref)
     depth, vocab_size = chars_ref.shape
@@ -174,7 +176,7 @@
             for k, (buf, hbm) in enumerate(((x_buf, x_hbm), (p_buf, p_hbm)))
         ]
 
-    group = lax.broadcasted_iota(jnp.int32, (1, WORD_TILE, LANES), 2) // 16
+    lane_group = lax.broadcasted_iota(jnp.int32, (1, WORD_TILE, LANES), 2) // 16
     vocab = lax.broadcasted_iota(jnp.int32, (table_ref.shape[1], padded * WORD_TILE), 0)
 
     def tile_step(index):
@@ -188,9 +190,9 @@
         one_hot = jnp.where(vocab == ids_ref[pl.ds(index, 1), :], 1.0, 0.0).astype(bf16)
         found = dot(table_ref[...], one_hot, 1, 0).astype(bf16).T
         y_buf[0:padded] = found.reshape(padded, WORD_TILE, LANES)
-        value = jnp.where(group == 7, pattern_ref[...], y_buf[0:chars])
+        value = jnp.where(lane_group == 7, pattern_ref[...], y_buf[0:chars])
         for tap in range(1, 7):
-            value = jnp.where(group == tap, y_buf[tap : chars + tap], value)
+            value = jnp.where(lane_group == tap, y_buf[tap : chars + tap], value)
         x2 = value.reshape(chars * WORD_TILE, LANES)
         x_buf[slot] = x2
         conv = dot(x2, w_ref[...], 1, 0).reshape(chars, WORD_TILE, filters)
@@ -208,14 +210,18 @@
         h_refs[0][tile, :] = hidden
         whole0_ref[tile, own] = hidden.astype(bf16)
 
-    def layer_step(layer, part):
-        rows = slice(part * half, (part + 1) * half)
+    size = words // 4
+    group = tiles // 4
+
+    def layer_step(layer, quarter):
+        start = quarter * size
+        rows = pl.ds(pl.multiple_of(start, size), size)
         for j, out in enumerate((t_refs[layer], g_refs[layer])):
             bias = hb_ref[2 * layer + j : 2 * layer + j + 1, :]
             out[rows, :] = dot(wholes[layer][rows, :], hw_ref[layer, j], 1, 0) + bias
 
         def mix(index, carry):
-            tile = pl.ds(pl.multiple_of(part * half + index * WORD_TILE, WORD_TILE), WORD_TILE)
+            tile = pl.ds(pl.multiple_of(start + index * WORD_TILE, WORD_TILE), WORD_TILE)
             trans = t_refs[layer][tile, :]
             gate = jax.nn.sigmoid(g_refs[layer][tile, :])
             hidden = gate * (trans * jax.nn.sigmoid(trans)) + (1.0 - gate) * h_refs[layer][tile, :]
@@ -226,11 +232,11 @@
                 top_ref[tile, :] = hidden.astype(bf16)
             return carry
 
-        lax.fori_loop(0, half // WORD_TILE, mix, 0)
+        lax.fori_loop(0, size // WORD_TILE, mix, 0)
 
     spacing = 2
     fill = spacing * (count - 1)
-    shift = tiles // 2 + fill
+    shift = group + fill
     last = shift + tiles + fill
 
     def step_fn(step, carry):
@@ -243,29 +249,37 @@
             gather_step(views[0], step, tiles, me, count, sems0, spacing)
 
         @pl.when(step == shift)
-        def first_half():
+        def weights0():
             loads[0].wait()
-            layer_step(0, 0)
-
-        @pl.when(step == shift + tiles // 2)
-        def second_half():
-            layer_step(0, 1)
-            for copy in stores[:3]:
+
+        since = step - shift
+
+        @pl.when((since >= 0) & (since < tiles) & (since % group == 0))
+        def layer0():
+            layer_step(0, jnp.maximum(since, 0) // group)
+
+        @pl.when(since == tiles - group)
+        def leave():
+            for copy in stores[:3] + [logs_copy, whole_copy]:
                 copy.start()
 
         @pl.when(step >= shift)
         def second_gather():
             gather_step(views[1], step - shift, tiles, me, count, sems1, spacing)
 
-        @pl.when(step == 2 * shift - 1)
-        def third_half():
+        since = step - shift - fill - group + 1
+
+        @pl.when(since == 0)
+        def weights1():
             loads[1].wait()
-            layer_step(1, 0)
+
+        @pl.when((since >= 0) & (since % group == 0))
+        def layer1():
+            layer_step(1, jnp.maximum(since, 0) // group)
 
         return carry
 
     lax.fori_loop(0, last, step_fn, 0)
-    layer_step(1, 1)
     for copy in stores[3:]:
         copy.start()
     for index in (tiles - 2, tiles - 1):
@@ -273,7 +287,7 @@
             copy.wait()
     for sems, view in zip((sems0, sems1), views):
         gather_drain(view, tiles, me, count, sems)
-    for copy in stores:
+    for copy in stores + [logs_copy, whole_copy]:
         copy.wait()
 
 
@@ -295,7 +309,7 @@
         )
         + (shape(flat, f32),) * 6,
         in_specs=[VMEM] * 9 + [ANY],
-        out_specs=(VMEM,) * 4 + (ANY,) * 8,
+        out_specs=(ANY, ANY, VMEM, VMEM) + (ANY,) * 8,
         scratch_shapes=[
             pltpu.VMEM((chars + 6, WORD_TILE, LANES), bf16),
             pltpu.VMEM((2, chars * WORD_TILE, LANES), bf16),
@@ -305,10 +319,11 @@
             pltpu.VMEM((LANES, filters), bf16),
             pltpu.VMEM((8, filters), f32),
             DMA((2, 2)),
-            DMA((8,)),
+            DMA((10,)),
         ]
         + [pltpu.VMEM(flat, f32)] * 6
-        + [DMA((count, tiles))] * 8,
+        + [DMA((count, tiles))] * 8
+        + [pltpu.VMEM(flat, f32), pltpu.VMEM((words, count * filters), bf16)],
         compiler_params=params(cid, 58),
         name="embed_forward",
     )(ids, table, pattern, *conv, off, bias, weight)
@@ -383,10 +398,14 @@
 
         lax.fori_loop(0, self.messages, one, 0)
 
-    def run(self, done, after, extra):
+    def run(self, before, done, after, extra):
         size = self.chunks // 4
 
         def one(step, carry):
+            @pl.when((step < self.chunks) & (step % size == 0))
+            def prepare():
+                before(self.tile(jnp.minimum(step, self.chunks - 1), size))
+
             self.step(step)
             for k, work in extra.items():
                 pl.when(step == k)(work)
@@ -431,13 +450,28 @@
     return jnp.sum(values, axis=0, keepdims=True)
 
 
+def mix_back(d_hidden, trans, gate_pre, previous):
+    gate = jax.nn.sigmoid(gate_pre)
+    sig = jax.nn.sigmoid(trans)
+    act = trans * sig
+    d_trans = (d_hidden * gate * (sig * (1.0 + trans * (1.0 - sig)))).astype(bf16)
+    d_gate = (d_hidden * (act - previous) * gate * (1.0 - gate)).astype(bf16)
+    return d_trans, d_gate, (1.0 - gate) * d_hidden
+
+
 def encoder_kernel(count, chunks, spacing, *refs):
     top_ref, pw_ref, qw_ref, ow_ref, uw_ref, dw_ref = refs[:6]
     bias_refs, norm_refs, qv_ref, og_ref, len_ref = refs[6:10], refs[10:12], *refs[12:15]
-    enc_ref, dh2_ref, tra_ref, trb_ref, sums_ref, qsum_ref, vec_ref, qb_ref = refs[15:23]
+    mix_refs = refs[15:18]
+    refs = refs[3:]
+    enc_ref, prev_ref, dt_ref, dg_ref, mix_sums = refs[15:20]
+    refs = refs[3:]
+    tra_out, trb_ref, sums_ref, qsum_ref, vec_ref, qb_ref = refs[17:23]
     (inp, mid, slope, sent, sent_mid, act, d_two, d_up, d_branch, d_emb, qkv, attended, probs,
      d_heads, d_proj, grad_all, enc_all, outs, parts, from_left, from_right) = refs[23:44]
     line_sems, gather_sems = refs[44:48], refs[48:52]
+    tra_ref, tra_sem = refs[52:54]
+    tra_copy = pltpu.make_async_copy(tra_ref, tra_out, tra_sem)
     emb, midpre, fin, dmid, din = [outs.at[k] for k in range(5)]
     me = lax.axis_index("tensor")
     line_greet(me, count)
@@ -449,6 +483,7 @@
     own_tile = pl.ds(pl.multiple_of(me * own, own), own)
     grad_all[own_tile, :] = og_ref[...]
     sums_ref[...] = jnp.zeros_like(sums_ref)
+    mix_sums[...] = jnp.zeros_like(mix_sums)
     trb_ref[...] = jnp.zeros_like(trb_ref)
     for k, bias_ref in zip((0, 1, 2, 9), bias_refs):
         vec_ref[k : k + 1, :] = bias_ref[...].astype(f32).reshape(1, features)
@@ -505,7 +540,6 @@
     def add_sum(index, value):
         sums_ref[index : index + 1, :] += column_sum(value)
 
-    tiles(256, product(top_ref, pw_ref, 0, 0))
     line_meet(me, count)
 
     def first_norm(tile):
@@ -518,7 +552,7 @@
     def project(tile):
         qkv[tile, :] = (dot(sent[tile, :], qw_ref[...], 1, 1) + qb_ref[...]).astype(bf16)
 
-    line(0, 1).run([first_norm], [project], {})
+    line(0, 1).run(product(top_ref, pw_ref, 0, 0), [first_norm], [project], {})
     gather_step(gather_view, 0, 1, me, count, gather_sems)
 
     for head in range(heads):
@@ -530,14 +564,13 @@
             scores = dot(qkv[tile, lanes], qkv[:, keys], 1, 1) * scale
             scores = jnp.where(live, scores, big_neg)
             exps = jnp.exp(scores - jnp.max(scores, axis=1, keepdims=True))
-            value = exps / jnp.sum(exps, axis=1, keepdims=True)
+            value = exps * (1.0 / jnp.sum(exps, axis=1, keepdims=True))
             probs[head, tile, :] = value
             attended[tile, lanes] = dot(value.astype(bf16), qkv[:, vals], 1, 0).astype(bf16)
 
-        tiles(128, attend)
+        tiles(256, attend)
         if head == heads - 2:
             gather_step(gather_view, 1, 1, me, count, gather_sems)
-    tiles(256, product(attended, ow_ref, 0, 1))
 
     def pass_grads():
         for step in range(2, count - 1):
@@ -598,8 +631,10 @@
     work = grads(d_two, act, tra_ref, features) + grads(sent_mid, d_up, tra_ref, 0)
     extra.update({2 * chunks + spacing * (count - 1) + k: w for k, w in enumerate(work)})
     line(1, 3).run(
+        product(attended, ow_ref, 0, 1),
         [second_norm, third_norm, second_back], [feed, feed_back, heads_back], extra
     )
+    tra_copy.start()
     enc_ref[...] = enc_all[own_tile, :]
 
     for head in range(heads):
@@ -614,7 +649,6 @@
         d_scores = (weights * (d_probs - inner)).astype(bf16)
         d_proj[:, lanes] = (dot(d_scores, qkv[:, keys], 1, 0) * scale).astype(bf16)
         d_proj[:, keys] = (dot(d_scores, qkv[:, lanes], 0, 0) * scale).astype(bf16)
-    tiles(256, product(d_proj, qw_ref, 0, 4))
     qsum_ref[...] = column_sum(d_proj[...].astype(f32))
 
     def first_back(tile):
@@ -627,17 +661,25 @@
         add_sum(6, cotangent)
 
     def last(tile):
-        dh2_ref[tile, :] = dot(d_emb[tile, :], pw_ref[...], 1, 1)
+        d_hidden = dot(d_emb[tile, :], pw_ref[...], 1, 1)
+        d_trans, d_gate, prev_ref[tile, :] = mix_back(d_hidden, *[ref[tile, :] for ref in mix_refs])
+        dt_ref[tile, :] = d_trans
+        dg_ref[tile, :] = d_gate
+        mix_sums[0:1, :] += column_sum(d_trans.astype(f32))
+        mix_sums[1:2, :] += column_sum(d_gate.astype(f32))
 
     work = grads(sent, d_proj, trb_ref, top_ref.shape[1])
     work += grads(d_branch, attended, trb_ref, 1152)
-    line(4, 1).run([first_back], [last], dict(enumerate(work)))
+    line(4, 1).run(
+        product(d_proj, qw_ref, 0, 4), [first_back], [last], {5 + k: w for k, w in enumerate(work)}
+    )
     for work in grads(d_emb, top_ref, trb_ref, 0):
         work()
     gather_drain(gather_view, 1, me, count, gather_sems)
-
-
-def encoder(top, weights, biases, out_grad, lengths, count, cid):
+    tra_copy.wait()
+
+
+def encoder(top, weights, biases, out_grad, lengths, mix, count, cid):
     words, filters = top.shape
     features = weights[0].shape[1]
     three = weights[1].shape[0]
@@ -658,22 +700,26 @@
     scratch += [pltpu.VMEM((5, words, features), f32)]
     scratch += [pltpu.VMEM((5, words, features), bf16)] * 3
     scratch += [DMA((5, chunks))] * 4 + [DMA((count, 1))] * 4
+    scratch += [pltpu.VMEM((2, 2, 2, rows, features + units), bf16), DMA]
     return pl.pallas_call(
         functools.partial(encoder_kernel, count, chunks, spacing),
         out_shape=(
             shape((words // count, features), bf16),
             shape((words, filters), f32),
+            shape((words, filters), bf16),
+            shape((words, filters), bf16),
+            shape((2, filters), f32),
             shape((2, 2, 2, rows, features + units), bf16),
             shape((2, 2, 2, rows, 1408), bf16),
             shape((16, features), f32),
             shape((1, three), f32),
         ),
-        in_specs=[VMEM] * 14 + [pl.BlockSpec(memory_space=pltpu.SMEM)],
-        out_specs=(VMEM,) * 6,
+        in_specs=[VMEM] * 14 + [pl.BlockSpec(memory_space=pltpu.SMEM)] + [VMEM] * 3,
+        out_specs=(VMEM,) * 5 + (ANY, VMEM, VMEM, VMEM),
         scratch_shapes=scratch,
         compiler_params=params(cid, 58),
         name="encoder",
-    )(top, *weights, *biases, out_grad, lengths)
+    )(top, *weights, *biases, out_grad, lengths, *mix)
 
 
 class LineScatter:
@@ -831,15 +877,6 @@
     pl.semaphore_wait(pltpu.get_barrier_semaphore(), len(peers))
 
 
-def mix_back(d_hidden, trans, gate_pre, previous):
-    gate = jax.nn.sigmoid(gate_pre)
-    sig = jax.nn.sigmoid(trans)
-    act = trans * sig
-    d_trans = (d_hidden * gate * (sig * (1.0 + trans * (1.0 - sig)))).astype(bf16)
-    d_gate = (d_hidden * (act - previous) * gate * (1.0 - gate)).astype(bf16)
-    return d_trans, d_gate, (1.0 - gate) * d_hidden
-
-
 def weight_grad_piece(piece, whole_ref, d_refs, outs):
     rows = outs[0].shape[-2]
     lanes = pl.ds(pl.multiple_of(piece * rows, rows), rows)
@@ -849,7 +886,7 @@
 
 
 def highway_back_kernel(count, chunks, reduce, *refs):
-    d_h2_ref, t1_ref, g1_ref, h1_ref = refs[:4]
+    prev1_hbm, dt1_ref, dg1_ref, sums1_ref = refs[:4]
     late_hbm = refs[4:9]
     refs = refs[9:]
     if reduce:
@@ -867,11 +904,13 @@
     else:
         hw_refs = refs[:2]
         refs = refs[2:]
-    part1_ref, from_left, from_right, d_h1_ref, dt1_ref, dg1_ref = refs[:6]
-    t0_ref, g0_ref, h0_ref, whole1_ref, w_ref, late_sem = refs[6:12]
-    sems = refs[12:]
+    part1_ref, from_left, from_right, d_h1_ref = refs[:4]
+    t0_ref, g0_ref, h0_ref, whole1_ref, w_ref, late_sem = refs[4:10]
+    sems = refs[10:]
     me = lax.axis_index("tensor")
-    words, filters = d_h2_ref.shape
+    words, filters = dt1_ref.shape
+    prev_load = pltpu.make_async_copy(prev1_hbm, d_h1_ref, late_sem.at[8])
+    prev_load.start()
     w_hbm = late_hbm[4]
     loads = [
         pltpu.make_async_copy(w_hbm.at[1], w_ref.at[1], late_sem.at[0]),
@@ -895,7 +934,8 @@
     ring = [{"tensor": lax.rem(me + k, count)} for k in range(1, count)]
     everyone = (peers if reduce else []) + ring
     greet_all(everyone)
-    sums_ref[...] = jnp.zeros_like(sums_ref)
+    sums_ref[0:2, :] = jnp.zeros_like(sums1_ref)
+    sums_ref[2:4, :] = sums1_ref[...]
 
     def mix(layer, d_h_ref, t_ref, g_ref, h_ref, dt_ref, dg_ref, prev_ref, tile):
         dt, dg, prev = mix_back(d_h_ref[tile, :], t_ref[tile, :], g_ref[tile, :], h_ref[tile, :])
@@ -925,19 +965,15 @@
     def tile_of(index):
         return pl.ds(pl.multiple_of(index * rows, rows), rows)
 
-    def first(index, carry):
-        mix(1, d_h2_ref, t1_ref, g1_ref, h1_ref, dt1_ref, dg1_ref, d_h1_ref, tile_of(index))
-        return carry
-
     def own_part(part):
         tile = slice(part * (words // 2), (part + 1) * (words // 2))
         d_h1_ref[tile, :] += part1_ref[
             tile, pl.ds(pl.multiple_of(me * filters, filters), filters)
         ].astype(f32)
 
-    lax.fori_loop(0, chunks // 2, first, 0)
     loads[0].wait()
     products(1, dt1_ref, dg1_ref, part1_ref, 0)
+    prev_load.wait()
     own_part(0)
     meet_all(everyone)
     if reduce:
@@ -962,7 +998,6 @@
 
         @pl.when(step == 0)
         def rest():
-            lax.fori_loop(chunks // 2, chunks, first, 0)
             products(1, dt1_ref, dg1_ref, part1_ref, 1)
             own_part(1)
             loads[1].wait()
@@ -1025,8 +1060,8 @@
     scatter.drain()
 
 
-def highway_back(d_h2, t1, g1, h1, t0, g0, h0, whole1, weight, tra, trb, count, cid):
-    words, filters = d_h2.shape
+def highway_back(prev1, dt1, dg1, sums1, t0, g0, h0, whole1, weight, tra, trb, count, cid):
+    words, filters = dt1.shape
     chunks = 8
     reduce = tra is not None
     rows = whole1.shape[1] // 8
@@ -1038,8 +1073,8 @@
         shape((words, filters), bf16),
         shape((4, filters), f32),
     ]
-    operands = [d_h2, t1, g1, h1, t0, g0, h0, whole1, weight]
-    in_specs = [VMEM] * 4 + [ANY] * 5
+    operands = [prev1, dt1, dg1, sums1, t0, g0, h0, whole1, weight]
+    in_specs = [ANY] + [VMEM] * 3 + [ANY] * 5
     hw_shape = (2, 2, 2, rows, filters)
     scratch = []
     if reduce:
@@ -1057,9 +1092,8 @@
     else:
         out_shape += [shape(hw_shape, bf16)] * 2
     scratch += [pltpu.VMEM(whole1.shape, bf16)] * 3
-    scratch += [pltpu.VMEM((words, filters), f32)] + [pltpu.VMEM((words, filters), bf16)] * 2
-    scratch += [pltpu.VMEM((words, filters), f32)] * 3
-    scratch += [pltpu.VMEM(whole1.shape, bf16), pltpu.VMEM(weight.shape, bf16), DMA((8,))]
+    scratch += [pltpu.VMEM((words, filters), f32)] * 4
+    scratch += [pltpu.VMEM(whole1.shape, bf16), pltpu.VMEM(weight.shape, bf16), DMA((9,))]
     scratch += [DMA((count, chunks))] * 4
     return pl.pallas_call(
         functools.partial(highway_back_kernel, count, chunks, reduce),
@@ -1081,8 +1115,9 @@
 
     def remote(self, src, dst, phase, hop, axis, peer):
         send, recv = self.sems[2 * phase : 2 * phase + 2]
+        index = (hop - 1,) if phase < 2 else hop
         return pltpu.make_async_remote_copy(
-            src_ref=src, dst_ref=dst, send_sem=send.at[hop - 1], recv_sem=recv.at[hop - 1],
+            src_ref=src, dst_ref=dst, send_sem=send.at[index], recv_sem=recv.at[index],
             device_id={axis: peer}, device_id_type=MESH,
         )
 
@@ -1094,9 +1129,14 @@
         peer = lax.rem(self.me + hop, self.count)
         return self.remote(self.mid.at[self.me], self.mid.at[self.me], 1, hop, "tensor", peer)
 
-    def around(self, hop):
+    def around(self, hop, rank):
         peer = lax.rem(self.place + hop, self.dp_count)
-        return self.remote(self.mid, self.out_ref.at[self.place], 2, hop, "dp", peer)
+        dst = self.out_ref.at[self.place, rank]
+        return self.remote(self.mid.at[rank], dst, 2, (rank, hop - 1), "dp", peer)
+
+    def hand_on(self, rank):
+        self.loop(lambda hop: self.around(hop, rank).start(), self.dp_count)
+        self.out_ref[self.place, rank] = self.mid[rank]
 
     def loop(self, fn, stop):
         def one(hop, carry):
@@ -1118,14 +1158,18 @@
         )
         self.mid[self.me] = total.astype(bf16)
         self.loop(lambda hop: self.across(hop).start(), self.count)
+        self.hand_on(self.me)
 
     def third(self):
-        self.loop(lambda hop: self.across(hop).wait(), self.count)
-        self.loop(lambda hop: self.around(hop).start(), self.dp_count)
-        self.out_ref[self.place] = self.mid[...]
+        def one(hop):
+            self.across(hop).wait()
+            self.hand_on(lax.rem(self.me + self.count - hop, self.count))
+
+        self.loop(one, self.count)
 
     def finish(self):
-        self.loop(lambda hop: self.around(hop).wait(), self.dp_count)
+        for rank in range(self.count):
+            self.loop(lambda hop: self.around(hop, rank).wait(), self.dp_count)
 
 
 def early_parts(rows):
@@ -1394,7 +1438,7 @@
                 pltpu.VMEM((count,) + small, bf16),
                 pltpu.VMEM((8, count) + small, bf16),
             ]
-            scratch += [DMA((7,))] * 2 + [DMA((count - 1,))] * 2 + [DMA((7,))] * 2
+            scratch += [DMA((7,))] * 2 + [DMA((count - 1,))] * 2 + [DMA((count, 7))] * 2
     else:
         out_shape = [shape(shape_of, f32) for shape_of in sums] + [shape(hw_shape, bf16)] * 2
     scratch += [
@@ -1459,8 +1503,8 @@
             DMA((dp_count - 1,)),
             DMA((count - 1,)),
             DMA((count - 1,)),
-            DMA((dp_count - 1,)),
-            DMA((dp_count - 1,)),
+            DMA((count, dp_count - 1)),
+            DMA((count, dp_count - 1)),
         ],
         compiler_params=params(cid, 32),
         name="sum_small",
@@ -1597,7 +1641,7 @@
         chars,
         1,
     )
-    encoded, d_hidden, tr_a, tr_b, row_sums, proj_sums = encoder(
+    encoded, prev1, dt1, dg1, sums1, tr_a, tr_b, row_sums, proj_sums = encoder(
         top,
         (
             proj_weight,
@@ -1609,11 +1653,12 @@
         (proj_bias, out_bias, down_bias, up_bias, norm_gain, norm_shift, qv_bias),
         out_grad[:, 0],
         seq_lengths,
+        (t1, g1, h1),
         count,
         4,
     )
 
-    back_args = (d_hidden, t1, g1, h1, t0, g0, h0, whole1, highway_weight)
+    back_args = (prev1, dt1, dg1, sums1, t0, g0, h0, whole1, highway_weight)
     conv_args = (ids_tiles, x_tiles, p_tiles, conv_weight, mask, off, logs)
     three = 3 * heads * HEAD_DIM
     units = up_weight.shape[1]

time: 354 us -> 350 us (0.989)
  Pallas kernels: 351 us -> 346 us
    pallas_call x1, Pallas kernels: 127 us -> 122 us  [encoder(): pl.pallas_call(functools.partial(encoder_kernel, count, chunks, spacing),...]
where the time goes in v7:
time: 350 us; the launch traced here: 349 us
  Pallas kernels  346 us (99%)
    pallas_call x1, Pallas kernels, encoder(): pl.pallas_call(functools.partial(encoder_kernel, count, chunks, spacing),...  122 us
    pallas_call x1, Pallas kernels, embed_forward(): pl.pallas_call(functools.partial(embed_forward_kernel, count, chars), out...  86.6 us
    pallas_call x1, Pallas kernels, conv_backward(): pl.pallas_call(functools.partial(conv_backward_kernel, count, chars, cuts...  72.3 us
    pallas_call x1, Pallas kernels, highway_back(): pl.pallas_call(functools.partial(highway_back_kernel, count, chunks, redu...  60.1 us

profile of v7, /device:TPU:1, one launch (start us, length us, event | category | flops | bytes accessed | tf_op | source)
XLA Modules:
  0.0 349.1 jit_solution(2741766269523083591)
XLA Ops:
  1.3 1.0 copy.43
  2.3 0.2 copy.44
  2.6 0.8 reshape.42.refs_0_
  3.4 86.6 %embed_forward.1 = (f32[512,512]{1,0:T(8,128)}, bf16[512,2048]{1,0:T(8,128)(2,1)}, bf16[512,2048]{1,0:T(8,128)(2,1)}, bf16[512,512]{1,0:T(8,128)(2,1)}, bf16[16,...) custom-call(s32[16,1600]{1,0:T(8,128)} %reshape.42.refs_0_, ...), custom_call_target="tpu_custom_call" | custom-call | tf_op jit(solution)/shard_map/embed_forward/pallas_call | solution.py:300
  90.0 122.5 %encoder.1 = (bf16[128,768]{1,0:T(8,128)(2,1)}, f32[512,512]{1,0:T(8,128)}, bf16[512,512]{1,0:T(8,128)(2,1)}, bf16[512,512]{1,0:T(8,128)(2,1)}, f32[2,512]{1,0:T...) custom-call(bf16[512,512]{1,0:T(8,128)(2,1)} %get-tuple-element.74.r, ...), custom_call_target="tpu_custom_call" | custom-call | tf_op jit(solution)/shard_map/encoder/pallas_call | solution.py:704
  212.4 60.1 %highway_back.1 = (bf16[512,2048]{1,0:T(8,128)(2,1)}, f32[512,512]{1,0:T(8,128)}, bf16[512,512]{1,0:T(8,128)(2,1)}, bf16[512,512]{1,0:T(8,128)(2,1)}, f32[4,512]...) custom-call(f32[512,512]{1,0:T(8,128)} %get-tuple-element.82.refs_0_, ...), custom_call_target="tpu_custom_call" | custom-call | tf_op jit(solution)/shard_map/highway_back/pallas_call | solution.py:1098
  272.5 72.3 %conv_backward.1 = (bf16[2,2,256,512]{3,2,1,0:T(8,128)(2,1)}, bf16[112,2048]{1,0:T(8,128)(2,1)}, f32[1,2048]{1,0:T(1,128)}, f32[264,16]{1,0:T(8,128)}, f32[4,204...) custom-call(s32[16,1600]{1,0:T(8,128)} %reshape.42.refs_0_, ...), custom_call_target="tpu_custom_call" | custom-call | tf_op jit(solution)/shard_map/conv_backward/pallas_call | solution.py:1458
  344.8 4.1 %finish.1 = (bf16[1,128,768]{2,1,0:T(8,128)(2,1)}, f32[16,262]{1,0:T(8,128)}, f32[112,2048]{1,0:T(8,128)}, f32[2048]{0:T(1024)}, f32[2,2,256,512]{3,2,1,0:T(8,12...) custom-call(bf16[128,768]{1,0:T(8,128)(2,1)} %get-tuple-element.78.r, ...), custom_call_target="tpu_custom_call" | custom-call | tf_op jit(solution)/shard_map/finish/pallas_call | solution.py:1566

commit v8 on v7

--- a/solution.py
+++ b/solution.py
@@ -947,8 +947,8 @@
                 d.astype(f32), axis=0, keepdims=True
             )
 
-    def products(layer, dt_ref, dg_ref, p_ref, part):
-        tile = slice(part * (words // 2), (part + 1) * (words // 2))
+    def products(layer, dt_ref, dg_ref, p_ref, start, size):
+        tile = slice(start, start + size)
 
         def one(block, carry):
             lanes = pl.ds(pl.multiple_of(block * filters, filters), filters)
@@ -965,6 +965,8 @@
     def tile_of(index):
         return pl.ds(pl.multiple_of(index * rows, rows), rows)
 
+    half, quarter = words // 2, words // 4
+
     def own_part(part):
         tile = slice(part * (words // 2), (part + 1) * (words // 2))
         d_h1_ref[tile, :] += part1_ref[
@@ -972,7 +974,7 @@
         ].astype(f32)
 
     loads[0].wait()
-    products(1, dt1_ref, dg1_ref, part1_ref, 0)
+    products(1, dt1_ref, dg1_ref, part1_ref, 0, half)
     prev_load.wait()
     own_part(0)
     meet_all(everyone)
@@ -998,7 +1000,7 @@
 
         @pl.when(step == 0)
         def rest():
-            products(1, dt1_ref, dg1_ref, part1_ref, 1)
+            products(1, dt1_ref, dg1_ref, part1_ref, half, half)
             own_part(1)
             loads[1].wait()
 
@@ -1047,12 +1049,16 @@
 
         @pl.when(step == scatter.due(chunks // 2 - 1) + 1)
         def early():
-            products(0, dt0_ref, dg0_ref, part0_ref, 0)
+            products(0, dt0_ref, dg0_ref, part0_ref, 0, half)
+
+        @pl.when(step == scatter.due(3 * chunks // 4 - 1) + 1)
+        def third_quarter():
+            products(0, dt0_ref, dg0_ref, part0_ref, half, quarter)
 
         return carry
 
     lax.fori_loop(0, scatter.steps, step_fn, 0)
-    products(0, dt0_ref, dg0_ref, part0_ref, 1)
+    products(0, dt0_ref, dg0_ref, part0_ref, half + quarter, quarter)
     for item in items[:2]:
         item.finish1()
     for item, out in zip(items[2:], tr_outs if reduce else ()):

time: 350 us -> 350 us (level)
  no operation moved by 1% of the time
where the time goes in v8:
time: 350 us; the launch traced here: 349 us
  Pallas kernels  346 us (99%)
    pallas_call x1, Pallas kernels, encoder(): pl.pallas_call(functools.partial(encoder_kernel, count, chunks, spacing),...  122 us
    pallas_call x1, Pallas kernels, embed_forward(): pl.pallas_call(functools.partial(embed_forward_kernel, count, chars), out...  86.6 us
    pallas_call x1, Pallas kernels, conv_backward(): pl.pallas_call(functools.partial(conv_backward_kernel, count, chars, cuts...  71.7 us
    pallas_call x1, Pallas kernels, highway_back(): pl.pallas_call(functools.partial(highway_back_kernel, count, chunks, redu...  60.8 us

profile of v8, /device:TPU:1, one launch (start us, length us, event | category | flops | bytes accessed | tf_op | source)
XLA Modules:
  0.0 349.3 jit_solution(8857895072746411399)
XLA Ops:
  1.3 1.0 copy.43
  2.3 0.2 copy.44
  2.6 0.8 reshape.42.refs_0_
  3.4 86.6 %embed_forward.1 = (f32[512,512]{1,0:T(8,128)}, bf16[512,2048]{1,0:T(8,128)(2,1)}, bf16[512,2048]{1,0:T(8,128)(2,1)}, bf16[512,512]{1,0:T(8,128)(2,1)}, bf16[16,...) custom-call(s32[16,1600]{1,0:T(8,128)} %reshape.42.refs_0_, ...), custom_call_target="tpu_custom_call" | custom-call | tf_op jit(solution)/shard_map/embed_forward/pallas_call | solution.py:300
  90.0 122.5 %encoder.1 = (bf16[128,768]{1,0:T(8,128)(2,1)}, f32[512,512]{1,0:T(8,128)}, bf16[512,512]{1,0:T(8,128)(2,1)}, bf16[512,512]{1,0:T(8,128)(2,1)}, f32[2,512]{1,0:T...) custom-call(bf16[512,512]{1,0:T(8,128)(2,1)} %get-tuple-element.74.r, ...), custom_call_target="tpu_custom_call" | custom-call | tf_op jit(solution)/shard_map/encoder/pallas_call | solution.py:704
  212.4 60.8 %highway_back.1 = (bf16[512,2048]{1,0:T(8,128)(2,1)}, f32[512,512]{1,0:T(8,128)}, bf16[512,512]{1,0:T(8,128)(2,1)}, bf16[512,512]{1,0:T(8,128)(2,1)}, f32[4,512]...) custom-call(f32[512,512]{1,0:T(8,128)} %get-tuple-element.82.refs_0_, ...), custom_call_target="tpu_custom_call" | custom-call | tf_op jit(solution)/shard_map/highway_back/pallas_call | solution.py:1104
  273.3 71.7 %conv_backward.1 = (bf16[2,2,256,512]{3,2,1,0:T(8,128)(2,1)}, bf16[112,2048]{1,0:T(8,128)(2,1)}, f32[1,2048]{1,0:T(1,128)}, f32[264,16]{1,0:T(8,128)}, f32[4,204...) custom-call(s32[16,1600]{1,0:T(8,128)} %reshape.42.refs_0_, ...), custom_call_target="tpu_custom_call" | custom-call | tf_op jit(solution)/shard_map/conv_backward/pallas_call | solution.py:1464
  345.0 4.1 %finish.1 = (bf16[1,128,768]{2,1,0:T(8,128)(2,1)}, f32[16,262]{1,0:T(8,128)}, f32[112,2048]{1,0:T(8,128)}, f32[2048]{0:T(1024)}, f32[2,2,256,512]{3,2,1,0:T(8,12...) custom-call(bf16[128,768]{1,0:T(8,128)(2,1)} %get-tuple-element.78.r, ...), custom_call_target="tpu_custom_call" | custom-call | tf_op jit(solution)/shard_map/finish/pallas_call | solution.py:1572
